TPU v7x, 32 devices: a whole 2x2x4 slice. The times are simulated.
32 devices in a mesh: dom: 2 (over x), frame: 16 (over z, y, core).
Axes of the slice: x: 2, y: 2, z: 4, core: 2. Of those that a mesh axis runs over, the one named last changes fastest.
Arguments:
- queries: bfloat16 [32, 512, 1024], P(('dom', 'frame')), parts along dimension 0, may hold values from -8 to 8
- keys: bfloat16 [32, 512, 1024], P(('dom', 'frame')), parts along dimension 0, may hold values from -8 to 8
- values: bfloat16 [32, 512, 1024], P(('dom', 'frame')), parts along dimension 0, may hold values from -6 to 6
- grad_out: bfloat16 [32, 512, 1024], P(('dom', 'frame')), parts along dimension 0, may hold values from -6 to 6
- links: int32 [32, 4], P(('dom', 'frame')), parts along dimension 0, may hold values from 0 to 1, as said below
- w_query: bfloat16 [1024, 1024], replicated, may hold values from -0.1875 to 0.1875
- w_key: bfloat16 [1024, 1024], replicated, may hold values from -0.1875 to 0.1875
- w_value: bfloat16 [1024, 1024], replicated, may hold values from -0.1875 to 0.1875
Outputs:
- grad_input: bfloat16 [32, 512, 1024], P(('dom', 'frame')), parts along dimension 0
There are 2 independent parts, one for each index of `dom`. A program takes and returns all parts, laid end to end along the dimension named above; an argument that names none is the same for every part. Nothing has to cross between parts.
Inputs may be any that keep to these rules, and one draw needn't show every extreme that they name: links[t, j] is 0 whenever t < 2**j; otherwise 0 or 1, so frames attend to ragged numbers of up to 4 earlier frames.
All inputs are finite; a program needn't handle non-finite values.
Results may differ from a plain program's by a relative error of at most 0.0049.
Values may be sent and summed in bfloat16 or wider, within the bound.
No kernel may reach another device: no remote copies, remote signals or barrier semaphores. Data moves between devices by JAX's collectives and lax.ppermute only.
A program may use at most 128 MiB of HBM per device.

v0:
```python
import jax
import jax.numpy as jnp
from jax import lax
from jax.sharding import PartitionSpec as P

HEADS = 16
NDIL = 4


def from_behind(block, axis, distance):
    devices = range(lax.axis_size(axis))
    route = [(i - distance, i) for i in devices if i - distance in devices]
    return lax.ppermute(block, axis, route)


def attention_core(query_f, grad_f, key_list, value_list, live_list, score_scale):
    live_mask = jnp.stack([m[:, None, None] for m in live_list])
    scores = jnp.stack([jnp.sum(query_f * k, axis=-1) for k in key_list]) * score_scale
    scores = jnp.where(live_mask > 0, scores, -1e30)
    highest = jnp.max(scores, axis=0)
    weights_raw = jnp.exp(scores - highest) * live_mask
    probability = weights_raw / jnp.sum(weights_raw, axis=0)
    grad_prob = jnp.stack([jnp.sum(grad_f * v, axis=-1) for v in value_list])
    inner_sum = jnp.sum(probability * grad_prob, axis=0)
    grad_score = probability * (grad_prob - inner_sum) * score_scale
    grad_query = jnp.zeros_like(query_f)
    grad_keys = []
    grad_values = []
    for i in range(len(key_list)):
        grad_query = grad_query + grad_score[i][..., None] * key_list[i]
        grad_keys.append(grad_score[i][..., None] * query_f)
        grad_values.append(probability[i][..., None] * grad_f)
    return (grad_query, grad_keys, grad_values, grad_score, probability)


def dot_transposed(left, weight):
    return lax.dot_general(
        left, weight, (((1,), (1,)), ((), ())), preferred_element_type=jnp.float32
    )


def fetch_pairs(paired, spacing):
    return from_behind(paired, "frame", spacing)


def return_inputs(input_pair, spacing):
    return from_behind(input_pair, "frame", -spacing)


def return_weights(weight_pair, spacing):
    return from_behind(weight_pair, "frame", -spacing)


def per_device(queries, keys, values, grad_out, links, w_query, w_key, w_value):
    frames, patches, model_width = queries.shape
    head_size = model_width // HEADS
    score_scale = head_size ** (-0.5)

    def spread_heads(a):
        return a.astype(jnp.float32).reshape(frames, patches, HEADS, head_size)

    query_f = spread_heads(queries)
    grad_f = spread_heads(grad_out)
    paired = jnp.stack([keys, values])
    key_list = [spread_heads(keys)]
    value_list = [spread_heads(values)]
    live_list = [jnp.ones((frames,), jnp.float32)]
    for j in range(NDIL):
        arrived = fetch_pairs(paired, 2**j)
        key_list.append(spread_heads(arrived[0]))
        value_list.append(spread_heads(arrived[1]))
        live_list.append((links[:, j] > 0).astype(jnp.float32))
    grad_query, grad_keys, grad_values, grad_score, probability = attention_core(
        query_f, grad_f, key_list, value_list, live_list, score_scale
    )
    key_total = grad_keys[0]
    value_total = grad_values[0]
    input_pair = jnp.stack([queries, grad_out])
    for j in range(NDIL):
        weight_pair = jnp.stack([grad_score[j + 1], probability[j + 1]]).reshape(
            2, frames, patches * HEADS
        )
        came_inputs = return_inputs(input_pair, 2**j)
        came_weights = return_weights(weight_pair, 2**j).reshape(2, frames, patches, HEADS)
        key_total = key_total + came_weights[0][..., None] * spread_heads(came_inputs[0])
        value_total = value_total + came_weights[1][..., None] * spread_heads(came_inputs[1])
    flat_rows = frames * patches
    total = dot_transposed(grad_query.reshape(flat_rows, model_width).astype(jnp.bfloat16), w_query)
    total = total + dot_transposed(
        key_total.reshape(flat_rows, model_width).astype(jnp.bfloat16), w_key
    )
    total = total + dot_transposed(
        value_total.reshape(flat_rows, model_width).astype(jnp.bfloat16), w_value
    )
    return total.reshape(frames, patches, model_width).astype(jnp.bfloat16)


def solution(mesh):
    placed = (
        P(("dom", "frame"), None, None),
        P(("dom", "frame"), None, None),
        P(("dom", "frame"), None, None),
        P(("dom", "frame"), None, None),
        P(("dom", "frame"), None),
        P(),
        P(),
        P(),
    )
    return jax.shard_map(
        per_device,
        mesh=mesh,
        in_specs=placed,
        out_specs=P(("dom", "frame"), None, None),
        check_vma=False,
    )
```

profile of v0, /device:TPU:27, one launch (start us, length us, event | category | flops | bytes accessed | tf_op | source)
XLA Modules:
  0.0 277.9 jit_solution(18089176259684921676)
XLA Ops:
  1.7 2.7 copy.35
  4.3 2.7 pad_maximum_fusion
  7.1 3.1 %collective-permute-start.1 = (bf16[2,1,512,1024]{2,3,1,0:T(8,128)(2,1)}, bf16[2,1,512,1024]{2,3,1,0:T(8,128)(2,1)}, u32[]{:S(2)}, u32[]{:S(2)}) collective-permute-start(bf16[2,1,512,1024]{2,3,1,0:T(8,128)(2,1)} %pad_maximum_fusion), channel_id=1, source_target_pairs={{0,2},{1,3},{2,4},{3,5},{4,6},{5,7},{6,8},{7,9},{8,10},{9,11},{10,... | collective-permute-start | bytes 6291464 | tf_op jit(solution)/shard_map/ppermute | solution.py:13
  12.8 1.9 collective-permute-start
  14.7 2.3 copy.32
  18.5 2.7 pad_maximum_fusion.1
  21.2 8.9 %collective-permute-start.11 = (bf16[2,1,512,1024]{2,3,1,0:T(8,128)(2,1)}, bf16[2,1,512,1024]{2,3,1,0:T(8,128)(2,1)}, u32[]{:S(2)}, u32[]{:S(2)}) collective-permute-start(bf16[2,1,512,1024]{2,3,1,0:T(8,128)(2,1)} %pad_maximum_fusion.1), channel_id=1, source_target_pairs={{8,0},{9,1},{10,2},{11,3},{12,4},{13,5},{14,6},{15,7},{24,16},{25,... | collective-permute-start | bytes 6291464 | tf_op jit(solution)/shard_map/ppermute | solution.py:13
  33.6 23.1 %collective-permute-done.1 = bf16[2,1,512,1024]{2,3,1,0:T(8,128)(2,1)} collective-permute-done((bf16[2,1,512,1024]{2,3,1,0:T(8,128)(2,1)}, bf16[2,1,512,1024]{2,3,1,0:T(8,128)(2,1)}, u32[]{:S(2)}, u32[]{:S(2)}) %collective-permute-start.1) | collective-permute-done | bytes 2097184 | tf_op jit(solution)/shard_map/ppermute | solution.py:13
  56.7 4.6 %collective-permute-start.5 = (bf16[2,1,512,1024]{2,3,1,0:T(8,128)(2,1)}, bf16[2,1,512,1024]{2,3,1,0:T(8,128)(2,1)}, u32[]{:S(2)}, u32[]{:S(2)}) collective-permute-start(bf16[2,1,512,1024]{2,3,1,0:T(8,128)(2,1)} %pad_maximum_fusion.1), channel_id=1, source_target_pairs={{1,0},{2,1},{3,2},{4,3},{5,4},{6,5},{7,6},{8,7},{9,8},{10,9},{11,1... | collective-permute-start | bytes 6291464 | tf_op jit(solution)/shard_map/ppermute | solution.py:13
  63.2 40.6 %collective-permute-start.7 = (bf16[2,1,512,1024]{2,3,1,0:T(8,128)(2,1)}, bf16[2,1,512,1024]{2,3,1,0:T(8,128)(2,1)}, u32[]{:S(2)}, u32[]{:S(2)}) collective-permute-start(bf16[2,1,512,1024]{2,3,1,0:T(8,128)(2,1)} %pad_maximum_fusion.1), channel_id=1, source_target_pairs={{2,0},{3,1},{4,2},{5,3},{6,4},{7,5},{8,6},{9,7},{10,8},{11,9},{12,... | collective-permute-start | bytes 6291464 | tf_op jit(solution)/shard_map/ppermute | solution.py:13
  105.7 42.7 %collective-permute-done.3 = bf16[2,1,512,1024]{2,3,1,0:T(8,128)(2,1)} collective-permute-done((bf16[2,1,512,1024]{2,3,1,0:T(8,128)(2,1)}, bf16[2,1,512,1024]{2,3,1,0:T(8,128)(2,1)}, u32[]{:S(2)}, u32[]{:S(2)}) %collective-permute-start.3) | collective-permute-done | bytes 2097184 | tf_op jit(solution)/shard_map/ppermute | solution.py:13
  148.4 2.6 collective-permute-start.9
  152.9 2.0 slice_convert_fusion.3
  161.5 1.9 reshape.1111
  163.4 7.0 %collective-permute-start.4 = (f32[2,1,8192]{2,0,1:T(2,128)}, f32[2,1,8192]{2,0,1:T(2,128)}, u32[]{:S(2)}, u32[]{:S(2)}) collective-permute-start(f32[2,1,8192]{2,0,1:T(2,128)} %reshape.1111), channel_id=1, source_target_pairs={{1,0},{2,1},{3,2},{4,3},{5,4},{6,5},{7,6},{8,7},{9,8},{10,9},{11,1... | collective-permute-start | bytes 196616 | tf_op jit(solution)/shard_map/ppermute | solution.py:13
  172.2 1.9 reshape.1112
  175.2 2.0 reshape.1113
  178.1 1.9 reshape.1114
  180.1 33.4 %collective-permute-done.4 = f32[2,1,8192]{2,0,1:T(2,128)} collective-permute-done((f32[2,1,8192]{2,0,1:T(2,128)}, f32[2,1,8192]{2,0,1:T(2,128)}, u32[]{:S(2)}, u32[]{:S(2)}) %collective-permute-start.4) | collective-permute-done | bytes 65568 | tf_op jit(solution)/shard_map/ppermute | solution.py:13
  213.5 9.8 %collective-permute-start.6 = (f32[2,1,8192]{2,0,1:T(2,128)}, f32[2,1,8192]{2,0,1:T(2,128)}, u32[]{:S(2)}, u32[]{:S(2)}) collective-permute-start(f32[2,1,8192]{2,0,1:T(2,128)} %reshape.1112), channel_id=1, source_target_pairs={{2,0},{3,1},{4,2},{5,3},{6,4},{7,5},{8,6},{9,7},{10,8},{11,9},{12,... | collective-permute-start | bytes 196616 | tf_op jit(solution)/shard_map/ppermute | solution.py:13
  226.6 19.4 %collective-permute-start.8 = (f32[2,1,8192]{2,0,1:T(2,128)}, f32[2,1,8192]{2,0,1:T(2,128)}, u32[]{:S(2)}, u32[]{:S(2)}) collective-permute-start(f32[2,1,8192]{2,0,1:T(2,128)} %reshape.1113), channel_id=1, source_target_pairs={{4,0},{5,1},{6,2},{7,3},{8,4},{9,5},{10,6},{11,7},{12,8},{13,9},{1... | collective-permute-start | bytes 196616 | tf_op jit(solution)/shard_map/ppermute | solution.py:13
  264.2 5.1 %fusion.9 = (bf16[512,1024]{0,1:T(8,128)(2,1)S(1)}, bf16[512,1024]{0,1:T(8,128)(2,1)S(1)}) fusion(bf16[2,1,512,1024]{2,3,1,0:T(8,128)(2,1)} %collective-permute-done.11, bf16[2,1,512,1024]{2,3,1,0:T(8,128)(2,1)} %collective-permute-done.9, bf16[2,1,512,1024]{2,3,1,0:T(8,128)(2,1)} %collective-permute-done.7, ...), kind=kLoop, calls=%fused_computation.11 | loop fusion | flops 15728640 | bytes 12877824 | tf_op jit(solution)/shard_map/convert_element_type | solution.py:90
  272.3 3.3 %fusion.11 = bf16[512,1024]{0,1:T(8,128)(2,1)S(1)} fusion(bf16[2,1,512,1024]{2,3,1,0:T(8,128)(2,1)} %collective-permute-done.11, bf16[2,1,512,1024]{2,3,1,0:T(8,128)(2,1)} %collective-permute-done.9, bf16[2,1,512,1024]{2,3,1,0:T(8,128)(2,1)} %collective-permute-done.7, bf16[2,1,512,1024]{2,3,1,0:T(8,128)(2,1)} %collective-permute-done.5, ...), kind=kLoop, calls=%fused_computation.16 | loop fusion | flops 7864320 | bytes 6455296 | tf_op jit(solution)/shard_map/convert_element_type | solution.py:93
  275.6 2.3 fusion.20
  (94 shorter events, 46.7 us)
Async XLA Ops:
  0.0 269.3 %copy-start = (bf16[1024,1024]{1,0:T(8,128)(2,1)S(1)}, bf16[1024,1024]{1,0:T(8,128)(2,1)}, u32[]{:S(2)}) copy-start(bf16[1024,1024]{1,0:T(8,128)(2,1)} %param.13) | copy-start | bytes 6291460
  1.7 5.4 %copy-start.1 = (bf16[1,512,1024]{1,2,0:T(8,128)(2,1)}, bf16[1,512,1024]{1,2,0:T(8,128)(2,1)S(1)}, u32[]{:S(2)}) copy-start(bf16[1,512,1024]{1,2,0:T(8,128)(2,1)S(1)} %copy.33) | copy-start | bytes 3145732
  7.1 49.6 %collective-permute-start.1 = (bf16[2,1,512,1024]{2,3,1,0:T(8,128)(2,1)}, bf16[2,1,512,1024]{2,3,1,0:T(8,128)(2,1)}, u32[]{:S(2)}, u32[]{:S(2)}) collective-permute-start(bf16[2,1,512,1024]{2,3,1,0:T(8,128)(2,1)} %pad_maximum_fusion), channel_id=1, source_target_pairs={{0,2},{1,3},{2,4},{3,5},{4,6},{5,7},{6,8},{7,9},{8,10},{9,11},{10,... | collective-permute-start | bytes 6291464 | tf_op jit(solution)/shard_map/ppermute | solution.py:13
  10.2 52.9 %collective-permute-start.2 = (bf16[2,1,512,1024]{2,3,1,0:T(8,128)(2,1)}, bf16[2,1,512,1024]{2,3,1,0:T(8,128)(2,1)}, u32[]{:S(2)}, u32[]{:S(2)}) collective-permute-start(bf16[2,1,512,1024]{2,3,1,0:T(8,128)(2,1)} %pad_maximum_fusion), channel_id=1, source_target_pairs={{0,4},{1,5},{2,6},{3,7},{4,8},{5,9},{6,10},{7,11},{8,12},{9,13},{1... | collective-permute-start | bytes 6291464 | tf_op jit(solution)/shard_map/ppermute | solution.py:13
  11.5 136.9 %collective-permute-start.3 = (bf16[2,1,512,1024]{2,3,1,0:T(8,128)(2,1)}, bf16[2,1,512,1024]{2,3,1,0:T(8,128)(2,1)}, u32[]{:S(2)}, u32[]{:S(2)}) collective-permute-start(bf16[2,1,512,1024]{2,3,1,0:T(8,128)(2,1)} %pad_maximum_fusion), channel_id=1, source_target_pairs={{0,8},{1,9},{2,10},{3,11},{4,12},{5,13},{6,14},{7,15},{16,24},{17,... | collective-permute-start | bytes 6291464 | tf_op jit(solution)/shard_map/ppermute | solution.py:13
  12.8 140.1 %collective-permute-start = (bf16[2,1,512,1024]{2,3,1,0:T(8,128)(2,1)}, bf16[2,1,512,1024]{2,3,1,0:T(8,128)(2,1)}, u32[]{:S(2)}, u32[]{:S(2)}) collective-permute-start(bf16[2,1,512,1024]{2,3,1,0:T(8,128)(2,1)} %pad_maximum_fusion), channel_id=1, source_target_pairs={{0,1},{1,2},{2,3},{3,4},{4,5},{5,6},{6,7},{7,8},{8,9},{9,10},{10,1... | collective-permute-start | bytes 6291464 | tf_op jit(solution)/shard_map/ppermute | solution.py:13
  18.5 11.6 %copy-start.10 = (s32[1,4]{1,0:T(1,128)S(1)}, s32[1,4]{1,0:T(1,128)}, u32[]{:S(2)}) copy-start(s32[1,4]{1,0:T(1,128)} %param.12) | copy-start | bytes 52
  21.2 242.9 %collective-permute-start.11 = (bf16[2,1,512,1024]{2,3,1,0:T(8,128)(2,1)}, bf16[2,1,512,1024]{2,3,1,0:T(8,128)(2,1)}, u32[]{:S(2)}, u32[]{:S(2)}) collective-permute-start(bf16[2,1,512,1024]{2,3,1,0:T(8,128)(2,1)} %pad_maximum_fusion.1), channel_id=1, source_target_pairs={{8,0},{9,1},{10,2},{11,3},{12,4},{13,5},{14,6},{15,7},{24,16},{25,... | collective-permute-start | bytes 6291464 | tf_op jit(solution)/shard_map/ppermute | solution.py:13
  56.7 207.5 %collective-permute-start.5 = (bf16[2,1,512,1024]{2,3,1,0:T(8,128)(2,1)}, bf16[2,1,512,1024]{2,3,1,0:T(8,128)(2,1)}, u32[]{:S(2)}, u32[]{:S(2)}) collective-permute-start(bf16[2,1,512,1024]{2,3,1,0:T(8,128)(2,1)} %pad_maximum_fusion.1), channel_id=1, source_target_pairs={{1,0},{2,1},{3,2},{4,3},{5,4},{6,5},{7,6},{8,7},{9,8},{10,9},{11,1... | collective-permute-start | bytes 6291464 | tf_op jit(solution)/shard_map/ppermute | solution.py:13
  63.2 201.0 %collective-permute-start.7 = (bf16[2,1,512,1024]{2,3,1,0:T(8,128)(2,1)}, bf16[2,1,512,1024]{2,3,1,0:T(8,128)(2,1)}, u32[]{:S(2)}, u32[]{:S(2)}) collective-permute-start(bf16[2,1,512,1024]{2,3,1,0:T(8,128)(2,1)} %pad_maximum_fusion.1), channel_id=1, source_target_pairs={{2,0},{3,1},{4,2},{5,3},{6,4},{7,5},{8,6},{9,7},{10,8},{11,9},{12,... | collective-permute-start | bytes 6291464 | tf_op jit(solution)/shard_map/ppermute | solution.py:13
  148.4 115.8 %collective-permute-start.9 = (bf16[2,1,512,1024]{2,3,1,0:T(8,128)(2,1)}, bf16[2,1,512,1024]{2,3,1,0:T(8,128)(2,1)}, u32[]{:S(2)}, u32[]{:S(2)}) collective-permute-start(bf16[2,1,512,1024]{2,3,1,0:T(8,128)(2,1)} %pad_maximum_fusion.1), channel_id=1, source_target_pairs={{4,0},{5,1},{6,2},{7,3},{8,4},{9,5},{10,6},{11,7},{12,8},{13,9},{1... | collective-permute-start | bytes 6291464 | tf_op jit(solution)/shard_map/ppermute | solution.py:13
  152.9 2.1 copy-start.2
  152.9 2.2 copy-start.3
  155.1 1.9 copy-start.4
  163.4 50.0 %collective-permute-start.4 = (f32[2,1,8192]{2,0,1:T(2,128)}, f32[2,1,8192]{2,0,1:T(2,128)}, u32[]{:S(2)}, u32[]{:S(2)}) collective-permute-start(f32[2,1,8192]{2,0,1:T(2,128)} %reshape.1111), channel_id=1, source_target_pairs={{1,0},{2,1},{3,2},{4,3},{5,4},{6,5},{7,6},{8,7},{9,8},{10,9},{11,1... | collective-permute-start | bytes 196616 | tf_op jit(solution)/shard_map/ppermute | solution.py:13
  213.5 13.1 %collective-permute-start.6 = (f32[2,1,8192]{2,0,1:T(2,128)}, f32[2,1,8192]{2,0,1:T(2,128)}, u32[]{:S(2)}, u32[]{:S(2)}) collective-permute-start(f32[2,1,8192]{2,0,1:T(2,128)} %reshape.1112), channel_id=1, source_target_pairs={{2,0},{3,1},{4,2},{5,3},{6,4},{7,5},{8,6},{9,7},{10,8},{11,9},{12,... | collective-permute-start | bytes 196616 | tf_op jit(solution)/shard_map/ppermute | solution.py:13
  226.6 22.7 %collective-permute-start.8 = (f32[2,1,8192]{2,0,1:T(2,128)}, f32[2,1,8192]{2,0,1:T(2,128)}, u32[]{:S(2)}, u32[]{:S(2)}) collective-permute-start(f32[2,1,8192]{2,0,1:T(2,128)} %reshape.1113), channel_id=1, source_target_pairs={{4,0},{5,1},{6,2},{7,3},{8,4},{9,5},{10,6},{11,7},{12,8},{13,9},{1... | collective-permute-start | bytes 196616 | tf_op jit(solution)/shard_map/ppermute | solution.py:13
  249.3 5.2 %collective-permute-start.10 = (f32[2,1,8192]{2,0,1:T(2,128)}, f32[2,1,8192]{2,0,1:T(2,128)}, u32[]{:S(2)}, u32[]{:S(2)}) collective-permute-start(f32[2,1,8192]{2,0,1:T(2,128)} %reshape.1114), channel_id=1, source_target_pairs={{8,0},{9,1},{10,2},{11,3},{12,4},{13,5},{14,6},{15,7},{24,16},{25,... | collective-permute-start | bytes 196616 | tf_op jit(solution)/shard_map/ppermute | solution.py:13
  269.3 1.6 copy-start.11
  270.9 1.4 copy-start.6
  270.9 1.4 copy-start.7
  270.9 1.4 copy-start.8
  270.9 1.4 copy-start.9
  272.3 3.3 %copy-start.12 = (bf16[1024,1024]{1,0:T(8,128)(2,1)S(1)}, bf16[1024,1024]{1,0:T(8,128)(2,1)}, u32[]{:S(2)}) copy-start(bf16[1024,1024]{1,0:T(8,128)(2,1)} %param.15) | copy-start | bytes 6291460
  (1 other events, 1.3 us)
where the time goes:
time: 283 us; the launch traced here: 278 us
  starting transfers between devices  102 us (36%)
  waiting for transfers between devices  99.2 us (35%)
  local copies, waits for them, and re-layouts  41.9 us (15%)
  other arithmetic  26.3 us (9%)
  matrix products  4.93 us (2%)
  between operations  3.09 us (1%)
    ppermute x12, starting transfers between devices, from_behind(): return lax.ppermute(block, axis, route)  102 us
    ppermute x12, waiting for transfers between devices, from_behind(): return lax.ppermute(block, axis, route)  99.2 us
    unnamed x38, local copies, waits for them, and re-layouts  8.55 us
    reshape x4, local copies, waits for them, and re-layouts, per_device(): jnp.stack([grad_score[j + 1], probability[j + 1]])  7.8 us
    convert_element_type x4, other arithmetic, spread_heads(): return a.astype(jnp.float32).reshape(frames, patches, HEADS, head_size)  7.67 us
    slice x4, local copies, waits for them, and re-layouts, per_device(): came_weights[0][..., None] * spread_heads(came_inputs[0])  6.82 us
    mul x8, local copies, waits for them, and re-layouts, per_device(): came_weights[0][..., None] * spread_heads(came_inputs[0])  6.35 us
    mul x8, local copies, waits for them, and re-layouts, per_device(): came_weights[1][..., None] * spread_heads(came_inputs[1])  6.34 us
  transfers between devices with their start and end apart: 12, of which 3 were waited for; matrix products, arithmetic and copies ran while one was open for 19% of the time, Pallas kernels for 0%

commit v1 on v0

v1 whole, which is shorter than its diff:
```python
import functools

import jax
import jax.numpy as jnp
from jax import lax
from jax.experimental import pallas as pl
from jax.experimental.pallas import tpu as pltpu
from jax.sharding import PartitionSpec as P

HEADS = 16
NDIL = 4
LANES = 128
VMEM_BYTES = 56 * 2**20
CHUNKS = (2, 2)


def shift(block, distance):
    n = lax.axis_size("frame")
    return lax.ppermute(block, "frame", [(i, i + distance) for i in range(n) if 0 <= i + distance < n])


def swap(block, bit):
    n = lax.axis_size("frame")
    return lax.ppermute(block, "frame", [(i, i ^ bit) for i in range(n)])


def head_rows(width, head_size):
    row = lax.broadcasted_iota(jnp.int32, (HEADS, width), 0)
    feature = lax.broadcasted_iota(jnp.int32, (HEADS, width), 1)
    return jnp.where(feature // head_size == row, 1.0, 0.0).astype(jnp.bfloat16)


def spread_matrix(slot, width, head_size):
    row = lax.broadcasted_iota(jnp.int32, (2 * LANES, width), 0) % LANES
    feature = lax.broadcasted_iota(jnp.int32, (2 * LANES, width), 1)
    return jnp.where(feature // head_size + slot * HEADS == row, 1.0, 0.0).astype(jnp.bfloat16)


def split_high_low(wide):
    high = wide.astype(jnp.bfloat16)
    return high, (wide - high.astype(jnp.float32)).astype(jnp.bfloat16)


def dot(left, right, left_dim, right_dim):
    return lax.dot_general(
        left, right, (((left_dim,), (right_dim,)), ((), ())), preferred_element_type=jnp.float32
    )


def spread_operand(per_source):
    rows = per_source[0].shape[1]
    gap = LANES - HEADS * len(per_source)
    stacked = jnp.concatenate([*per_source, jnp.zeros((gap, rows), jnp.float32)], axis=0)
    return jnp.concatenate(split_high_low(stacked.T), axis=1)


def score_kernel(head_size, flags, query_grad, own, first, second, near, far8, far4, spread, rows_ref,
                 pair1, pair2, pair4, pair8, self_pair, grad_query):
    scale = head_size ** (-0.5)
    width = query_grad.shape[2]
    heads = rows_ref[...]
    query = query_grad[0].astype(jnp.float32)
    grad = query_grad[1].astype(jnp.float32)
    two_first = flags[NDIL] > 0
    one_first = flags[NDIL + 1] > 0

    def pick(use_first, a, b, i):
        return jnp.where(use_first, a[i], b[i])

    getters = (
        lambda i: own[i],
        lambda i: pick(one_first, near[0], near[1], i),
        lambda i: pick(two_first, first, second, i),
        lambda i: far4[i],
        lambda i: far8[i],
    )

    def per_head(left, right):
        high, low = split_high_low(left * right.astype(jnp.float32))
        return dot(heads, high, 1, 1) + dot(heads, low, 1, 1)

    scores, grad_probs = [], []
    for slot, get in enumerate(getters):
        score = per_head(query, get(0)) * scale
        if slot:
            score = jnp.where(flags[slot - 1] > 0, score, -1e30)
        scores.append(score)
        grad_probs.append(per_head(grad, get(1)))
    highest = functools.reduce(jnp.maximum, scores)
    raw = [jnp.exp(s - highest) for s in scores]
    raw = raw[:1] + [jnp.where(flags[j] > 0, r, 0.0) for j, r in enumerate(raw[1:])]
    total = functools.reduce(jnp.add, raw)
    probability = [r / total for r in raw]
    inner = functools.reduce(jnp.add, [p * g for p, g in zip(probability, grad_probs)])
    grad_score = [p * (g - inner) * scale for p, g in zip(probability, grad_probs)]
    for slot, out in enumerate((self_pair, pair1, pair2, pair4, pair8)):
        out[:HEADS, :] = grad_score[slot]
        out[HEADS:, :] = probability[slot]
    operand = spread_operand(grad_score)
    sum_ = None
    for slot, get in enumerate(getters):
        term = dot(operand, spread[slot], 1, 0) * get(0).astype(jnp.float32)
        sum_ = term if sum_ is None else sum_ + term
    grad_query[...] = sum_.astype(jnp.bfloat16)


def sum_kernel(flags, own, first, second, near, far8, far4, self_pair, pair1, pair2, pair4, pair8,
               grad_query, spread, w_query, w_key, w_value, out):
    two_first = flags[NDIL] == 0
    one_first = flags[NDIL + 1] == 0

    def pick(use_first, a, b, i):
        return jnp.where(use_first, a[i], b[i])

    getters = (
        lambda i: own[i],
        lambda i: pick(one_first, near[0], near[1], i),
        lambda i: pick(two_first, first, second, i),
        lambda i: far4[i],
        lambda i: far8[i],
    )
    pairs = (self_pair, pair1, pair2, pair4, pair8)
    sums = []
    for part in range(2):
        operand = spread_operand([p[part * HEADS:(part + 1) * HEADS, :] for p in pairs])
        sum_ = None
        for slot, get in enumerate(getters):
            term = dot(operand, spread[slot], 1, 0) * get(part).astype(jnp.float32)
            sum_ = term if sum_ is None else sum_ + term
        sums.append(sum_.astype(jnp.bfloat16))
    total = dot(grad_query[...], w_query[...], 1, 1)
    total = total + dot(sums[0], w_key[...], 1, 1)
    total = total + dot(sums[1], w_value[...], 1, 1)
    out[...] = total.astype(jnp.bfloat16)


def whole(a):
    return pl.BlockSpec(a.shape, lambda i: (0,) * a.ndim)


def by_rows(width, tile):
    return pl.BlockSpec((2, tile, width), lambda i: (0, i, 0))


def params():
    return pltpu.CompilerParams(vmem_limit_bytes=VMEM_BYTES, dimension_semantics=("arbitrary",))


def scores_of(flags, query_grad, own, first, second, near, far8, far4, spread, rows_of_heads, head_size, tile):
    _, rows, width = own.shape
    wide = by_rows(width, tile)
    pair = pl.BlockSpec((2 * HEADS, tile), lambda i: (0, i))
    pair_shape = jax.ShapeDtypeStruct((2 * HEADS, rows), jnp.float32)

    def kernel(flags_ref, qg, kv, a, b, c, d, e, f, sp, rw, *outs):
        score_kernel(head_size, flags_ref, qg, kv, a, b, (c, d), e, f, sp, rw, *outs)

    return pl.pallas_call(
        kernel,
        grid=(rows // tile,),
        in_specs=[pl.BlockSpec(memory_space=pltpu.SMEM)] + [wide] * 8 + [whole(spread), whole(rows_of_heads)],
        out_specs=[pair] * 5 + [pl.BlockSpec((tile, width), lambda i: (i, 0))],
        out_shape=[pair_shape] * 5 + [jax.ShapeDtypeStruct((rows, width), jnp.bfloat16)],
        compiler_params=params(),
        cost_estimate=pl.CostEstimate(flops=rows * width * 4000, bytes_accessed=rows * width * 36, transcendentals=0),
        name="scores",
    )(flags, query_grad, own, first, second, *near, far8, far4, spread, rows_of_heads)


def sums_of(flags, own, first, second, near, far8, far4, pairs, grad_query, spread, weights, tile):
    _, rows, width = own.shape
    wide = by_rows(width, tile)
    pair = pl.BlockSpec((2 * HEADS, tile), lambda i: (0, i))

    def kernel(flags_ref, qg, a, b, c, d, e, f, p0, p1, p2, p4, p8, gq, sp, wq, wk, wv, out):
        sum_kernel(flags_ref, qg, a, b, (c, d), e, f, p0, p1, p2, p4, p8, gq, sp, wq, wk, wv, out)

    return pl.pallas_call(
        kernel,
        grid=(rows // tile,),
        in_specs=[pl.BlockSpec(memory_space=pltpu.SMEM)] + [wide] * 7 + [pair] * 5
        + [pl.BlockSpec((tile, width), lambda i: (i, 0)), whole(spread)] + [whole(w) for w in weights],
        out_specs=pl.BlockSpec((tile, width), lambda i: (i, 0)),
        out_shape=jax.ShapeDtypeStruct((rows, width), jnp.bfloat16),
        compiler_params=params(),
        cost_estimate=pl.CostEstimate(flops=rows * width * 8000, bytes_accessed=rows * width * 36, transcendentals=0),
        name="sums",
    )(flags, own, first, second, *near, far8, far4, *pairs, grad_query, spread, *weights)


def per_device(queries, keys, values, grad_out, links, w_query, w_key, w_value):
    _, patches, width = queries.shape
    head_size = width // HEADS
    me = lax.axis_index("frame")
    bit0 = lax.rem(me, 2)
    bit1 = lax.rem(me // 2, 2)
    flags = jnp.concatenate([links[0].astype(jnp.int32), jnp.stack([bit1, bit0]).astype(jnp.int32)])
    spread = jnp.stack([spread_matrix(s, width, head_size) for s in range(NDIL + 1)])
    rows_of_heads = head_rows(width, head_size)

    tile = LANES
    unit = patches // sum(CHUNKS)
    bounds = [0]
    for c in CHUNKS:
        bounds.append(bounds[-1] + c * unit)
    chunks = list(zip(bounds[:-1], bounds[1:]))

    key_value, query_grad = [], []
    for lo, hi in chunks:
        key_value.append(jnp.stack([keys[0, lo:hi], values[0, lo:hi]]))
        query_grad.append(jnp.stack([queries[0, lo:hi], grad_out[0, lo:hi]]))
    up4, down4, up8, down8, y_own, y_far, c_own, c_far = [], [], [], [], [], [], [], []
    for kv, qg in zip(key_value, query_grad):
        up4.append(shift(kv, 4))
        down4.append(shift(qg, -4))
        y_own.append(swap(jnp.where(bit1 == 0, kv, qg), 2))
        c_own.append(swap(jnp.where(bit0 == 0, kv, qg), 1))
    for i in range(len(chunks)):
        up8.append(shift(up4[i], 4))
        down8.append(shift(down4[i], -4))
        y_far.append(swap(jnp.where(bit1 == 0, down4[i], up4[i]), 2))
    for i in range(len(chunks)):
        c_far.append(swap(jnp.where(bit0 == bit1, y_own[i], y_far[i]), 1))
    outs = []
    for i in range(len(chunks)):
        near = (c_own[i], c_far[i])
        pair1, pair2, pair4, pair8, self_pair, grad_query = scores_of(
            flags, query_grad[i], key_value[i], y_own[i], y_far[i], near, up8[i], up4[i], spread, rows_of_heads,
            head_size, tile)
        came = [shift(p, -d) for p, d in ((pair1, 1), (pair2, 2), (pair4, 4), (pair8, 8))]
        outs.append(sums_of(flags, query_grad[i], y_own[i], y_far[i], near, down8[i], down4[i], [self_pair, *came],
                            grad_query, spread, (w_query, w_key, w_value), tile))
    return jnp.concatenate(outs, axis=0)[None]


def solution(mesh):
    by_frame = P(("dom", "frame"), None, None)
    return jax.shard_map(
        per_device,
        mesh=mesh,
        in_specs=(by_frame,) * 4 + (P(("dom", "frame"), None), P(), P(), P()),
        out_specs=by_frame,
        check_vma=False,
    )
```

time: 283 us -> 195 us (0.69); the launches traced: 278 us -> 195 us
  Pallas kernels: 0 us -> 40.8 us
  local copies, waits for them, and re-layouts: 41.9 us -> 4.48 us
  starting transfers between devices: 102 us -> 68.8 us
  waiting for transfers between devices: 99.2 us -> 67.6 us
  other arithmetic: 26.3 us -> 12.3 us
  matrix products: 4.93 us -> 0 us
    pallas_call x0 -> x4, Pallas kernels: none -> 40.8 us  [the longest x2 24 us: sums_of(): pl.pallas_call(kernel, grid=(rows // tile,), in_specs=[pl.BlockSpec(memor...]
    ppermute x12 -> x24, starting transfers between devices: 102 us -> 68.8 us  [the longest x16 48.1 us: shift(): lax.ppermute(block, 'frame', [(i, i + distance) for i in range(n) if 0 <=...]
    ppermute x12 -> x24, waiting for transfers between devices: 99.2 us -> 67.6 us  [the longest x8 36.3 us: swap(): return lax.ppermute(block, 'frame', [(i, i ^ bit) for i in range(n)])]
    convert_element_type x6 -> x1, other arithmetic: 16.1 us -> 0.64 us  [head_rows(): return jnp.where(feature // head_size == row, 1.0, 0.0).astype(jnp.bfloat16)]
    mul x18 -> x0, local copies, waits for them, and re-layouts: 13.9 us -> none  [the longest x8 6.35 us: per_device(): came_weights[0][..., None] * spread_heads(came_inputs[0])]
    select_n x0 -> x6, other arithmetic: none -> 8 us  [the longest x2 3.21 us: per_device(): c_own.append(swap(jnp.where(bit0 == 0, kv, qg), 1))]
    reshape x4 -> x0, local copies, waits for them, and re-layouts: 7.8 us -> none  [per_device(): jnp.stack([grad_score[j + 1], probability[j + 1]])]
    unnamed x38 -> x56, local copies, waits for them, and re-layouts: 8.55 us -> 2.46 us
  transfers between devices with their start and end apart: 12 -> 24, of which waited for: 3 -> 7; matrix products, arithmetic and copies ran while one was open for 19% -> 4% of each run, Pallas kernels for 0% -> 15%
where the time goes in v1:
time: 195 us
  starting transfers between devices  68.8 us (35%)
  waiting for transfers between devices  67.6 us (35%)
  Pallas kernels  40.8 us (21%)
  other arithmetic  12.3 us (6%)
  local copies, waits for them, and re-layouts  4.48 us (2%)
    ppermute x16, starting transfers between devices, shift(): lax.ppermute(block, 'frame', [(i, i + distance) for i in range(n) if 0 <=...  48.1 us
    ppermute x8, waiting for transfers between devices, swap(): return lax.ppermute(block, 'frame', [(i, i ^ bit) for i in range(n)])  36.3 us
    ppermute x16, waiting for transfers between devices, shift(): lax.ppermute(block, 'frame', [(i, i + distance) for i in range(n) if 0 <=...  31.3 us
    pallas_call x2, Pallas kernels, sums_of(): pl.pallas_call(kernel, grid=(rows // tile,), in_specs=[pl.BlockSpec(memor...  24 us
    ppermute x8, starting transfers between devices, swap(): return lax.ppermute(block, 'frame', [(i, i ^ bit) for i in range(n)])  20.7 us
    pallas_call x2, Pallas kernels, scores_of(): pl.pallas_call(kernel, grid=(rows // tile,), in_specs=[pl.BlockSpec(memor...  16.8 us
  transfers between devices with their start and end apart: 24, of which 7 were waited for; matrix products, arithmetic and copies ran while one was open for 4% of the time, Pallas kernels for 15%

profile of v1, /device:TPU:27, one launch (start us, length us, event | category | flops | bytes accessed | tf_op | source)
XLA Modules:
  0.0 194.6 jit_solution(5345284098202583994)
XLA Ops:
  9.0 4.1 %collective-permute-start.13 = (bf16[2,256,1024]{2,1,0:T(8,128)(2,1)S(1)}, bf16[2,256,1024]{2,1,0:T(8,128)(2,1)S(1)}, u32[]{:S(2)}, u32[]{:S(2)}) collective-permute-start(bf16[2,256,1024]{2,1,0:T(8,128)(2,1)S(1)} %get-tuple-element.43.qg), channel_id=1, source_target_pairs={{4,0},{5,1},{6,2},{7,3},{8,4},{9,5},{10,6},{11,7},{12,8},{13,9},{1... | collective-permute-start | bytes 3145736 | tf_op jit(solution)/shard_map/ppermute | solution.py:19
  15.7 12.1 %collective-permute-done.1.f = bf16[2,256,1024]{2,1,0:T(8,128)(2,1)S(1)} collective-permute-done((bf16[2,256,1024]{2,1,0:T(8,128)(2,1)S(1)}, bf16[2,256,1024]{2,1,0:T(8,128)(2,1)S(1)}, u32[]{:S(2)}, u32[]{:S(2)}) %collective-permute-start.1) | collective-permute-done | bytes 1048608 | tf_op jit(solution)/shard_map/ppermute | solution.py:19
  27.8 3.9 %collective-permute-done.2.f = bf16[2,256,1024]{2,1,0:T(8,128)(2,1)S(1)} collective-permute-done((bf16[2,256,1024]{2,1,0:T(8,128)(2,1)S(1)}, bf16[2,256,1024]{2,1,0:T(8,128)(2,1)S(1)}, u32[]{:S(2)}, u32[]{:S(2)}) %collective-permute-start.2) | collective-permute-done | bytes 1048608 | tf_op jit(solution)/shard_map/ppermute | solution.py:19
  34.1 3.6 %collective-permute-start.4 = (bf16[2,256,1024]{2,1,0:T(8,128)(2,1)}, bf16[2,256,1024]{2,1,0:T(8,128)(2,1)}, u32[]{:S(2)}, u32[]{:S(2)}) collective-permute-start(bf16[2,256,1024]{2,1,0:T(8,128)(2,1)} %get-tuple-element.29), channel_id=1, source_target_pairs={{0,1},{1,0},{2,3},{3,2},{4,5},{5,4},{6,7},{7,6},{8,9},{9,8},{10,11... | collective-permute-start | bytes 3145736 | tf_op jit(solution)/shard_map/ppermute | solution.py:24
  37.7 12.6 %collective-permute-done.13.f = bf16[2,256,1024]{2,1,0:T(8,128)(2,1)S(1)} collective-permute-done((bf16[2,256,1024]{2,1,0:T(8,128)(2,1)S(1)}, bf16[2,256,1024]{2,1,0:T(8,128)(2,1)S(1)}, u32[]{:S(2)}, u32[]{:S(2)}) %collective-permute-start.13) | collective-permute-done | bytes 1048608 | tf_op jit(solution)/shard_map/ppermute | solution.py:19
  51.5 2.7 %collective-permute-done.14.f = bf16[2,256,1024]{2,1,0:T(8,128)(2,1)} collective-permute-done((bf16[2,256,1024]{2,1,0:T(8,128)(2,1)S(1)}, bf16[2,256,1024]{2,1,0:T(8,128)(2,1)}, u32[]{:S(2)}, u32[]{:S(2)}) %collective-permute-start.14) | collective-permute-done | bytes 1048608 | tf_op jit(solution)/shard_map/ppermute | solution.py:19
  55.4 2.5 %collective-permute-start.15 = (bf16[2,256,1024]{2,1,0:T(8,128)(2,1)}, bf16[2,256,1024]{2,1,0:T(8,128)(2,1)S(1)}, u32[]{:S(2)}, u32[]{:S(2)}) collective-permute-start(bf16[2,256,1024]{2,1,0:T(8,128)(2,1)} %broadcast_select_fusion.4), channel_id=1, source_target_pairs={{0,2},{1,3},{2,0},{3,1},{4,6},{5,7},{6,4},{7,5},{8,10},{9,11},{10,... | collective-permute-start | bytes 3145736 | tf_op jit(solution)/shard_map/ppermute | solution.py:24
  61.7 3.3 %collective-permute-start.5 = (bf16[2,256,1024]{2,1,0:T(8,128)(2,1)S(1)}, bf16[2,256,1024]{2,1,0:T(8,128)(2,1)S(1)}, u32[]{:S(2)}, u32[]{:S(2)}) collective-permute-start(bf16[2,256,1024]{2,1,0:T(8,128)(2,1)S(1)} %broadcast_select_fusion.1), channel_id=1, source_target_pairs={{0,1},{1,0},{2,3},{3,2},{4,5},{5,4},{6,7},{7,6},{8,9},{9,8},{10,11... | collective-permute-start | bytes 3145736 | tf_op jit(solution)/shard_map/ppermute | solution.py:24
  65.4 17.3 %collective-permute-done.12.a = bf16[2,256,1024]{2,1,0:T(8,128)(2,1)S(1)} collective-permute-done((bf16[2,256,1024]{2,1,0:T(8,128)(2,1)}, bf16[2,256,1024]{2,1,0:T(8,128)(2,1)S(1)}, u32[]{:S(2)}, u32[]{:S(2)}) %collective-permute-start.12) | collective-permute-done | bytes 1048608 | tf_op jit(solution)/shard_map/ppermute | solution.py:24
  82.7 4.5 %collective-permute-start.16 = (bf16[2,256,1024]{2,1,0:T(8,128)(2,1)}, bf16[2,256,1024]{2,1,0:T(8,128)(2,1)}, u32[]{:S(2)}, u32[]{:S(2)}) collective-permute-start(bf16[2,256,1024]{2,1,0:T(8,128)(2,1)} %get-tuple-element.31), channel_id=1, source_target_pairs={{0,1},{1,0},{2,3},{3,2},{4,5},{5,4},{6,7},{7,6},{8,9},{9,8},{10,11... | collective-permute-start | bytes 3145736 | tf_op jit(solution)/shard_map/ppermute | solution.py:24
  87.2 18.0 %collective-permute-done.15.b = bf16[2,256,1024]{2,1,0:T(8,128)(2,1)S(1)} collective-permute-done((bf16[2,256,1024]{2,1,0:T(8,128)(2,1)}, bf16[2,256,1024]{2,1,0:T(8,128)(2,1)S(1)}, u32[]{:S(2)}, u32[]{:S(2)}) %collective-permute-start.15) | collective-permute-done | bytes 1048608 | tf_op jit(solution)/shard_map/ppermute | solution.py:24
  105.2 4.7 %collective-permute-start.6 = (bf16[2,256,1024]{2,1,0:T(8,128)(2,1)S(1)}, bf16[2,256,1024]{2,1,0:T(8,128)(2,1)}, u32[]{:S(2)}, u32[]{:S(2)}) collective-permute-start(bf16[2,256,1024]{2,1,0:T(8,128)(2,1)S(1)} %copy-done.9), channel_id=1, source_target_pairs={{4,0},{5,1},{6,2},{7,3},{8,4},{9,5},{10,6},{11,7},{12,8},{13,9},{1... | collective-permute-start | bytes 3145736 | tf_op jit(solution)/shard_map/ppermute | solution.py:19
  112.3 3.1 %collective-permute-start.17 = (bf16[2,256,1024]{2,1,0:T(8,128)(2,1)}, bf16[2,256,1024]{2,1,0:T(8,128)(2,1)S(1)}, u32[]{:S(2)}, u32[]{:S(2)}) collective-permute-start(bf16[2,256,1024]{2,1,0:T(8,128)(2,1)} %broadcast_select_fusion), channel_id=1, source_target_pairs={{0,1},{1,0},{2,3},{3,2},{4,5},{5,4},{6,7},{7,6},{8,9},{9,8},{10,11... | collective-permute-start | bytes 3145736 | tf_op jit(solution)/shard_map/ppermute | solution.py:24
  116.2 5.3 %collective-permute-start.18 = (bf16[2,256,1024]{2,1,0:T(8,128)(2,1)S(1)}, bf16[2,256,1024]{2,1,0:T(8,128)(2,1)}, u32[]{:S(2)}, u32[]{:S(2)}) collective-permute-start(bf16[2,256,1024]{2,1,0:T(8,128)(2,1)S(1)} %copy-done.7), channel_id=1, source_target_pairs={{4,0},{5,1},{6,2},{7,3},{8,4},{9,5},{10,6},{11,7},{12,8},{13,9},{1... | collective-permute-start | bytes 3145736 | tf_op jit(solution)/shard_map/ppermute | solution.py:19
  124.0 8.4 %scores.2 = (f32[32,256]{1,0:T(8,128)}, f32[32,256]{1,0:T(8,128)}, f32[32,256]{1,0:T(8,128)}, f32[32,256]{1,0:T(8,128)}, f32[32,256]{1,0:T(8,128)}, /*index=5*/bf16[256,1024]{1,0:T(8,128)(2,1)}) custom-call(s32[6]{0:T(128)} %pad_add_fusion.flags_ref, bf16[2,256,1024]{2,1,0:T(8,128)(2,1)} %copy-done.5, bf16[2,256,1024]{2,1,0:T(8,128)(2,1)} %copy-done.14, ...), custom_call_target="tpu_custom_call" | custom-call | flops 1048576000 | bytes 9437184 | tf_op jit(solution)/shard_map/scores/pallas_call | solution.py:158
  133.8 2.4 %collective-permute-start.11 = (f32[32,256]{1,0:T(8,128)}, f32[32,256]{1,0:T(8,128)S(1)}, u32[]{:S(2)}, u32[]{:S(2)}) collective-permute-start(f32[32,256]{1,0:T(8,128)} %get-tuple-element.21), channel_id=1, source_target_pairs={{8,0},{9,1},{10,2},{11,3},{12,4},{13,5},{14,6},{15,7},{24,16},{25,... | collective-permute-start | bytes 98312 | tf_op jit(solution)/shard_map/ppermute | solution.py:19
  136.2 5.5 %collective-permute-start.8 = (f32[32,256]{1,0:T(8,128)}, f32[32,256]{1,0:T(8,128)S(1)}, u32[]{:S(2)}, u32[]{:S(2)}) collective-permute-start(f32[32,256]{1,0:T(8,128)} %get-tuple-element.18), channel_id=1, source_target_pairs={{1,0},{2,1},{3,2},{4,3},{5,4},{6,5},{7,6},{8,7},{9,8},{10,9},{11,1... | collective-permute-start | bytes 98312 | tf_op jit(solution)/shard_map/ppermute | solution.py:19
  141.7 4.0 %collective-permute-start.9 = (f32[32,256]{1,0:T(8,128)}, f32[32,256]{1,0:T(8,128)S(1)}, u32[]{:S(2)}, u32[]{:S(2)}) collective-permute-start(f32[32,256]{1,0:T(8,128)} %get-tuple-element.19), channel_id=1, source_target_pairs={{2,0},{3,1},{4,2},{5,3},{6,4},{7,5},{8,6},{9,7},{10,8},{11,9},{12,... | collective-permute-start | bytes 98312 | tf_op jit(solution)/shard_map/ppermute | solution.py:19
  145.7 8.4 %scores.3 = (f32[32,256]{1,0:T(8,128)}, f32[32,256]{1,0:T(8,128)}, f32[32,256]{1,0:T(8,128)}, f32[32,256]{1,0:T(8,128)}, f32[32,256]{1,0:T(8,128)}, /*index=5*/bf16[256,1024]{1,0:T(8,128)(2,1)}) custom-call(s32[6]{0:T(128)} %pad_add_fusion.flags_ref, bf16[2,256,1024]{2,1,0:T(8,128)(2,1)} %copy-done.4, bf16[2,256,1024]{2,1,0:T(8,128)(2,1)} %copy-done.13, ...), custom_call_target="tpu_custom_call" | custom-call | flops 1048576000 | bytes 9437184 | tf_op jit(solution)/shard_map/scores/pallas_call | solution.py:158
  154.2 4.0 %collective-permute-start.20 = (f32[32,256]{1,0:T(8,128)}, f32[32,256]{1,0:T(8,128)S(1)}, u32[]{:S(2)}, u32[]{:S(2)}) collective-permute-start(f32[32,256]{1,0:T(8,128)} %get-tuple-element.24), channel_id=1, source_target_pairs={{1,0},{2,1},{3,2},{4,3},{5,4},{6,5},{7,6},{8,7},{9,8},{10,9},{11,1... | collective-permute-start | bytes 98312 | tf_op jit(solution)/shard_map/ppermute | solution.py:19
  158.2 4.6 %collective-permute-start.21 = (f32[32,256]{1,0:T(8,128)}, f32[32,256]{1,0:T(8,128)S(1)}, u32[]{:S(2)}, u32[]{:S(2)}) collective-permute-start(f32[32,256]{1,0:T(8,128)} %get-tuple-element.25), channel_id=1, source_target_pairs={{2,0},{3,1},{4,2},{5,3},{6,4},{7,5},{8,6},{9,7},{10,8},{11,9},{12,... | collective-permute-start | bytes 98312 | tf_op jit(solution)/shard_map/ppermute | solution.py:19
  165.1 2.6 %collective-permute-start.23 = (f32[32,256]{1,0:T(8,128)}, f32[32,256]{1,0:T(8,128)S(1)}, u32[]{:S(2)}, u32[]{:S(2)}) collective-permute-start(f32[32,256]{1,0:T(8,128)} %get-tuple-element.27), channel_id=1, source_target_pairs={{8,0},{9,1},{10,2},{11,3},{12,4},{13,5},{14,6},{15,7},{24,16},{25,... | collective-permute-start | bytes 98312 | tf_op jit(solution)/shard_map/ppermute | solution.py:19
  167.8 12.0 %sums.2 = bf16[256,1024]{1,0:T(8,128)(2,1)} custom-call(s32[6]{0:T(128)} %pad_add_fusion.flags_ref, bf16[2,256,1024]{2,1,0:T(8,128)(2,1)} %copy-done.5, bf16[2,256,1024]{2,1,0:T(8,128)(2,1)} %copy-done.3, bf16[2,256,1024]{2,1,0:T(8,128)(2,1)} %collective-permute-done.3.b, bf16[2,256,1024]{2,1,0:T(8,128)(2,1)} %collective-permute-done.4.c, ...), custom_call_target="tpu_custom_call" | custom-call | flops 2097152000 | bytes 9437184 | tf_op jit(solution)/shard_map/sums/pallas_call | solution.py:178
  180.5 12.0 %sums.3 = bf16[256,1024]{1,0:T(8,128)(2,1)} custom-call(s32[6]{0:T(128)} %pad_add_fusion.flags_ref, bf16[2,256,1024]{2,1,0:T(8,128)(2,1)} %copy-done.4, bf16[2,256,1024]{2,1,0:T(8,128)(2,1)} %copy-done.1, bf16[2,256,1024]{2,1,0:T(8,128)(2,1)} %copy-done.2, bf16[2,256,1024]{2,1,0:T(8,128)(2,1)} %collective-permute-done.16.c, ...), custom_call_target="tpu_custom_call" | custom-call | flops 2097152000 | bytes 9437184 | tf_op jit(solution)/shard_map/sums/pallas_call | solution.py:178
  (104 shorter events, 32.6 us)
Async XLA Ops:
  3.9 23.9 %collective-permute-start.1 = (bf16[2,256,1024]{2,1,0:T(8,128)(2,1)S(1)}, bf16[2,256,1024]{2,1,0:T(8,128)(2,1)S(1)}, u32[]{:S(2)}, u32[]{:S(2)}) collective-permute-start(bf16[2,256,1024]{2,1,0:T(8,128)(2,1)S(1)} %get-tuple-element.33.qg), channel_id=1, source_target_pairs={{4,0},{5,1},{6,2},{7,3},{8,4},{9,5},{10,6},{11,7},{12,8},{13,9},{1... | collective-permute-start | bytes 3145736 | tf_op jit(solution)/shard_map/ppermute | solution.py:19
  6.1 25.6 %collective-permute-start.2 = (bf16[2,256,1024]{2,1,0:T(8,128)(2,1)S(1)}, bf16[2,256,1024]{2,1,0:T(8,128)(2,1)S(1)}, u32[]{:S(2)}, u32[]{:S(2)}) collective-permute-start(bf16[2,256,1024]{2,1,0:T(8,128)(2,1)S(1)} %get-tuple-element.34.kv), channel_id=1, source_target_pairs={{0,4},{1,5},{2,6},{3,7},{4,8},{5,9},{6,10},{7,11},{8,12},{9,13},{1... | collective-permute-start | bytes 3145736 | tf_op jit(solution)/shard_map/ppermute | solution.py:19
  9.0 41.3 %collective-permute-start.13 = (bf16[2,256,1024]{2,1,0:T(8,128)(2,1)S(1)}, bf16[2,256,1024]{2,1,0:T(8,128)(2,1)S(1)}, u32[]{:S(2)}, u32[]{:S(2)}) collective-permute-start(bf16[2,256,1024]{2,1,0:T(8,128)(2,1)S(1)} %get-tuple-element.43.qg), channel_id=1, source_target_pairs={{4,0},{5,1},{6,2},{7,3},{8,4},{9,5},{10,6},{11,7},{12,8},{13,9},{1... | collective-permute-start | bytes 3145736 | tf_op jit(solution)/shard_map/ppermute | solution.py:19
  13.1 41.2 %collective-permute-start.14 = (bf16[2,256,1024]{2,1,0:T(8,128)(2,1)S(1)}, bf16[2,256,1024]{2,1,0:T(8,128)(2,1)}, u32[]{:S(2)}, u32[]{:S(2)}) collective-permute-start(bf16[2,256,1024]{2,1,0:T(8,128)(2,1)S(1)} %get-tuple-element.44.kv), channel_id=1, source_target_pairs={{0,4},{1,5},{2,6},{3,7},{4,8},{5,9},{6,10},{7,11},{8,12},{9,13},{1... | collective-permute-start | bytes 3145736 | tf_op jit(solution)/shard_map/ppermute | solution.py:19
  14.4 43.6 %collective-permute-start = (bf16[2,256,1024]{2,1,0:T(8,128)(2,1)}, bf16[2,256,1024]{2,1,0:T(8,128)(2,1)S(1)}, u32[]{:S(2)}, u32[]{:S(2)}) collective-permute-start(bf16[2,256,1024]{2,1,0:T(8,128)(2,1)} %get-tuple-element.30), channel_id=1, source_target_pairs={{0,2},{1,3},{2,0},{3,1},{4,6},{5,7},{6,4},{7,5},{8,10},{9,11},{10,... | collective-permute-start | bytes 3145736 | tf_op jit(solution)/shard_map/ppermute | solution.py:24
  32.8 27.5 %collective-permute-start.3 = (bf16[2,256,1024]{2,1,0:T(8,128)(2,1)}, bf16[2,256,1024]{2,1,0:T(8,128)(2,1)}, u32[]{:S(2)}, u32[]{:S(2)}) collective-permute-start(bf16[2,256,1024]{2,1,0:T(8,128)(2,1)} %broadcast_select_fusion.6), channel_id=1, source_target_pairs={{0,2},{1,3},{2,0},{3,1},{4,6},{5,7},{6,4},{7,5},{8,10},{9,11},{10,... | collective-permute-start | bytes 3145736 | tf_op jit(solution)/shard_map/ppermute | solution.py:24
  34.1 76.9 %collective-permute-start.4 = (bf16[2,256,1024]{2,1,0:T(8,128)(2,1)}, bf16[2,256,1024]{2,1,0:T(8,128)(2,1)}, u32[]{:S(2)}, u32[]{:S(2)}) collective-permute-start(bf16[2,256,1024]{2,1,0:T(8,128)(2,1)} %get-tuple-element.29), channel_id=1, source_target_pairs={{0,1},{1,0},{2,3},{3,2},{4,5},{5,4},{6,7},{7,6},{8,9},{9,8},{10,11... | collective-permute-start | bytes 3145736 | tf_op jit(solution)/shard_map/ppermute | solution.py:24
  50.3 32.4 %collective-permute-start.12 = (bf16[2,256,1024]{2,1,0:T(8,128)(2,1)}, bf16[2,256,1024]{2,1,0:T(8,128)(2,1)S(1)}, u32[]{:S(2)}, u32[]{:S(2)}) collective-permute-start(bf16[2,256,1024]{2,1,0:T(8,128)(2,1)} %get-tuple-element.32), channel_id=1, source_target_pairs={{0,2},{1,3},{2,0},{3,1},{4,6},{5,7},{6,4},{7,5},{8,10},{9,11},{10,... | collective-permute-start | bytes 3145736 | tf_op jit(solution)/shard_map/ppermute | solution.py:24
  55.4 49.8 %collective-permute-start.15 = (bf16[2,256,1024]{2,1,0:T(8,128)(2,1)}, bf16[2,256,1024]{2,1,0:T(8,128)(2,1)S(1)}, u32[]{:S(2)}, u32[]{:S(2)}) collective-permute-start(bf16[2,256,1024]{2,1,0:T(8,128)(2,1)} %broadcast_select_fusion.4), channel_id=1, source_target_pairs={{0,2},{1,3},{2,0},{3,1},{4,6},{5,7},{6,4},{7,5},{8,10},{9,11},{10,... | collective-permute-start | bytes 3145736 | tf_op jit(solution)/shard_map/ppermute | solution.py:24
  58.0 54.3 %collective-permute-start.7 = (bf16[2,256,1024]{2,1,0:T(8,128)(2,1)}, bf16[2,256,1024]{2,1,0:T(8,128)(2,1)S(1)}, u32[]{:S(2)}, u32[]{:S(2)}) collective-permute-start(bf16[2,256,1024]{2,1,0:T(8,128)(2,1)} %copy-done.12), channel_id=1, source_target_pairs={{0,4},{1,5},{2,6},{3,7},{4,8},{5,9},{6,10},{7,11},{8,12},{9,13},{1... | collective-permute-start | bytes 3145736 | tf_op jit(solution)/shard_map/ppermute | solution.py:19
  61.7 54.5 %collective-permute-start.5 = (bf16[2,256,1024]{2,1,0:T(8,128)(2,1)S(1)}, bf16[2,256,1024]{2,1,0:T(8,128)(2,1)S(1)}, u32[]{:S(2)}, u32[]{:S(2)}) collective-permute-start(bf16[2,256,1024]{2,1,0:T(8,128)(2,1)S(1)} %broadcast_select_fusion.1), channel_id=1, source_target_pairs={{0,1},{1,0},{2,3},{3,2},{4,5},{5,4},{6,7},{7,6},{8,9},{9,8},{10,11... | collective-permute-start | bytes 3145736 | tf_op jit(solution)/shard_map/ppermute | solution.py:24
  82.7 49.7 %collective-permute-start.16 = (bf16[2,256,1024]{2,1,0:T(8,128)(2,1)}, bf16[2,256,1024]{2,1,0:T(8,128)(2,1)}, u32[]{:S(2)}, u32[]{:S(2)}) collective-permute-start(bf16[2,256,1024]{2,1,0:T(8,128)(2,1)} %get-tuple-element.31), channel_id=1, source_target_pairs={{0,1},{1,0},{2,3},{3,2},{4,5},{5,4},{6,7},{7,6},{8,9},{9,8},{10,11... | collective-permute-start | bytes 3145736 | tf_op jit(solution)/shard_map/ppermute | solution.py:24
  105.2 28.6 %collective-permute-start.6 = (bf16[2,256,1024]{2,1,0:T(8,128)(2,1)S(1)}, bf16[2,256,1024]{2,1,0:T(8,128)(2,1)}, u32[]{:S(2)}, u32[]{:S(2)}) collective-permute-start(bf16[2,256,1024]{2,1,0:T(8,128)(2,1)S(1)} %copy-done.9), channel_id=1, source_target_pairs={{4,0},{5,1},{6,2},{7,3},{8,4},{9,5},{10,6},{11,7},{12,8},{13,9},{1... | collective-permute-start | bytes 3145736 | tf_op jit(solution)/shard_map/ppermute | solution.py:19
  111.0 25.2 %collective-permute-start.19 = (bf16[2,256,1024]{2,1,0:T(8,128)(2,1)}, bf16[2,256,1024]{2,1,0:T(8,128)(2,1)}, u32[]{:S(2)}, u32[]{:S(2)}) collective-permute-start(bf16[2,256,1024]{2,1,0:T(8,128)(2,1)} %collective-permute-done.14.f), channel_id=1, source_target_pairs={{0,4},{1,5},{2,6},{3,7},{4,8},{5,9},{6,10},{7,11},{8,12},{9,13},{1... | collective-permute-start | bytes 3145736 | tf_op jit(solution)/shard_map/ppermute | solution.py:19
  112.3 29.4 %collective-permute-start.17 = (bf16[2,256,1024]{2,1,0:T(8,128)(2,1)}, bf16[2,256,1024]{2,1,0:T(8,128)(2,1)S(1)}, u32[]{:S(2)}, u32[]{:S(2)}) collective-permute-start(bf16[2,256,1024]{2,1,0:T(8,128)(2,1)} %broadcast_select_fusion), channel_id=1, source_target_pairs={{0,1},{1,0},{2,3},{3,2},{4,5},{5,4},{6,7},{7,6},{8,9},{9,8},{10,11... | collective-permute-start | bytes 3145736 | tf_op jit(solution)/shard_map/ppermute | solution.py:24
  116.2 63.5 %collective-permute-start.18 = (bf16[2,256,1024]{2,1,0:T(8,128)(2,1)S(1)}, bf16[2,256,1024]{2,1,0:T(8,128)(2,1)}, u32[]{:S(2)}, u32[]{:S(2)}) collective-permute-start(bf16[2,256,1024]{2,1,0:T(8,128)(2,1)S(1)} %copy-done.7), channel_id=1, source_target_pairs={{4,0},{5,1},{6,2},{7,3},{8,4},{9,5},{10,6},{11,7},{12,8},{13,9},{1... | collective-permute-start | bytes 3145736 | tf_op jit(solution)/shard_map/ppermute | solution.py:19
  132.5 21.7 %collective-permute-start.10 = (f32[32,256]{1,0:T(8,128)}, f32[32,256]{1,0:T(8,128)S(1)}, u32[]{:S(2)}, u32[]{:S(2)}) collective-permute-start(f32[32,256]{1,0:T(8,128)} %get-tuple-element.20), channel_id=1, source_target_pairs={{4,0},{5,1},{6,2},{7,3},{8,4},{9,5},{10,6},{11,7},{12,8},{13,9},{1... | collective-permute-start | bytes 98312 | tf_op jit(solution)/shard_map/ppermute | solution.py:19
  133.8 24.4 %collective-permute-start.11 = (f32[32,256]{1,0:T(8,128)}, f32[32,256]{1,0:T(8,128)S(1)}, u32[]{:S(2)}, u32[]{:S(2)}) collective-permute-start(f32[32,256]{1,0:T(8,128)} %get-tuple-element.21), channel_id=1, source_target_pairs={{8,0},{9,1},{10,2},{11,3},{12,4},{13,5},{14,6},{15,7},{24,16},{25,... | collective-permute-start | bytes 98312 | tf_op jit(solution)/shard_map/ppermute | solution.py:19
  136.2 26.6 %collective-permute-start.8 = (f32[32,256]{1,0:T(8,128)}, f32[32,256]{1,0:T(8,128)S(1)}, u32[]{:S(2)}, u32[]{:S(2)}) collective-permute-start(f32[32,256]{1,0:T(8,128)} %get-tuple-element.18), channel_id=1, source_target_pairs={{1,0},{2,1},{3,2},{4,3},{5,4},{6,5},{7,6},{8,7},{9,8},{10,9},{11,1... | collective-permute-start | bytes 98312 | tf_op jit(solution)/shard_map/ppermute | solution.py:19
  141.7 23.4 %collective-permute-start.9 = (f32[32,256]{1,0:T(8,128)}, f32[32,256]{1,0:T(8,128)S(1)}, u32[]{:S(2)}, u32[]{:S(2)}) collective-permute-start(f32[32,256]{1,0:T(8,128)} %get-tuple-element.19), channel_id=1, source_target_pairs={{2,0},{3,1},{4,2},{5,3},{6,4},{7,5},{8,6},{9,7},{10,8},{11,9},{12,... | collective-permute-start | bytes 98312 | tf_op jit(solution)/shard_map/ppermute | solution.py:19
  154.2 25.6 %collective-permute-start.20 = (f32[32,256]{1,0:T(8,128)}, f32[32,256]{1,0:T(8,128)S(1)}, u32[]{:S(2)}, u32[]{:S(2)}) collective-permute-start(f32[32,256]{1,0:T(8,128)} %get-tuple-element.24), channel_id=1, source_target_pairs={{1,0},{2,1},{3,2},{4,3},{5,4},{6,5},{7,6},{8,7},{9,8},{10,9},{11,1... | collective-permute-start | bytes 98312 | tf_op jit(solution)/shard_map/ppermute | solution.py:19
  158.2 21.6 %collective-permute-start.21 = (f32[32,256]{1,0:T(8,128)}, f32[32,256]{1,0:T(8,128)S(1)}, u32[]{:S(2)}, u32[]{:S(2)}) collective-permute-start(f32[32,256]{1,0:T(8,128)} %get-tuple-element.25), channel_id=1, source_target_pairs={{2,0},{3,1},{4,2},{5,3},{6,4},{7,5},{8,6},{9,7},{10,8},{11,9},{12,... | collective-permute-start | bytes 98312 | tf_op jit(solution)/shard_map/ppermute | solution.py:19
  162.8 17.0 %collective-permute-start.22 = (f32[32,256]{1,0:T(8,128)}, f32[32,256]{1,0:T(8,128)S(1)}, u32[]{:S(2)}, u32[]{:S(2)}) collective-permute-start(f32[32,256]{1,0:T(8,128)} %get-tuple-element.26), channel_id=1, source_target_pairs={{4,0},{5,1},{6,2},{7,3},{8,4},{9,5},{10,6},{11,7},{12,8},{13,9},{1... | collective-permute-start | bytes 98312 | tf_op jit(solution)/shard_map/ppermute | solution.py:19
  165.1 14.7 %collective-permute-start.23 = (f32[32,256]{1,0:T(8,128)}, f32[32,256]{1,0:T(8,128)S(1)}, u32[]{:S(2)}, u32[]{:S(2)}) collective-permute-start(f32[32,256]{1,0:T(8,128)} %get-tuple-element.27), channel_id=1, source_target_pairs={{8,0},{9,1},{10,2},{11,3},{12,4},{13,5},{14,6},{15,7},{24,16},{25,... | collective-permute-start | bytes 98312 | tf_op jit(solution)/shard_map/ppermute | solution.py:19
  (28 other events, 519.8 us)

commit v2 on v0

v2 whole, which is shorter than its diff:
```python
import functools

import jax
import jax.numpy as jnp
from jax import lax
from jax.experimental import pallas as pl
from jax.experimental.pallas import tpu as pltpu
from jax.sharding import PartitionSpec as P

HEADS = 16
NDIL = 4
LANES = 128
VMEM_BYTES = 40 * 2**20
CHUNKS = (2, 2)


def shift(block, distance):
    n = lax.axis_size("frame")
    return lax.ppermute(block, "frame", [(i, i + distance) for i in range(n) if 0 <= i + distance < n])


def swap(block, bit):
    n = lax.axis_size("frame")
    return lax.ppermute(block, "frame", [(i, i ^ bit) for i in range(n)])


def params():
    return pltpu.CompilerParams(vmem_limit_bytes=VMEM_BYTES, dimension_semantics=("arbitrary",))


SMEM = pl.BlockSpec(memory_space=pltpu.SMEM)


def columns(width, tile, offset=0):
    return pl.BlockSpec((2, width, tile), lambda i: (0, 0, i + offset))


def pack(flags, queries, keys, values, grad_out, bounds):
    _, patches, width = queries.shape
    n_chunks = len(bounds) - 1
    tile = LANES

    def kernel(flags_ref, q_ref, k_ref, v_ref, g_ref, *outs):
        kv_outs, qg_outs = outs[:n_chunks], outs[n_chunks:2 * n_chunks]
        y_out, c_out = outs[2 * n_chunks:]
        step = pl.program_id(0)
        kv = [r[0].T for r in (k_ref, v_ref)]
        qg = [r[0].T for r in (q_ref, g_ref)]
        for c in range(n_chunks):
            @pl.when((step >= bounds[c] // tile) & (step < bounds[c + 1] // tile))
            def _(c=c):
                for part in range(2):
                    kv_outs[c][part] = kv[part]
                    qg_outs[c][part] = qg[part]
        for out, flag in ((y_out, NDIL), (c_out, NDIL + 1)):
            @pl.when(flags_ref[flag] == 0)
            def _(out=out):
                for part in range(2):
                    out[part] = kv[part]

            @pl.when(flags_ref[flag] != 0)
            def _(out=out):
                for part in range(2):
                    out[part] = qg[part]

    def chunk_spec(c):
        lo, hi = bounds[c] // tile, bounds[c + 1] // tile
        return pl.BlockSpec((2, width, tile), lambda i: (0, 0, jnp.clip(i - lo, 0, hi - lo - 1)))

    chunk_shapes = [jax.ShapeDtypeStruct((2, width, hi - lo), jnp.bfloat16) for lo, hi in zip(bounds[:-1], bounds[1:])]
    whole_shape = jax.ShapeDtypeStruct((2, width, patches), jnp.bfloat16)
    outs = pl.pallas_call(
        kernel,
        grid=(patches // tile,),
        in_specs=[SMEM] + [pl.BlockSpec((1, tile, width), lambda i: (0, i, 0))] * 4,
        out_specs=[chunk_spec(c) for c in range(n_chunks)] * 2 + [columns(width, tile)] * 2,
        out_shape=chunk_shapes * 2 + [whole_shape] * 2,
        compiler_params=params(),
        name="pack",
    )(flags, queries, keys, values, grad_out)
    return outs[:n_chunks], outs[n_chunks:2 * n_chunks], outs[-2], outs[-1]


def source_getters(own, first, second, near, far4, far8, two_first, one_first):
    return (
        lambda i, rows: own[i, rows, :],
        lambda i, rows: jnp.where(one_first, near[0][i, rows, :], near[1][i, rows, :]),
        lambda i, rows: jnp.where(two_first, first[i, rows, :], second[i, rows, :]),
        lambda i, rows: far4[i, rows, :],
        lambda i, rows: far8[i, rows, :],
    )


def score_kernel(head_size, flags, qg, own, first, second, near_a, near_b, far4, far8, self_pair, pair1, pair2, pair4,
                 pair8, grad_query, score_ref, prob_ref):
    scale = head_size ** (-0.5)
    getters = source_getters(own, first, second, (near_a, near_b), far4, far8, flags[NDIL] > 0, flags[NDIL + 1] > 0)
    for h in range(HEADS):
        rows = slice(h * head_size, (h + 1) * head_size)
        for part, into in ((0, score_ref), (1, prob_ref)):
            mine = qg[part, rows, :].astype(jnp.float32)
            for slot, get in enumerate(getters):
                other = get(part, rows).astype(jnp.float32)
                into[slot, h:h + 1, :] = jnp.sum(mine * other, axis=0, keepdims=True)
    scores = [score_ref[slot] * scale for slot in range(NDIL + 1)]
    scores = scores[:1] + [jnp.where(flags[j] > 0, s, -1e30) for j, s in enumerate(scores[1:])]
    highest = functools.reduce(jnp.maximum, scores)
    raw = [jnp.exp(s - highest) for s in scores]
    raw = raw[:1] + [jnp.where(flags[j] > 0, r, 0.0) for j, r in enumerate(raw[1:])]
    total = functools.reduce(jnp.add, raw)
    probability = [r / total for r in raw]
    grad_probs = [prob_ref[slot] for slot in range(NDIL + 1)]
    inner = functools.reduce(jnp.add, [p * g for p, g in zip(probability, grad_probs)])
    pairs = (self_pair, pair1, pair2, pair4, pair8)
    for slot, (p, g) in enumerate(zip(probability, grad_probs)):
        pairs[slot][:HEADS, :] = p * (g - inner) * scale
        pairs[slot][HEADS:, :] = p
    for h in range(HEADS):
        rows = slice(h * head_size, (h + 1) * head_size)
        terms = [pairs[s][h:h + 1, :] * get(0, rows).astype(jnp.float32) for s, get in enumerate(getters)]
        grad_query[rows, :] = functools.reduce(jnp.add, terms).astype(jnp.bfloat16)


def scores_of(flags, qg, own, first, second, near_a, near_b, far4, far8, start, head_size):
    _, width, rows = own.shape
    tile = LANES
    chunk, whole = columns(width, tile), columns(width, tile, start // tile)
    pair = pl.BlockSpec((2 * HEADS, tile), lambda i: (0, i))
    pair_shape = jax.ShapeDtypeStruct((2 * HEADS, rows), jnp.float32)
    return pl.pallas_call(
        functools.partial(score_kernel, head_size),
        grid=(rows // tile,),
        in_specs=[SMEM, chunk, chunk, whole, chunk, whole, chunk, chunk, chunk],
        out_specs=[pair] * 5 + [pl.BlockSpec((width, tile), lambda i: (0, i))],
        out_shape=[pair_shape] * 5 + [jax.ShapeDtypeStruct((width, rows), jnp.bfloat16)],
        scratch_shapes=[pltpu.VMEM((NDIL + 1, HEADS, tile), jnp.float32)] * 2,
        compiler_params=params(),
        cost_estimate=pl.CostEstimate(flops=rows * width * 100, bytes_accessed=rows * width * 36, transcendentals=0),
        name="scores",
    )(flags, qg, own, first, second, near_a, near_b, far4, far8)


def sum_kernel(head_size, flags, own, first, second, near_a, near_b, far4, far8, self_pair, pair1, pair2, pair4, pair8,
               grad_query, w_query, w_key, w_value, *rest):
    out, key_ref, value_ref, wq, wk, wv, sems = rest[-7:]
    copies = [pltpu.make_async_copy(a, b, sems.at[i])
              for i, (a, b) in enumerate(((w_query, wq), (w_key, wk), (w_value, wv)))]

    @pl.when(pl.program_id(0) == 0)
    def _():
        for copy in copies:
            copy.start()

    getters = source_getters(own, first, second, (near_a, near_b), far4, far8, flags[NDIL] == 0, flags[NDIL + 1] == 0)
    pairs = (self_pair, pair1, pair2, pair4, pair8)
    for h in range(HEADS):
        rows = slice(h * head_size, (h + 1) * head_size)
        for part, into in ((0, key_ref), (1, value_ref)):
            row = part * HEADS + h
            terms = [pairs[s][row:row + 1, :] * get(part, rows).astype(jnp.float32) for s, get in enumerate(getters)]
            into[rows, :] = functools.reduce(jnp.add, terms).astype(jnp.bfloat16)

    @pl.when(pl.program_id(0) == 0)
    def _():
        for copy in copies:
            copy.wait()

    total = jnp.dot(wq[...], grad_query[...], preferred_element_type=jnp.float32)
    total = total + jnp.dot(wk[...], key_ref[...], preferred_element_type=jnp.float32)
    total = total + jnp.dot(wv[...], value_ref[...], preferred_element_type=jnp.float32)
    out[...] = total.T.astype(jnp.bfloat16)


def sums_of(flags, own, first, second, near_a, near_b, far4, far8, pairs, grad_query, weights, before, start, patches,
            head_size):
    _, width, rows = own.shape
    tile = 2 * LANES if rows % (2 * LANES) == 0 and start % (2 * LANES) == 0 else LANES
    chunk, whole = columns(width, tile), columns(width, tile, start // tile)
    pair = pl.BlockSpec((2 * HEADS, tile), lambda i: (0, i))
    anywhere = pl.BlockSpec(memory_space=pl.ANY)
    specs = [SMEM, chunk, whole, chunk, whole, chunk, chunk, chunk] + [pair] * 5
    specs += [pl.BlockSpec((width, tile), lambda i: (0, i))] + [anywhere] * 3
    operands = [flags, own, first, second, near_a, near_b, far4, far8, *pairs, grad_query, *weights]
    aliases = {}
    if before is not None:
        aliases = {len(operands): 0}
        specs.append(anywhere)
        operands.append(before)
    return pl.pallas_call(
        functools.partial(sum_kernel, head_size),
        grid=(rows // tile,),
        in_specs=specs,
        out_specs=pl.BlockSpec((tile, width), lambda i: (i + start // tile, 0)),
        out_shape=jax.ShapeDtypeStruct((patches, width), jnp.bfloat16),
        scratch_shapes=[pltpu.VMEM((width, tile), jnp.bfloat16)] * 2 + [pltpu.VMEM(w.shape, w.dtype) for w in weights]
        + [pltpu.SemaphoreType.DMA((3,))],
        input_output_aliases=aliases,
        compiler_params=params(),
        cost_estimate=pl.CostEstimate(flops=rows * width * 8000, bytes_accessed=rows * width * 36, transcendentals=0),
        name="sums",
    )(*operands)


def per_device(queries, keys, values, grad_out, links, w_query, w_key, w_value):
    _, patches, width = queries.shape
    head_size = width // HEADS
    me = lax.axis_index("frame")
    bit0 = lax.rem(me, 2)
    bit1 = lax.rem(me // 2, 2)
    flags = jnp.concatenate([links[0].astype(jnp.int32), jnp.stack([bit1, bit0]).astype(jnp.int32)])

    unit = patches // sum(CHUNKS)
    bounds = [0]
    for c in CHUNKS:
        bounds.append(bounds[-1] + c * unit)
    n_chunks = len(CHUNKS)

    key_value, query_grad, y_out, c_out = pack(flags, queries, keys, values, grad_out, bounds)
    up4 = [shift(kv, 4) for kv in key_value]
    down4 = [shift(qg, -4) for qg in query_grad]
    y_own = swap(y_out, 2)
    c_own = swap(c_out, 1)
    up8 = [shift(a, 4) for a in up4]
    down8 = [shift(a, -4) for a in down4]
    y_far = [swap(jnp.where(bit1 == 0, d, u), 2) for d, u in zip(down4, up4)]
    c_far = [swap(jnp.where(bit0 == bit1, y_own[:, :, bounds[i]:bounds[i + 1]], y_far[i]), 1) for i in range(n_chunks)]
    out = None
    for i in range(n_chunks):
        middle = (y_own, y_far[i], c_own, c_far[i])
        self_pair, pair1, pair2, pair4, pair8, grad_query = scores_of(
            flags, query_grad[i], key_value[i], *middle, up4[i], up8[i], bounds[i], head_size)
        came = [shift(p, -d) for p, d in ((pair1, 1), (pair2, 2), (pair4, 4), (pair8, 8))]
        out = sums_of(flags, query_grad[i], *middle, down4[i], down8[i], [self_pair, *came], grad_query,
                      (w_query, w_key, w_value), out, bounds[i], patches, head_size)
    return out[None]


def solution(mesh):
    by_frame = P(("dom", "frame"), None, None)
    return jax.shard_map(
        per_device,
        mesh=mesh,
        in_specs=(by_frame,) * 4 + (P(("dom", "frame"), None), P(), P(), P()),
        out_specs=by_frame,
        check_vma=False,
    )
```

time: 283 us -> 196 us (0.69); the launches traced: 278 us -> 195 us
  starting transfers between devices: 102 us -> 64.8 us
  local copies, waits for them, and re-layouts: 41.9 us -> 8.25 us
  Pallas kernels: 0 us -> 26.1 us
  other arithmetic: 26.3 us -> 5.56 us
  waiting for transfers between devices: 99.2 us -> 89.7 us
  matrix products: 4.93 us -> 0 us
    ppermute x12 -> x22, starting transfers between devices: 102 us -> 64.8 us  [the longest x16 55.5 us: shift(): lax.ppermute(block, 'frame', [(i, i + distance) for i in range(n) if 0 <=...]
    pallas_call x0 -> x5, Pallas kernels: none -> 26.1 us  [the longest x2 12.7 us: sums_of(): pl.pallas_call(functools.partial(sum_kernel, head_size), grid=(rows // ti...]
    convert_element_type x6 -> x0, other arithmetic: 16.1 us -> none  [the longest x4 7.67 us: spread_heads(): return a.astype(jnp.float32).reshape(frames, patches, HEADS, head_size)]
    mul x18 -> x0, local copies, waits for them, and re-layouts: 13.9 us -> none  [the longest x8 6.35 us: per_device(): came_weights[0][..., None] * spread_heads(came_inputs[0])]
    ppermute x12 -> x22, waiting for transfers between devices: 99.2 us -> 89.7 us  [the longest x16 45.5 us: shift(): lax.ppermute(block, 'frame', [(i, i + distance) for i in range(n) if 0 <=...]
    reshape x4 -> x0, local copies, waits for them, and re-layouts: 7.8 us -> none  [per_device(): jnp.stack([grad_score[j + 1], probability[j + 1]])]
    slice x5 -> x0, local copies, waits for them, and re-layouts: 7.47 us -> none  [the longest x4 6.82 us: per_device(): came_weights[0][..., None] * spread_heads(came_inputs[0])]
    another operation x6 -> x0, other arithmetic: 6.21 us -> none  [the longest x1 2.72 us: per_device(): input_pair = jnp.stack([queries, grad_out])]
  transfers between devices with their start and end apart: 12 -> 22, of which waited for: 3 -> 7; matrix products, arithmetic and copies ran while one was open for 19% -> 2% of each run, Pallas kernels for 0% -> 7%
where the time goes in v2:
time: 196 us; the launch traced here: 195 us
  waiting for transfers between devices  89.7 us (46%)
  starting transfers between devices  64.8 us (33%)
  Pallas kernels  26.1 us (13%)
  local copies, waits for them, and re-layouts  8.25 us (4%)
  other arithmetic  5.56 us (3%)
    ppermute x16, starting transfers between devices, shift(): lax.ppermute(block, 'frame', [(i, i + distance) for i in range(n) if 0 <=...  55.5 us
    ppermute x16, waiting for transfers between devices, shift(): lax.ppermute(block, 'frame', [(i, i + distance) for i in range(n) if 0 <=...  45.5 us
    ppermute x6, waiting for transfers between devices, swap(): return lax.ppermute(block, 'frame', [(i, i ^ bit) for i in range(n)])  44.2 us
    pallas_call x2, Pallas kernels, sums_of(): pl.pallas_call(functools.partial(sum_kernel, head_size), grid=(rows // ti...  12.7 us
    ppermute x6, starting transfers between devices, swap(): return lax.ppermute(block, 'frame', [(i, i ^ bit) for i in range(n)])  9.35 us
    unnamed x28, local copies, waits for them, and re-layouts  8.25 us
    pallas_call x2, Pallas kernels, scores_of(): pl.pallas_call(functools.partial(score_kernel, head_size), grid=(rows //...  8 us
    pallas_call x1, Pallas kernels, pack(): pl.pallas_call(kernel, grid=(patches // tile,), in_specs=[SMEM] + [pl.Blo...  5.46 us
  transfers between devices with their start and end apart: 22, of which 7 were waited for; matrix products, arithmetic and copies ran while one was open for 2% of the time, Pallas kernels for 7%

profile of v2, /device:TPU:27, one launch (start us, length us, event | category | flops | bytes accessed | tf_op | source)
XLA Modules:
  0.0 194.8 jit_solution(13288797991110486452)
XLA Ops:
  5.6 5.5 %pack.1 = (bf16[2,1024,256]{2,1,0:T(8,128)(2,1)}, bf16[2,1024,256]{2,1,0:T(8,128)(2,1)}, bf16[2,1024,256]{2,1,0:T(8,128)(2,1)}, bf16[2,1024,256]{2,1,0:T(8,128)(...) custom-call(s32[6]{0:T(128)S(1)} %pad_add_fusion.flags_ref.flags, ...), custom_call_target="tpu_custom_call" | custom-call | tf_op jit(solution)/shard_map/pack/pallas_call | solution.py:72
  11.1 3.0 %collective-permute-start.1 = (bf16[2,1024,256]{2,1,0:T(8,128)(2,1)S(1)}, bf16[2,1024,256]{2,1,0:T(8,128)(2,1)}, u32[]{:S(2)}, u32[]{:S(2)}) collective-permute-start(bf16[2,1024,256]{2,1,0:T(8,128)(2,1)S(1)} %get-tuple-element.23.qg.own), channel_id=1, source_target_pairs={{4,0},{5,1},{6,2},{7,3},{8,4},{9,5},{10,6},{11,7},{12,8},{13,9},{1... | collective-permute-start | bytes 3145736 | tf_op jit(solution)/shard_map/ppermute | solution.py:19
  16.4 4.1 %collective-permute-start.12 = (bf16[2,1024,256]{2,1,0:T(8,128)(2,1)}, bf16[2,1024,256]{2,1,0:T(8,128)(2,1)S(1)}, u32[]{:S(2)}, u32[]{:S(2)}) collective-permute-start(bf16[2,1024,256]{2,1,0:T(8,128)(2,1)} %get-tuple-element.33.qg.own), channel_id=1, source_target_pairs={{4,0},{5,1},{6,2},{7,3},{8,4},{9,5},{10,6},{11,7},{12,8},{13,9},{1... | collective-permute-start | bytes 3145736 | tf_op jit(solution)/shard_map/ppermute | solution.py:19
  23.1 11.9 %collective-permute-done.1.far4 = bf16[2,1024,256]{2,1,0:T(8,128)(2,1)} collective-permute-done((bf16[2,1024,256]{2,1,0:T(8,128)(2,1)S(1)}, bf16[2,1024,256]{2,1,0:T(8,128)(2,1)}, u32[]{:S(2)}, u32[]{:S(2)}) %collective-permute-start.1) | collective-permute-done | bytes 1048608 | tf_op jit(solution)/shard_map/ppermute | solution.py:19
  35.0 2.7 %collective-permute-start.4 = (bf16[2,1024,512]{2,1,0:T(8,128)(2,1)}, bf16[2,1024,512]{2,1,0:T(8,128)(2,1)}, u32[]{:S(2)}, u32[]{:S(2)}) collective-permute-start(bf16[2,1024,512]{2,1,0:T(8,128)(2,1)} %get-tuple-element.26), channel_id=1, source_target_pairs={{0,1},{1,0},{2,3},{3,2},{4,5},{5,4},{6,7},{7,6},{8,9},{9,8},{10,11... | collective-permute-start | bytes 6291464 | tf_op jit(solution)/shard_map/ppermute | solution.py:24
  37.7 3.4 %collective-permute-done.2.far4 = bf16[2,1024,256]{2,1,0:T(8,128)(2,1)} collective-permute-done((bf16[2,1024,256]{2,1,0:T(8,128)(2,1)}, bf16[2,1024,256]{2,1,0:T(8,128)(2,1)}, u32[]{:S(2)}, u32[]{:S(2)}) %collective-permute-start.2) | collective-permute-done | bytes 1048608 | tf_op jit(solution)/shard_map/ppermute | solution.py:19
  41.1 2.3 %broadcast_select_fusion.1 = bf16[2,1024,256]{2,1,0:T(8,128)(2,1)} fusion(bf16[2,1024,256]{2,1,0:T(8,128)(2,1)} %collective-permute-done.1.far4, bf16[2,1024,256]{2,1,0:T(8,128)(2,1)} %collective-permute-done.2.far4, pred[]{:T(512)S(6)} %eq.8), kind=kLoop, calls=%fused_computation.3 | loop fusion | flops 524288 | bytes 3145729 | tf_op jit(solution)/shard_map/jit(_where)/select_n | solution.py:225
  44.6 12.9 %collective-permute-done.12.far4 = bf16[2,1024,256]{2,1,0:T(8,128)(2,1)S(1)} collective-permute-done((bf16[2,1024,256]{2,1,0:T(8,128)(2,1)}, bf16[2,1024,256]{2,1,0:T(8,128)(2,1)S(1)}, u32[]{:S(2)}, u32[]{:S(2)}) %collective-permute-start.12) | collective-permute-done | bytes 1048608 | tf_op jit(solution)/shard_map/ppermute | solution.py:19
  57.6 6.0 %collective-permute-done.13.far4 = bf16[2,1024,256]{2,1,0:T(8,128)(2,1)} collective-permute-done((bf16[2,1024,256]{2,1,0:T(8,128)(2,1)}, bf16[2,1024,256]{2,1,0:T(8,128)(2,1)}, u32[]{:S(2)}, u32[]{:S(2)}) %collective-permute-start.13) | collective-permute-done | bytes 1048608 | tf_op jit(solution)/shard_map/ppermute | solution.py:19
  64.6 2.5 %collective-permute-start.14 = (bf16[2,1024,256]{2,1,0:T(8,128)(2,1)}, bf16[2,1024,256]{2,1,0:T(8,128)(2,1)S(1)}, u32[]{:S(2)}, u32[]{:S(2)}) collective-permute-start(bf16[2,1024,256]{2,1,0:T(8,128)(2,1)} %broadcast_select_fusion), channel_id=1, source_target_pairs={{0,2},{1,3},{2,0},{3,1},{4,6},{5,7},{6,4},{7,5},{8,10},{9,11},{10,... | collective-permute-start | bytes 3145736 | tf_op jit(solution)/shard_map/ppermute | solution.py:24
  68.4 21.9 %collective-permute-done.3.second = bf16[2,1024,256]{2,1,0:T(8,128)(2,1)} collective-permute-done((bf16[2,1024,256]{2,1,0:T(8,128)(2,1)}, bf16[2,1024,256]{2,1,0:T(8,128)(2,1)}, u32[]{:S(2)}, u32[]{:S(2)}) %collective-permute-start.3) | collective-permute-done | bytes 1048608 | tf_op jit(solution)/shard_map/ppermute | solution.py:24
  90.3 22.4 %collective-permute-done.14.second = bf16[2,1024,256]{2,1,0:T(8,128)(2,1)S(1)} collective-permute-done((bf16[2,1024,256]{2,1,0:T(8,128)(2,1)}, bf16[2,1024,256]{2,1,0:T(8,128)(2,1)S(1)}, u32[]{:S(2)}, u32[]{:S(2)}) %collective-permute-start.14) | collective-permute-done | bytes 1048608 | tf_op jit(solution)/shard_map/ppermute | solution.py:24
  116.6 4.7 %collective-permute-start.16 = (bf16[2,1024,256]{2,1,0:T(8,128)(2,1)S(1)}, bf16[2,1024,256]{2,1,0:T(8,128)(2,1)S(1)}, u32[]{:S(2)}, u32[]{:S(2)}) collective-permute-start(bf16[2,1024,256]{2,1,0:T(8,128)(2,1)S(1)} %copy-done.3), channel_id=1, source_target_pairs={{4,0},{5,1},{6,2},{7,3},{8,4},{9,5},{10,6},{11,7},{12,8},{13,9},{1... | collective-permute-start | bytes 3145736 | tf_op jit(solution)/shard_map/ppermute | solution.py:19
  121.7 3.6 %collective-permute-start.6 = (bf16[2,1024,256]{2,1,0:T(8,128)(2,1)}, bf16[2,1024,256]{2,1,0:T(8,128)(2,1)S(1)}, u32[]{:S(2)}, u32[]{:S(2)}) collective-permute-start(bf16[2,1024,256]{2,1,0:T(8,128)(2,1)} %collective-permute-done.1.far4), channel_id=1, source_target_pairs={{4,0},{5,1},{6,2},{7,3},{8,4},{9,5},{10,6},{11,7},{12,8},{13,9},{1... | collective-permute-start | bytes 3145736 | tf_op jit(solution)/shard_map/ppermute | solution.py:19
  125.4 4.0 %scores.3 = (f32[32,256]{1,0:T(8,128)S(1)}, f32[32,256]{1,0:T(8,128)S(1)}, f32[32,256]{1,0:T(8,128)S(1)}, f32[32,256]{1,0:T(8,128)S(1)}, f32[32,256]{1,0:T(8,128)S(1)}, /*index=5*/bf16[1024,256]{1,0:T(8,128)(2,1)S(1)}) custom-call(s32[6]{0:T(128)S(1)} %pad_add_fusion.flags_ref.flags, bf16[2,1024,256]{2,1,0:T(8,128)(2,1)} %get-tuple-element.33.qg.own, ...), custom_call_target="tpu_custom_call" | custom-call | flops 26214400 | bytes 9437184 | tf_op jit(solution)/shard_map/scores/pallas_call | solution.py:130
  129.4 2.4 %collective-permute-start.18 = (f32[32,256]{1,0:T(8,128)S(1)}, f32[32,256]{1,0:T(8,128)S(1)}, u32[]{:S(2)}, u32[]{:S(2)}) collective-permute-start(f32[32,256]{1,0:T(8,128)S(1)} %get-tuple-element.36), channel_id=1, source_target_pairs={{1,0},{2,1},{3,2},{4,3},{5,4},{6,5},{7,6},{8,7},{9,8},{10,9},{11,1... | collective-permute-start | bytes 98312 | tf_op jit(solution)/shard_map/ppermute | solution.py:19
  131.8 11.3 %collective-permute-done.7.far8 = bf16[2,1024,256]{2,1,0:T(8,128)(2,1)S(1)} collective-permute-done((bf16[2,1024,256]{2,1,0:T(8,128)(2,1)}, bf16[2,1024,256]{2,1,0:T(8,128)(2,1)S(1)}, u32[]{:S(2)}, u32[]{:S(2)}) %collective-permute-start.7) | collective-permute-done | bytes 1048608 | tf_op jit(solution)/shard_map/ppermute | solution.py:19
  143.0 5.3 %collective-permute-start.19 = (f32[32,256]{1,0:T(8,128)S(1)}, f32[32,256]{1,0:T(8,128)S(1)}, u32[]{:S(2)}, u32[]{:S(2)}) collective-permute-start(f32[32,256]{1,0:T(8,128)S(1)} %get-tuple-element.37), channel_id=1, source_target_pairs={{2,0},{3,1},{4,2},{5,3},{6,4},{7,5},{8,6},{9,7},{10,8},{11,9},{12,... | collective-permute-start | bytes 98312 | tf_op jit(solution)/shard_map/ppermute | solution.py:19
  151.9 4.0 %scores.2 = (f32[32,256]{1,0:T(8,128)S(1)}, f32[32,256]{1,0:T(8,128)S(1)}, f32[32,256]{1,0:T(8,128)S(1)}, f32[32,256]{1,0:T(8,128)S(1)}, f32[32,256]{1,0:T(8,128)S(1)}, /*index=5*/bf16[1024,256]{1,0:T(8,128)(2,1)S(1)}) custom-call(s32[6]{0:T(128)S(1)} %pad_add_fusion.flags_ref.flags, bf16[2,1024,256]{2,1,0:T(8,128)(2,1)S(1)} %copy-done.5, ...), custom_call_target="tpu_custom_call" | custom-call | flops 26214400 | bytes 9437184 | tf_op jit(solution)/shard_map/scores/pallas_call | solution.py:130
  155.9 14.2 %collective-permute-start.8 = (f32[32,256]{1,0:T(8,128)S(1)}, f32[32,256]{1,0:T(8,128)S(1)}, u32[]{:S(2)}, u32[]{:S(2)}) collective-permute-start(f32[32,256]{1,0:T(8,128)S(1)} %get-tuple-element.28), channel_id=1, source_target_pairs={{1,0},{2,1},{3,2},{4,3},{5,4},{6,5},{7,6},{8,7},{9,8},{10,9},{11,1... | collective-permute-start | bytes 98312 | tf_op jit(solution)/shard_map/ppermute | solution.py:19
  170.1 4.3 %collective-permute-start.9 = (f32[32,256]{1,0:T(8,128)S(1)}, f32[32,256]{1,0:T(8,128)S(1)}, u32[]{:S(2)}, u32[]{:S(2)}) collective-permute-start(f32[32,256]{1,0:T(8,128)S(1)} %get-tuple-element.29), channel_id=1, source_target_pairs={{2,0},{3,1},{4,2},{5,3},{6,4},{7,5},{8,6},{9,7},{10,8},{11,9},{12,... | collective-permute-start | bytes 98312 | tf_op jit(solution)/shard_map/ppermute | solution.py:19
  174.5 4.0 %collective-permute-start.10 = (f32[32,256]{1,0:T(8,128)S(1)}, f32[32,256]{1,0:T(8,128)S(1)}, u32[]{:S(2)}, u32[]{:S(2)}) collective-permute-start(f32[32,256]{1,0:T(8,128)S(1)} %get-tuple-element.30), channel_id=1, source_target_pairs={{4,0},{5,1},{6,2},{7,3},{8,4},{9,5},{10,6},{11,7},{12,8},{13,9},{1... | collective-permute-start | bytes 98312 | tf_op jit(solution)/shard_map/ppermute | solution.py:19
  179.8 6.2 %sums.2.rest_0_ = bf16[512,1024]{1,0:T(8,128)(2,1)} custom-call(s32[6]{0:T(128)S(1)} %pad_add_fusion.flags_ref.flags, bf16[2,1024,256]{2,1,0:T(8,128)(2,1)} %get-tuple-element.33.qg.own, bf16[2,1024,512]{2,1,0:T(8,128)(2,1)S(1)} %collective-permute-done.first, bf16[2,1024,256]{2,1,0:T(8,128)(2,1)S(1)} %collective-permute-done.14.second, ...), custom_call_target="tpu_custom_call" | custom-call | flops 2097152000 | bytes 9437184 | tf_op jit(solution)/shard_map/sums/pallas_call | solution.py:189
  188.4 6.4 %sums.3 = bf16[512,1024]{1,0:T(8,128)(2,1)} custom-call(s32[6]{0:T(128)S(1)} %pad_add_fusion.flags_ref.flags, bf16[2,1024,256]{2,1,0:T(8,128)(2,1)S(1)} %copy-done.5, bf16[2,1024,512]{2,1,0:T(8,128)(2,1)S(1)} %collective-permute-done.first, bf16[2,1024,256]{2,1,0:T(8,128)(2,1)} %collective-permute-done.3.second, ...), custom_call_target="tpu_custom_call", output_to_operand_aliasing={{}: (17, {})} | custom-call | flops 2097152000 | bytes 9437184 | tf_op jit(solution)/shard_map/sums/pallas_call | solution.py:189
  (57 shorter events, 25.6 us)
Async XLA Ops:
  11.1 23.9 %collective-permute-start.1 = (bf16[2,1024,256]{2,1,0:T(8,128)(2,1)S(1)}, bf16[2,1024,256]{2,1,0:T(8,128)(2,1)}, u32[]{:S(2)}, u32[]{:S(2)}) collective-permute-start(bf16[2,1024,256]{2,1,0:T(8,128)(2,1)S(1)} %get-tuple-element.23.qg.own), channel_id=1, source_target_pairs={{4,0},{5,1},{6,2},{7,3},{8,4},{9,5},{10,6},{11,7},{12,8},{13,9},{1... | collective-permute-start | bytes 3145736 | tf_op jit(solution)/shard_map/ppermute | solution.py:19
  15.2 25.9 %collective-permute-start.2 = (bf16[2,1024,256]{2,1,0:T(8,128)(2,1)}, bf16[2,1024,256]{2,1,0:T(8,128)(2,1)}, u32[]{:S(2)}, u32[]{:S(2)}) collective-permute-start(bf16[2,1024,256]{2,1,0:T(8,128)(2,1)} %get-tuple-element.25.own), channel_id=1, source_target_pairs={{0,4},{1,5},{2,6},{3,7},{4,8},{5,9},{6,10},{7,11},{8,12},{9,13},{1... | collective-permute-start | bytes 3145736 | tf_op jit(solution)/shard_map/ppermute | solution.py:19
  16.4 41.1 %collective-permute-start.12 = (bf16[2,1024,256]{2,1,0:T(8,128)(2,1)}, bf16[2,1024,256]{2,1,0:T(8,128)(2,1)S(1)}, u32[]{:S(2)}, u32[]{:S(2)}) collective-permute-start(bf16[2,1024,256]{2,1,0:T(8,128)(2,1)} %get-tuple-element.33.qg.own), channel_id=1, source_target_pairs={{4,0},{5,1},{6,2},{7,3},{8,4},{9,5},{10,6},{11,7},{12,8},{13,9},{1... | collective-permute-start | bytes 3145736 | tf_op jit(solution)/shard_map/ppermute | solution.py:19
  20.5 43.0 %collective-permute-start.13 = (bf16[2,1024,256]{2,1,0:T(8,128)(2,1)}, bf16[2,1024,256]{2,1,0:T(8,128)(2,1)}, u32[]{:S(2)}, u32[]{:S(2)}) collective-permute-start(bf16[2,1024,256]{2,1,0:T(8,128)(2,1)} %get-tuple-element.34.own), channel_id=1, source_target_pairs={{0,4},{1,5},{2,6},{3,7},{4,8},{5,9},{6,10},{7,11},{8,12},{9,13},{1... | collective-permute-start | bytes 3145736 | tf_op jit(solution)/shard_map/ppermute | solution.py:19
  21.8 46.6 %collective-permute-start = (bf16[2,1024,512]{2,1,0:T(8,128)(2,1)}, bf16[2,1024,512]{2,1,0:T(8,128)(2,1)S(1)}, u32[]{:S(2)}, u32[]{:S(2)}) collective-permute-start(bf16[2,1024,512]{2,1,0:T(8,128)(2,1)} %get-tuple-element.24), channel_id=1, source_target_pairs={{0,2},{1,3},{2,0},{3,1},{4,6},{5,7},{6,4},{7,5},{8,10},{9,11},{10,... | collective-permute-start | bytes 6291464 | tf_op jit(solution)/shard_map/ppermute | solution.py:24
  35.0 86.4 %collective-permute-start.4 = (bf16[2,1024,512]{2,1,0:T(8,128)(2,1)}, bf16[2,1024,512]{2,1,0:T(8,128)(2,1)}, u32[]{:S(2)}, u32[]{:S(2)}) collective-permute-start(bf16[2,1024,512]{2,1,0:T(8,128)(2,1)} %get-tuple-element.26), channel_id=1, source_target_pairs={{0,1},{1,0},{2,3},{3,2},{4,5},{5,4},{6,7},{7,6},{8,9},{9,8},{10,11... | collective-permute-start | bytes 6291464 | tf_op jit(solution)/shard_map/ppermute | solution.py:24
  43.4 46.9 %collective-permute-start.3 = (bf16[2,1024,256]{2,1,0:T(8,128)(2,1)}, bf16[2,1024,256]{2,1,0:T(8,128)(2,1)}, u32[]{:S(2)}, u32[]{:S(2)}) collective-permute-start(bf16[2,1024,256]{2,1,0:T(8,128)(2,1)} %broadcast_select_fusion.1), channel_id=1, source_target_pairs={{0,2},{1,3},{2,0},{3,1},{4,6},{5,7},{6,4},{7,5},{8,10},{9,11},{10,... | collective-permute-start | bytes 3145736 | tf_op jit(solution)/shard_map/ppermute | solution.py:24
  64.6 48.0 %collective-permute-start.14 = (bf16[2,1024,256]{2,1,0:T(8,128)(2,1)}, bf16[2,1024,256]{2,1,0:T(8,128)(2,1)S(1)}, u32[]{:S(2)}, u32[]{:S(2)}) collective-permute-start(bf16[2,1024,256]{2,1,0:T(8,128)(2,1)} %broadcast_select_fusion), channel_id=1, source_target_pairs={{0,2},{1,3},{2,0},{3,1},{4,6},{5,7},{6,4},{7,5},{8,10},{9,11},{10,... | collective-permute-start | bytes 3145736 | tf_op jit(solution)/shard_map/ppermute | solution.py:24
  67.1 54.6 %collective-permute-start.17 = (bf16[2,1024,256]{2,1,0:T(8,128)(2,1)}, bf16[2,1024,256]{2,1,0:T(8,128)(2,1)}, u32[]{:S(2)}, u32[]{:S(2)}) collective-permute-start(bf16[2,1024,256]{2,1,0:T(8,128)(2,1)} %collective-permute-done.13.far4), channel_id=1, source_target_pairs={{0,4},{1,5},{2,6},{3,7},{4,8},{5,9},{6,10},{7,11},{8,12},{9,13},{1... | collective-permute-start | bytes 3145736 | tf_op jit(solution)/shard_map/ppermute | solution.py:19
  68.4 48.3 %copy-start.3 = (bf16[2,1024,256]{2,1,0:T(8,128)(2,1)S(1)}, bf16[2,1024,256]{2,1,0:T(8,128)(2,1)}, u32[]{:S(2)}) copy-start(bf16[2,1024,256]{2,1,0:T(8,128)(2,1)} %copy-done.2) | copy-start | bytes 3145732
  114.1 11.3 %collective-permute-start.15 = (bf16[2,1024,256]{2,1,0:T(8,128)(2,1)S(1)}, bf16[2,1024,256]{2,1,0:T(8,128)(2,1)S(1)}, u32[]{:S(2)}, u32[]{:S(2)}) collective-permute-start(bf16[2,1024,256]{2,1,0:T(8,128)(2,1)S(1)} %get-tuple-element.41), channel_id=1, source_target_pairs={{0,1},{1,0},{2,3},{3,2},{4,5},{5,4},{6,7},{7,6},{8,9},{9,8},{10,11... | collective-permute-start | bytes 3145736 | tf_op jit(solution)/shard_map/ppermute | solution.py:24
  115.3 27.7 %collective-permute-start.7 = (bf16[2,1024,256]{2,1,0:T(8,128)(2,1)}, bf16[2,1024,256]{2,1,0:T(8,128)(2,1)S(1)}, u32[]{:S(2)}, u32[]{:S(2)}) collective-permute-start(bf16[2,1024,256]{2,1,0:T(8,128)(2,1)} %collective-permute-done.2.far4), channel_id=1, source_target_pairs={{0,4},{1,5},{2,6},{3,7},{4,8},{5,9},{6,10},{7,11},{8,12},{9,13},{1... | collective-permute-start | bytes 3145736 | tf_op jit(solution)/shard_map/ppermute | solution.py:19
  116.6 31.7 %collective-permute-start.16 = (bf16[2,1024,256]{2,1,0:T(8,128)(2,1)S(1)}, bf16[2,1024,256]{2,1,0:T(8,128)(2,1)S(1)}, u32[]{:S(2)}, u32[]{:S(2)}) collective-permute-start(bf16[2,1024,256]{2,1,0:T(8,128)(2,1)S(1)} %copy-done.3), channel_id=1, source_target_pairs={{4,0},{5,1},{6,2},{7,3},{8,4},{9,5},{10,6},{11,7},{12,8},{13,9},{1... | collective-permute-start | bytes 3145736 | tf_op jit(solution)/shard_map/ppermute | solution.py:19
  121.3 30.5 %copy-start.5 = (bf16[2,1024,256]{2,1,0:T(8,128)(2,1)S(1)}, bf16[2,1024,256]{2,1,0:T(8,128)(2,1)}, u32[]{:S(2)}) copy-start(bf16[2,1024,256]{2,1,0:T(8,128)(2,1)} %copy-done.4) | copy-start | bytes 3145732
  121.3 28.9 %collective-permute-start.5 = (bf16[2,1024,256]{2,1,0:T(8,128)(2,1)S(1)}, bf16[2,1024,256]{2,1,0:T(8,128)(2,1)S(1)}, u32[]{:S(2)}, u32[]{:S(2)}) collective-permute-start(bf16[2,1024,256]{2,1,0:T(8,128)(2,1)S(1)} %get-tuple-element.42), channel_id=1, source_target_pairs={{0,1},{1,0},{2,3},{3,2},{4,5},{5,4},{6,7},{7,6},{8,9},{9,8},{10,11... | collective-permute-start | bytes 3145736 | tf_op jit(solution)/shard_map/ppermute | solution.py:24
  121.7 64.3 %collective-permute-start.6 = (bf16[2,1024,256]{2,1,0:T(8,128)(2,1)}, bf16[2,1024,256]{2,1,0:T(8,128)(2,1)S(1)}, u32[]{:S(2)}, u32[]{:S(2)}) collective-permute-start(bf16[2,1024,256]{2,1,0:T(8,128)(2,1)} %collective-permute-done.1.far4), channel_id=1, source_target_pairs={{4,0},{5,1},{6,2},{7,3},{8,4},{9,5},{10,6},{11,7},{12,8},{13,9},{1... | collective-permute-start | bytes 3145736 | tf_op jit(solution)/shard_map/ppermute | solution.py:19
  129.4 26.4 %collective-permute-start.18 = (f32[32,256]{1,0:T(8,128)S(1)}, f32[32,256]{1,0:T(8,128)S(1)}, u32[]{:S(2)}, u32[]{:S(2)}) collective-permute-start(f32[32,256]{1,0:T(8,128)S(1)} %get-tuple-element.36), channel_id=1, source_target_pairs={{1,0},{2,1},{3,2},{4,3},{5,4},{6,5},{7,6},{8,7},{9,8},{10,9},{11,1... | collective-permute-start | bytes 98312 | tf_op jit(solution)/shard_map/ppermute | solution.py:19
  143.0 27.1 %collective-permute-start.19 = (f32[32,256]{1,0:T(8,128)S(1)}, f32[32,256]{1,0:T(8,128)S(1)}, u32[]{:S(2)}, u32[]{:S(2)}) collective-permute-start(f32[32,256]{1,0:T(8,128)S(1)} %get-tuple-element.37), channel_id=1, source_target_pairs={{2,0},{3,1},{4,2},{5,3},{6,4},{7,5},{8,6},{9,7},{10,8},{11,9},{12,... | collective-permute-start | bytes 98312 | tf_op jit(solution)/shard_map/ppermute | solution.py:19
  148.4 26.1 %collective-permute-start.20 = (f32[32,256]{1,0:T(8,128)S(1)}, f32[32,256]{1,0:T(8,128)S(1)}, u32[]{:S(2)}, u32[]{:S(2)}) collective-permute-start(f32[32,256]{1,0:T(8,128)S(1)} %get-tuple-element.38), channel_id=1, source_target_pairs={{4,0},{5,1},{6,2},{7,3},{8,4},{9,5},{10,6},{11,7},{12,8},{13,9},{1... | collective-permute-start | bytes 98312 | tf_op jit(solution)/shard_map/ppermute | solution.py:19
  150.3 28.2 %collective-permute-start.21 = (f32[32,256]{1,0:T(8,128)S(1)}, f32[32,256]{1,0:T(8,128)S(1)}, u32[]{:S(2)}, u32[]{:S(2)}) collective-permute-start(f32[32,256]{1,0:T(8,128)S(1)} %get-tuple-element.39), channel_id=1, source_target_pairs={{8,0},{9,1},{10,2},{11,3},{12,4},{13,5},{14,6},{15,7},{24,16},{25,... | collective-permute-start | bytes 98312 | tf_op jit(solution)/shard_map/ppermute | solution.py:19
  155.9 31.3 %collective-permute-start.8 = (f32[32,256]{1,0:T(8,128)S(1)}, f32[32,256]{1,0:T(8,128)S(1)}, u32[]{:S(2)}, u32[]{:S(2)}) collective-permute-start(f32[32,256]{1,0:T(8,128)S(1)} %get-tuple-element.28), channel_id=1, source_target_pairs={{1,0},{2,1},{3,2},{4,3},{5,4},{6,5},{7,6},{8,7},{9,8},{10,9},{11,1... | collective-permute-start | bytes 98312 | tf_op jit(solution)/shard_map/ppermute | solution.py:19
  170.1 17.0 %collective-permute-start.9 = (f32[32,256]{1,0:T(8,128)S(1)}, f32[32,256]{1,0:T(8,128)S(1)}, u32[]{:S(2)}, u32[]{:S(2)}) collective-permute-start(f32[32,256]{1,0:T(8,128)S(1)} %get-tuple-element.29), channel_id=1, source_target_pairs={{2,0},{3,1},{4,2},{5,3},{6,4},{7,5},{8,6},{9,7},{10,8},{11,9},{12,... | collective-permute-start | bytes 98312 | tf_op jit(solution)/shard_map/ppermute | solution.py:19
  174.5 12.7 %collective-permute-start.10 = (f32[32,256]{1,0:T(8,128)S(1)}, f32[32,256]{1,0:T(8,128)S(1)}, u32[]{:S(2)}, u32[]{:S(2)}) collective-permute-start(f32[32,256]{1,0:T(8,128)S(1)} %get-tuple-element.30), channel_id=1, source_target_pairs={{4,0},{5,1},{6,2},{7,3},{8,4},{9,5},{10,6},{11,7},{12,8},{13,9},{1... | collective-permute-start | bytes 98312 | tf_op jit(solution)/shard_map/ppermute | solution.py:19
  178.5 8.7 %collective-permute-start.11 = (f32[32,256]{1,0:T(8,128)S(1)}, f32[32,256]{1,0:T(8,128)S(1)}, u32[]{:S(2)}, u32[]{:S(2)}) collective-permute-start(f32[32,256]{1,0:T(8,128)S(1)} %get-tuple-element.31), channel_id=1, source_target_pairs={{8,0},{9,1},{10,2},{11,3},{12,4},{13,5},{14,6},{15,7},{24,16},{25,... | collective-permute-start | bytes 98312 | tf_op jit(solution)/shard_map/ppermute | solution.py:19
  (12 other events, 86.2 us)

commit v3 on v0

v3 whole, which is shorter than its diff:
```python
import functools

import jax
import jax.numpy as jnp
from jax import lax
from jax.experimental import pallas as pl
from jax.experimental.pallas import tpu as pltpu
from jax.sharding import PartitionSpec as P

HEADS = 16
NDIL = 4
LANES = 128
SUBLANES = 8
UNIT = 256
VMEM_BYTES = 32 * 2**20
PACK_VMEM_BYTES = 60 * 2**20


def shift(block, distance):
    n = lax.axis_size("frame")
    return lax.ppermute(block, "frame", [(i, i + distance) for i in range(n) if 0 <= i + distance < n])


def swap(block, bit):
    n = lax.axis_size("frame")
    return lax.ppermute(block, "frame", [(i, i ^ bit) for i in range(n)])


def place_bit(bit):
    return lax.rem(lax.axis_index("frame") // 2**bit, 2)


def params():
    return pltpu.CompilerParams(vmem_limit_bytes=VMEM_BYTES)


SMEM = pl.BlockSpec(memory_space=pltpu.SMEM)
VMEM = pl.BlockSpec(memory_space=pltpu.VMEM)
PIN = False


def columns(width, tile, offset=0):
    return pl.BlockSpec((2, width, tile), lambda i: (0, 0, i + offset))


def after(block, *done):
    return lax.optimization_barrier((block, *done))[0]


def pack(queries, keys, values, grad_out):
    _, patches, width = queries.shape
    tile = LANES
    steps = patches // tile
    half = steps // 2

    def kernel(q_ref, k_ref, v_ref, g_ref, kv0, kv1, qg0, qg1, y_out):
        step = pl.program_id(0)
        unit = jnp.where(lax.broadcasted_iota(jnp.int32, (UNIT, UNIT), 0) == lax.broadcasted_iota(
            jnp.int32, (UNIT, UNIT), 1), 1.0, 0.0).astype(jnp.bfloat16)

        def turned(ref):
            blocks = [lax.dot_general(unit, ref[0, :, i:i + UNIT], (((1,), (1,)), ((), ())),
                                      preferred_element_type=jnp.float32) for i in range(0, width, UNIT)]
            return jnp.concatenate([b.astype(jnp.bfloat16) for b in blocks], axis=0)

        kv = [turned(r) for r in (k_ref, v_ref)]
        qg = [turned(r) for r in (q_ref, g_ref)]
        for kv_out, qg_out, mine in ((kv0, qg0, step < half), (kv1, qg1, step >= half)):
            @pl.when(mine)
            def _(kv_out=kv_out, qg_out=qg_out):
                for part in range(2):
                    kv_out[part] = kv[part]
                    qg_out[part] = qg[part]
        for part in range(2):
            y_out[part] = jnp.where(place_bit(1) == 0, kv[part], qg[part])

    first = pl.BlockSpec((2, width, tile), lambda i: (0, 0, jnp.minimum(i, half - 1)))
    second = pl.BlockSpec((2, width, tile), lambda i: (0, 0, jnp.maximum(i - half, 0)))
    half_shape = jax.ShapeDtypeStruct((2, width, patches // 2), jnp.bfloat16)
    whole_shape = jax.ShapeDtypeStruct((2, width, patches), jnp.bfloat16)
    return pl.pallas_call(
        kernel,
        grid=(steps,),
        in_specs=[pl.BlockSpec((1, tile, width), lambda i: (0, i, 0))] * 4,
        out_specs=[first, second] * 2 + [columns(width, tile)],
        out_shape=[half_shape] * 4 + [whole_shape],
        compiler_params=pltpu.CompilerParams(vmem_limit_bytes=PACK_VMEM_BYTES),
        name="pack",
    )(queries, keys, values, grad_out)


def in_vmem(arrays):
    return [pltpu.with_memory_space_constraint(a, pltpu.VMEM) for a in arrays] if PIN else list(arrays)


def source_getters(own, y_own, y_far, c_own, c_far, far4, far8, wanted, here, there):
    def pick(first, second, bit, place):
        use_first = place_bit(bit) == wanted
        return lambda i, rows: jnp.where(use_first, first[i, rows, place], second[i, rows, here])

    return (
        lambda i, rows: own[i, rows, here],
        pick(c_own, c_far, 0, here),
        pick(y_own, y_far, 1, there),
        lambda i, rows: far4[i, rows, here],
        lambda i, rows: far8[i, rows, here],
    )


def head_slices(width):
    size = width // HEADS
    return [slice(h * size, (h + 1) * size) for h in range(HEADS)]


def lanes(step, start):
    here = pl.ds(pl.multiple_of(step * LANES, LANES), LANES)
    return here, pl.ds(pl.multiple_of(step * LANES + start, LANES), LANES)


def score_kernel(start, links, qg, own, y_own, y_far, c_own, c_far, far4, far8, self_pair, pair1, pair2, pair4, pair8,
                 grad_query, score_ref, prob_ref):
    _, width, patches = own.shape
    scale = (width // HEADS) ** (-0.5)
    pairs = (self_pair, pair1, pair2, pair4, pair8)

    @pl.loop(0, patches // LANES)
    def _(step):
        here, there = lanes(step, start)
        getters = source_getters(own, y_own, y_far, c_own, c_far, far4, far8, 1, here, there)
        for h, rows in enumerate(head_slices(width)):
            for part, into in ((0, score_ref), (1, prob_ref)):
                mine = qg[part, rows, here].astype(jnp.float32)
                for slot, get in enumerate(getters):
                    product = mine * get(part, rows).astype(jnp.float32)
                    into[slot, h * SUBLANES:(h + 1) * SUBLANES, :] = jnp.sum(
                        product.reshape(-1, SUBLANES, LANES), axis=0)

        def total_of(ref, slot):
            parts = [ref[slot, pl.ds(i, HEADS, stride=SUBLANES), :] for i in range(SUBLANES)]
            while len(parts) > 1:
                parts = [a + b for a, b in zip(parts[::2], parts[1::2])]
            return parts[0]

        scores = [total_of(score_ref, slot) * scale for slot in range(NDIL + 1)]
        scores = scores[:1] + [jnp.where(links[0, j] > 0, s, -1e30) for j, s in enumerate(scores[1:])]
        highest = functools.reduce(jnp.maximum, scores)
        raw = [jnp.exp(s - highest) for s in scores]
        raw = raw[:1] + [jnp.where(links[0, j] > 0, r, 0.0) for j, r in enumerate(raw[1:])]
        total = functools.reduce(jnp.add, raw)
        probability = [r / total for r in raw]
        grad_probs = [total_of(prob_ref, slot) for slot in range(NDIL + 1)]
        inner = functools.reduce(jnp.add, [p * g for p, g in zip(probability, grad_probs)])
        for slot, (p, g) in enumerate(zip(probability, grad_probs)):
            pairs[slot][:HEADS, here] = p * (g - inner) * scale
            pairs[slot][HEADS:, here] = p
        for h, rows in enumerate(head_slices(width)):
            terms = [pairs[s][h:h + 1, here] * get(0, rows).astype(jnp.float32) for s, get in enumerate(getters)]
            grad_query[rows, here] = functools.reduce(jnp.add, terms).astype(jnp.bfloat16)


def scores_of(links, qg, own, two, one, far4, far8, start):
    _, width, rows = own.shape
    pair_shape = jax.ShapeDtypeStruct((2 * HEADS, rows), jnp.float32)
    return pl.pallas_call(
        functools.partial(score_kernel, start),
        in_specs=[SMEM] + [VMEM] * 8,
        out_specs=[VMEM] * 6,
        out_shape=[pair_shape] * 5 + [jax.ShapeDtypeStruct((width, rows), jnp.bfloat16)],
        scratch_shapes=[pltpu.VMEM((NDIL + 1, HEADS * SUBLANES, LANES), jnp.float32)] * 2,
        compiler_params=params(),
        cost_estimate=pl.CostEstimate(flops=rows * width * 100, bytes_accessed=rows * width * 36, transcendentals=0),
        name="scores",
    )(links, *in_vmem([qg, own, *two, *one, far4, far8]))


def project_kernel(grad_query, w_query, out):
    out[...] = jnp.dot(w_query[...], grad_query[...], preferred_element_type=jnp.float32)


def project(grad_query, w_query):
    width, rows = grad_query.shape
    return pl.pallas_call(
        project_kernel,
        in_specs=[VMEM] * 2,
        out_specs=VMEM,
        out_shape=jax.ShapeDtypeStruct((w_query.shape[0], rows), jnp.float32),
        compiler_params=params(),
        cost_estimate=pl.CostEstimate(flops=2 * rows * w_query.size, bytes_accessed=2 * w_query.size, transcendentals=0),
        name="project",
    )(*in_vmem([grad_query, w_query]))


def sum_kernel(start, own, y_own, y_far, c_own, c_far, far4, far8, self_pair, pair1, pair2, pair4, pair8,
               query_part, w_key, w_value, *rest):
    out, key_ref, value_ref, result, sem = rest[-5:]
    _, width, patches = own.shape
    pairs = (self_pair, pair1, pair2, pair4, pair8)

    @pl.loop(0, patches // LANES)
    def _(step):
        here, there = lanes(step, start)
        getters = source_getters(own, y_own, y_far, c_own, c_far, far4, far8, 0, here, there)
        for h, rows in enumerate(head_slices(width)):
            for part, into in ((0, key_ref), (1, value_ref)):
                row = part * HEADS + h
                terms = [pairs[s][row:row + 1, here] * get(part, rows).astype(jnp.float32) for s, get in enumerate(getters)]
                into[rows, here] = functools.reduce(jnp.add, terms).astype(jnp.bfloat16)

    total = query_part[...] + jnp.dot(w_key[...], key_ref[...], preferred_element_type=jnp.float32)
    total = total + jnp.dot(w_value[...], value_ref[...], preferred_element_type=jnp.float32)
    result[...] = total.astype(jnp.bfloat16).T
    copy = pltpu.make_async_copy(result, out.at[pl.ds(start, patches), :], sem)
    copy.start()
    copy.wait()


def sums_of(own, two, one, far4, far8, pairs, query_part, weights, before, start, patches):
    _, width, rows = own.shape
    anywhere = pl.BlockSpec(memory_space=pl.ANY)
    operands = [*in_vmem([own, *two, *one, far4, far8, *pairs, query_part, *weights])]
    specs = [VMEM] * len(operands)
    aliases = {}
    if before is not None:
        aliases = {len(operands): 0}
        specs.append(anywhere)
        operands.append(before)
    return pl.pallas_call(
        functools.partial(sum_kernel, start),
        in_specs=specs,
        out_specs=anywhere,
        out_shape=jax.ShapeDtypeStruct((patches, width), jnp.bfloat16),
        scratch_shapes=[pltpu.VMEM((width, rows), jnp.bfloat16)] * 2
        + [pltpu.VMEM((rows, width), jnp.bfloat16), pltpu.SemaphoreType.DMA],
        input_output_aliases=aliases,
        compiler_params=params(),
        cost_estimate=pl.CostEstimate(flops=rows * width * 8000, bytes_accessed=rows * width * 36, transcendentals=0),
        name="sums",
    )(*operands)


def per_device(queries, keys, values, grad_out, links, w_query, w_key, w_value):
    patches = queries.shape[1]
    bit0, bit1 = place_bit(0), place_bit(1)
    half = patches // 2

    def choose(bit, if_set, if_clear):
        return jnp.where(bit == 1, if_set, if_clear)

    kv0, kv1, qg0, qg1, y_own = pack(queries, keys, values, grad_out)
    y_own = swap(y_own, 2)
    up4_0, down4_0 = shift(kv0, 4), shift(qg0, -4)
    up4_1, down4_1 = shift(kv1, 4), shift(qg1, -4)
    up8_0, down8_0 = shift(after(up4_0, down4_0), 4), shift(after(down4_0, up4_0), -4)
    y_far0 = swap(after(choose(bit1, up4_0, down4_0), up4_1, down4_1), 2)
    up8_1, down8_1 = shift(after(up4_1, y_own), 4), shift(after(down4_1, y_own), -4)
    y_far1 = swap(after(choose(bit1, up4_1, down4_1), y_far0, up8_0, down8_0), 2)
    c_own0 = swap(after(choose(bit0, qg0, kv0), up8_0, down8_0), 1)
    c_own1 = swap(after(choose(bit0, qg1, kv1), up8_1, down8_1), 1)

    def near(y_own, y_far):
        return choose(bit0, choose(bit1, y_own, y_far), choose(bit1, y_far, y_own))

    def pairs_back(pair8, pair4, pair2, pair1):
        return [shift(p, -d) for p, d in ((pair8, 8), (pair4, 4), (pair2, 2), (pair1, 1))]

    c_far0 = swap(near(y_own[:, :, :half], after(y_far0, c_own0)), 1)
    two, one = (y_own, y_far0), (c_own0, c_far0)
    self0, pair1, pair2, pair4, pair8, grad_query0 = scores_of(links, qg0, kv0, two, one, up4_0, up8_0, 0)
    came0 = pairs_back(pair8, pair4, pair2, pair1)
    query_part0 = project(grad_query0, w_query)
    c_far1 = swap(near(y_own[:, :, half:], after(y_far1, c_own1, pair8)), 1)
    near0 = two, one
    two, one = (y_own, y_far1), (c_own1, c_far1)
    self1, pair1, pair2, pair4, pair8, grad_query1 = scores_of(links, qg1, kv1, two, one, up4_1, up8_1, half)
    came1 = pairs_back(pair8, pair4, pair2, pair1)
    out = sums_of(after(qg0, pair8), *near0, down4_0, down8_0, [self0, *came0[::-1]], query_part0, (w_key, w_value), None, 0,
                  patches)
    query_part1 = project(grad_query1, w_query)
    out = sums_of(qg1, two, one, down4_1, down8_1, [self1, *came1[::-1]], query_part1, (w_key, w_value), out, half,
                  patches)
    return out[None]


def solution(mesh):
    by_frame = P(("dom", "frame"), None, None)
    return jax.shard_map(
        per_device,
        mesh=mesh,
        in_specs=(by_frame,) * 4 + (P(("dom", "frame"), None), P(), P(), P()),
        out_specs=by_frame,
        check_vma=False,
    )
```

time: 283 us -> 147 us (0.52); the launches traced: 278 us -> 147 us
  starting transfers between devices: 102 us -> 43.5 us
  local copies, waits for them, and re-layouts: 41.9 us -> 0.04 us
  Pallas kernels: 0 us -> 24.7 us
  waiting for transfers between devices: 99.2 us -> 74.7 us
  other arithmetic: 26.3 us -> 3.33 us
  matrix products: 4.93 us -> 0 us
    ppermute x12 -> x23, starting transfers between devices: 102 us -> 43.5 us  [the longest x16 36.3 us: shift(): lax.ppermute(block, 'frame', [(i, i + distance) for i in range(n) if 0 <=...]
    pallas_call x0 -> x7, Pallas kernels: none -> 24.7 us  [the longest x2 9.22 us: sums_of(): pl.pallas_call(functools.partial(sum_kernel, start), in_specs=specs, out_...]
    ppermute x12 -> x23, waiting for transfers between devices: 99.2 us -> 74.7 us  [the longest x16 74.7 us: shift(): lax.ppermute(block, 'frame', [(i, i + distance) for i in range(n) if 0 <=...]
    convert_element_type x6 -> x0, other arithmetic: 16.1 us -> none  [the longest x4 7.67 us: spread_heads(): return a.astype(jnp.float32).reshape(frames, patches, HEADS, head_size)]
    mul x18 -> x0, local copies, waits for them, and re-layouts: 13.9 us -> none  [the longest x8 6.35 us: per_device(): came_weights[0][..., None] * spread_heads(came_inputs[0])]
    unnamed x38 -> x16, local copies, waits for them, and re-layouts: 8.55 us -> 0.04 us
    reshape x4 -> x0, local copies, waits for them, and re-layouts: 7.8 us -> none  [per_device(): jnp.stack([grad_score[j + 1], probability[j + 1]])]
    slice x5 -> x0, local copies, waits for them, and re-layouts: 7.47 us -> none  [the longest x4 6.82 us: per_device(): came_weights[0][..., None] * spread_heads(came_inputs[0])]
  transfers between devices with their start and end apart: 12 -> 23, of which waited for: 3 -> 7; matrix products, arithmetic and copies ran while one was open for 19% -> 2% of each run, Pallas kernels for 0% -> 9%
where the time goes in v3:
time: 147 us
  waiting for transfers between devices  74.7 us (51%)
  starting transfers between devices  43.5 us (30%)
  Pallas kernels  24.7 us (17%)
  other arithmetic  3.33 us (2%)
    ppermute x16, waiting for transfers between devices, shift(): lax.ppermute(block, 'frame', [(i, i + distance) for i in range(n) if 0 <=...  74.7 us
    ppermute x16, starting transfers between devices, shift(): lax.ppermute(block, 'frame', [(i, i + distance) for i in range(n) if 0 <=...  36.3 us
    pallas_call x2, Pallas kernels, sums_of(): pl.pallas_call(functools.partial(sum_kernel, start), in_specs=specs, out_...  9.22 us
    ppermute x7, starting transfers between devices, swap(): return lax.ppermute(block, 'frame', [(i, i ^ bit) for i in range(n)])  7.28 us
    pallas_call x2, Pallas kernels, scores_of(): pl.pallas_call(functools.partial(score_kernel, start), in_specs=[SMEM] +...  7.03 us
    pallas_call x1, Pallas kernels, pack(): pl.pallas_call(kernel, grid=(steps,), in_specs=[pl.BlockSpec((1, tile, wi...  6.99 us
    select_n x6, other arithmetic, choose(): return jnp.where(bit == 1, if_set, if_clear)  3.33 us
  transfers between devices with their start and end apart: 23, of which 7 were waited for; matrix products, arithmetic and copies ran while one was open for 2% of the time, Pallas kernels for 9%

profile of v3, /device:TPU:27, one launch (start us, length us, event | category | flops | bytes accessed | tf_op | source)
XLA Modules:
  0.0 146.7 jit_solution(5330384101459424462)
XLA Ops:
  0.0 7.0 %pack.1 = (bf16[2,1024,256]{2,1,0:T(8,128)(2,1)}, bf16[2,1024,256]{2,1,0:T(8,128)(2,1)}, bf16[2,1024,256]{2,1,0:T(8,128)(2,1)}, bf16[2,1024,256]{2,1,0:T(8,128)(2,1)}, bf16[2,1024,512]{2,1,0:T(8,128)(2,1)}) custom-call(bf16[1,512,1024]{2,1,0:T(8,128)(2,1)} %q_ref.1, bf16[1,512,1024]{2,1,0:T(8,128)(2,1)} %k_ref.1, bf16[1,512,1024]{2,1,0:T(8,128)(2,1)} %v_ref.1, ...), custom_call_target="tpu_custom_call" | custom-call | tf_op jit(solution)/shard_map/pack/pallas_call | solution.py:81
  7.0 2.1 %collective-permute-start.4 = (bf16[2,1024,256]{2,1,0:T(8,128)(2,1)}, bf16[2,1024,256]{2,1,0:T(8,128)(2,1)S(1)}, u32[]{:S(2)}, u32[]{:S(2)}) collective-permute-start(bf16[2,1024,256]{2,1,0:T(8,128)(2,1)} %get-tuple-element.55.qg.own), channel_id=1, source_target_pairs={{4,0},{5,1},{6,2},{7,3},{8,4},{9,5},{10,6},{11,7},{12,8},{13,9},{1... | collective-permute-start | bytes 3145736 | tf_op jit(solution)/shard_map/ppermute | solution.py:21
  11.7 5.0 %collective-permute-start.2 = (bf16[2,1024,256]{2,1,0:T(8,128)(2,1)}, bf16[2,1024,256]{2,1,0:T(8,128)(2,1)}, u32[]{:S(2)}, u32[]{:S(2)}) collective-permute-start(bf16[2,1024,256]{2,1,0:T(8,128)(2,1)} %get-tuple-element.33.qg.own), channel_id=1, source_target_pairs={{4,0},{5,1},{6,2},{7,3},{8,4},{9,5},{10,6},{11,7},{12,8},{13,9},{1... | collective-permute-start | bytes 3145736 | tf_op jit(solution)/shard_map/ppermute | solution.py:21
  18.0 13.2 %collective-permute-done.4.far4 = bf16[2,1024,256]{2,1,0:T(8,128)(2,1)S(1)} collective-permute-done((bf16[2,1024,256]{2,1,0:T(8,128)(2,1)}, bf16[2,1024,256]{2,1,0:T(8,128)(2,1)S(1)}, u32[]{:S(2)}, u32[]{:S(2)}) %collective-permute-start.4) | collective-permute-done | bytes 1048608 | tf_op jit(solution)/shard_map/ppermute | solution.py:21
  31.2 3.9 %collective-permute-done.3.far4 = bf16[2,1024,256]{2,1,0:T(8,128)(2,1)} collective-permute-done((bf16[2,1024,256]{2,1,0:T(8,128)(2,1)}, bf16[2,1024,256]{2,1,0:T(8,128)(2,1)}, u32[]{:S(2)}, u32[]{:S(2)}) %collective-permute-start.3) | collective-permute-done | bytes 1048608 | tf_op jit(solution)/shard_map/ppermute | solution.py:21
  36.3 5.0 %collective-permute-start.7 = (bf16[2,1024,256]{2,1,0:T(8,128)(2,1)S(1)}, bf16[2,1024,256]{2,1,0:T(8,128)(2,1)}, u32[]{:S(2)}, u32[]{:S(2)}) collective-permute-start(bf16[2,1024,256]{2,1,0:T(8,128)(2,1)S(1)} %collective-permute-done.4.far4), channel_id=1, source_target_pairs={{4,0},{5,1},{6,2},{7,3},{8,4},{9,5},{10,6},{11,7},{12,8},{13,9},{1... | collective-permute-start | bytes 3145736 | tf_op jit(solution)/shard_map/ppermute | solution.py:21
  42.9 10.8 %collective-permute-done.2.far4 = bf16[2,1024,256]{2,1,0:T(8,128)(2,1)} collective-permute-done((bf16[2,1024,256]{2,1,0:T(8,128)(2,1)}, bf16[2,1024,256]{2,1,0:T(8,128)(2,1)}, u32[]{:S(2)}, u32[]{:S(2)}) %collective-permute-start.2) | collective-permute-done | bytes 1048608 | tf_op jit(solution)/shard_map/ppermute | solution.py:21
  53.7 3.9 %collective-permute-done.1.far4 = bf16[2,1024,256]{2,1,0:T(8,128)(2,1)} collective-permute-done((bf16[2,1024,256]{2,1,0:T(8,128)(2,1)}, bf16[2,1024,256]{2,1,0:T(8,128)(2,1)}, u32[]{:S(2)}, u32[]{:S(2)}) %collective-permute-start.1) | collective-permute-done | bytes 1048608 | tf_op jit(solution)/shard_map/ppermute | solution.py:21
  58.8 21.2 %collective-permute-done.6.far8 = bf16[2,1024,256]{2,1,0:T(8,128)(2,1)} collective-permute-done((bf16[2,1024,256]{2,1,0:T(8,128)(2,1)}, bf16[2,1024,256]{2,1,0:T(8,128)(2,1)}, u32[]{:S(2)}, u32[]{:S(2)}) %collective-permute-start.6) | collective-permute-done | bytes 1048608 | tf_op jit(solution)/shard_map/ppermute | solution.py:21
  80.0 1.9 %collective-permute-start.12 = (bf16[2,1024,256]{2,1,0:T(8,128)(2,1)S(1)}, bf16[2,1024,256]{2,1,0:T(8,128)(2,1)S(1)}, u32[]{:S(2)}, u32[]{:S(2)}) collective-permute-start(bf16[2,1024,256]{2,1,0:T(8,128)(2,1)S(1)} %broadcast_select_fusion), channel_id=1, source_target_pairs={{0,1},{1,0},{2,3},{3,2},{4,5},{5,4},{6,7},{7,6},{8,9},{9,8},{10,11... | collective-permute-start | bytes 3145736 | tf_op jit(solution)/shard_map/ppermute | solution.py:26
  81.9 2.1 %collective-permute-start.10 = (bf16[2,1024,256]{2,1,0:T(8,128)(2,1)}, bf16[2,1024,256]{2,1,0:T(8,128)(2,1)S(1)}, u32[]{:S(2)}, u32[]{:S(2)}) collective-permute-start(bf16[2,1024,256]{2,1,0:T(8,128)(2,1)} %collective-permute-done.2.far4), channel_id=1, source_target_pairs={{4,0},{5,1},{6,2},{7,3},{8,4},{9,5},{10,6},{11,7},{12,8},{13,9},{1... | collective-permute-start | bytes 3145736 | tf_op jit(solution)/shard_map/ppermute | solution.py:21
  88.8 18.0 %collective-permute-done.10.far8 = bf16[2,1024,256]{2,1,0:T(8,128)(2,1)S(1)} collective-permute-done((bf16[2,1024,256]{2,1,0:T(8,128)(2,1)}, bf16[2,1024,256]{2,1,0:T(8,128)(2,1)S(1)}, u32[]{:S(2)}, u32[]{:S(2)}) %collective-permute-start.10) | collective-permute-done | bytes 1048608 | tf_op jit(solution)/shard_map/ppermute | solution.py:21
  106.8 3.8 %collective-permute-done.9.far8 = bf16[2,1024,256]{2,1,0:T(8,128)(2,1)S(1)} collective-permute-done((bf16[2,1024,256]{2,1,0:T(8,128)(2,1)}, bf16[2,1024,256]{2,1,0:T(8,128)(2,1)S(1)}, u32[]{:S(2)}, u32[]{:S(2)}) %collective-permute-start.9) | collective-permute-done | bytes 1048608 | tf_op jit(solution)/shard_map/ppermute | solution.py:21
  111.6 3.6 %scores.2 = (f32[32,256]{1,0:T(8,128)S(1)}, f32[32,256]{1,0:T(8,128)S(1)}, f32[32,256]{1,0:T(8,128)S(1)}, f32[32,256]{1,0:T(8,128)S(1)}, f32[32,256]{1,0:T(8,128)S(1)}, /*index=5*/bf16[1024,256]{1,0:T(8,128)(2,1)S(1)}) custom-call(s32[1,4]{1,0:T(1,128)S(1)} %copy-done.7, bf16[2,1024,256]{2,1,0:T(8,128)(2,1)S(1)} %copy-done, ...), custom_call_target="tpu_custom_call" | custom-call | flops 26214400 | bytes 9437184 | tf_op jit(solution)/shard_map/scores/pallas_call | solution.py:164
  115.5 1.9 %collective-permute-start.22 = (f32[32,256]{1,0:T(8,128)S(1)}, f32[32,256]{1,0:T(8,128)S(1)}, u32[]{:S(2)}, u32[]{:S(2)}) collective-permute-start(f32[32,256]{1,0:T(8,128)S(1)} %get-tuple-element.47), channel_id=1, source_target_pairs={{8,0},{9,1},{10,2},{11,3},{12,4},{13,5},{14,6},{15,7},{24,16},{25,... | collective-permute-start | bytes 98312 | tf_op jit(solution)/shard_map/ppermute | solution.py:21
  117.3 2.5 %collective-permute-start.19 = (f32[32,256]{1,0:T(8,128)S(1)}, f32[32,256]{1,0:T(8,128)S(1)}, u32[]{:S(2)}, u32[]{:S(2)}) collective-permute-start(f32[32,256]{1,0:T(8,128)S(1)} %get-tuple-element.57), channel_id=1, source_target_pairs={{1,0},{2,1},{3,2},{4,3},{5,4},{6,5},{7,6},{8,7},{9,8},{10,9},{11,1... | collective-permute-start | bytes 98312 | tf_op jit(solution)/shard_map/ppermute | solution.py:21
  119.9 2.4 %collective-permute-start.20 = (f32[32,256]{1,0:T(8,128)S(1)}, f32[32,256]{1,0:T(8,128)S(1)}, u32[]{:S(2)}, u32[]{:S(2)}) collective-permute-start(f32[32,256]{1,0:T(8,128)S(1)} %get-tuple-element.58), channel_id=1, source_target_pairs={{2,0},{3,1},{4,2},{5,3},{6,4},{7,5},{8,6},{9,7},{10,8},{11,9},{12,... | collective-permute-start | bytes 98312 | tf_op jit(solution)/shard_map/ppermute | solution.py:21
  122.3 1.8 %collective-permute-start.21 = (f32[32,256]{1,0:T(8,128)S(1)}, f32[32,256]{1,0:T(8,128)S(1)}, u32[]{:S(2)}, u32[]{:S(2)}) collective-permute-start(f32[32,256]{1,0:T(8,128)S(1)} %get-tuple-element.59), channel_id=1, source_target_pairs={{4,0},{5,1},{6,2},{7,3},{8,4},{9,5},{10,6},{11,7},{12,8},{13,9},{1... | collective-permute-start | bytes 98312 | tf_op jit(solution)/shard_map/ppermute | solution.py:21
  124.8 3.5 %scores.3 = (f32[32,256]{1,0:T(8,128)S(1)}, f32[32,256]{1,0:T(8,128)S(1)}, f32[32,256]{1,0:T(8,128)S(1)}, f32[32,256]{1,0:T(8,128)S(1)}, f32[32,256]{1,0:T(8,128)S(1)}, /*index=5*/bf16[1024,256]{1,0:T(8,128)(2,1)S(1)}) custom-call(s32[1,4]{1,0:T(1,128)S(1)} %copy-done.7, bf16[2,1024,256]{2,1,0:T(8,128)(2,1)S(1)} %copy-done.1, ...), custom_call_target="tpu_custom_call" | custom-call | flops 26214400 | bytes 9437184 | tf_op jit(solution)/shard_map/scores/pallas_call | solution.py:164
  129.6 2.9 %collective-permute-start.15 = (f32[32,256]{1,0:T(8,128)S(1)}, f32[32,256]{1,0:T(8,128)S(1)}, u32[]{:S(2)}, u32[]{:S(2)}) collective-permute-start(f32[32,256]{1,0:T(8,128)S(1)} %get-tuple-element.50), channel_id=1, source_target_pairs={{1,0},{2,1},{3,2},{4,3},{5,4},{6,5},{7,6},{8,7},{9,8},{10,9},{11,1... | collective-permute-start | bytes 98312 | tf_op jit(solution)/shard_map/ppermute | solution.py:21
  132.5 2.5 %collective-permute-start.16 = (f32[32,256]{1,0:T(8,128)S(1)}, f32[32,256]{1,0:T(8,128)S(1)}, u32[]{:S(2)}, u32[]{:S(2)}) collective-permute-start(f32[32,256]{1,0:T(8,128)S(1)} %get-tuple-element.51), channel_id=1, source_target_pairs={{2,0},{3,1},{4,2},{5,3},{6,4},{7,5},{8,6},{9,7},{10,8},{11,9},{12,... | collective-permute-start | bytes 98312 | tf_op jit(solution)/shard_map/ppermute | solution.py:21
  135.1 1.6 %collective-permute-start.17 = (f32[32,256]{1,0:T(8,128)S(1)}, f32[32,256]{1,0:T(8,128)S(1)}, u32[]{:S(2)}, u32[]{:S(2)}) collective-permute-start(f32[32,256]{1,0:T(8,128)S(1)} %get-tuple-element.52), channel_id=1, source_target_pairs={{4,0},{5,1},{6,2},{7,3},{8,4},{9,5},{10,6},{11,7},{12,8},{13,9},{1... | collective-permute-start | bytes 98312 | tf_op jit(solution)/shard_map/ppermute | solution.py:21
  136.7 4.6 %sums.2.rest_0_ = bf16[512,1024]{1,0:T(8,128)(2,1)} custom-call(bf16[2,1024,256]{2,1,0:T(8,128)(2,1)S(1)} %copy-done, bf16[2,1024,512]{2,1,0:T(8,128)(2,1)S(1)} %collective-permute-done.y_own, bf16[2,1024,256]{2,1,0:T(8,128)(2,1)S(1)} %collective-permute-done.5.y_far, bf16[2,1024,256]{2,1,0:T(8,128)(2,1)S(1)} %collective-permute-done.12.c_own, ...), custom_call_target="tpu_custom_call" | custom-call | flops 2097152000 | bytes 9437184 | tf_op jit(solution)/shard_map/sums/pallas_call | solution.py:227
  142.1 4.6 %sums.3 = bf16[512,1024]{1,0:T(8,128)(2,1)} custom-call(bf16[2,1024,256]{2,1,0:T(8,128)(2,1)S(1)} %copy-done.1, bf16[2,1024,512]{2,1,0:T(8,128)(2,1)S(1)} %collective-permute-done.y_own, bf16[2,1024,256]{2,1,0:T(8,128)(2,1)S(1)} %collective-permute-done.8.y_far, ...), custom_call_target="tpu_custom_call", output_to_operand_aliasing={{}: (15, {})} | custom-call | flops 2097152000 | bytes 9437184 | tf_op jit(solution)/shard_map/sums/pallas_call | solution.py:227
  (51 shorter events, 16.7 us)
Async XLA Ops:
  7.0 24.2 %collective-permute-start.4 = (bf16[2,1024,256]{2,1,0:T(8,128)(2,1)}, bf16[2,1024,256]{2,1,0:T(8,128)(2,1)S(1)}, u32[]{:S(2)}, u32[]{:S(2)}) collective-permute-start(bf16[2,1024,256]{2,1,0:T(8,128)(2,1)} %get-tuple-element.55.qg.own), channel_id=1, source_target_pairs={{4,0},{5,1},{6,2},{7,3},{8,4},{9,5},{10,6},{11,7},{12,8},{13,9},{1... | collective-permute-start | bytes 3145736 | tf_op jit(solution)/shard_map/ppermute | solution.py:21
  9.1 25.9 %collective-permute-start.3 = (bf16[2,1024,256]{2,1,0:T(8,128)(2,1)}, bf16[2,1024,256]{2,1,0:T(8,128)(2,1)}, u32[]{:S(2)}, u32[]{:S(2)}) collective-permute-start(bf16[2,1024,256]{2,1,0:T(8,128)(2,1)} %get-tuple-element.36.own), channel_id=1, source_target_pairs={{0,4},{1,5},{2,6},{3,7},{4,8},{5,9},{6,10},{7,11},{8,12},{9,13},{1... | collective-permute-start | bytes 3145736 | tf_op jit(solution)/shard_map/ppermute | solution.py:21
  10.4 71.4 %collective-permute-start = (bf16[2,1024,512]{2,1,0:T(8,128)(2,1)}, bf16[2,1024,512]{2,1,0:T(8,128)(2,1)S(1)}, u32[]{:S(2)}, u32[]{:S(2)}) collective-permute-start(bf16[2,1024,512]{2,1,0:T(8,128)(2,1)} %get-tuple-element.34), channel_id=1, source_target_pairs={{0,2},{1,3},{2,0},{3,1},{4,6},{5,7},{6,4},{7,5},{8,10},{9,11},{10,... | collective-permute-start | bytes 6291464 | tf_op jit(solution)/shard_map/ppermute | solution.py:26
  11.7 41.9 %collective-permute-start.2 = (bf16[2,1024,256]{2,1,0:T(8,128)(2,1)}, bf16[2,1024,256]{2,1,0:T(8,128)(2,1)}, u32[]{:S(2)}, u32[]{:S(2)}) collective-permute-start(bf16[2,1024,256]{2,1,0:T(8,128)(2,1)} %get-tuple-element.33.qg.own), channel_id=1, source_target_pairs={{4,0},{5,1},{6,2},{7,3},{8,4},{9,5},{10,6},{11,7},{12,8},{13,9},{1... | collective-permute-start | bytes 3145736 | tf_op jit(solution)/shard_map/ppermute | solution.py:21
  16.7 40.8 %collective-permute-start.1 = (bf16[2,1024,256]{2,1,0:T(8,128)(2,1)}, bf16[2,1024,256]{2,1,0:T(8,128)(2,1)}, u32[]{:S(2)}, u32[]{:S(2)}) collective-permute-start(bf16[2,1024,256]{2,1,0:T(8,128)(2,1)} %get-tuple-element.35.own), channel_id=1, source_target_pairs={{0,4},{1,5},{2,6},{3,7},{4,8},{5,9},{6,10},{7,11},{8,12},{9,13},{1... | collective-permute-start | bytes 3145736 | tf_op jit(solution)/shard_map/ppermute | solution.py:21
  35.0 44.9 %collective-permute-start.6 = (bf16[2,1024,256]{2,1,0:T(8,128)(2,1)}, bf16[2,1024,256]{2,1,0:T(8,128)(2,1)}, u32[]{:S(2)}, u32[]{:S(2)}) collective-permute-start(bf16[2,1024,256]{2,1,0:T(8,128)(2,1)} %collective-permute-done.3.far4), channel_id=1, source_target_pairs={{0,4},{1,5},{2,6},{3,7},{4,8},{5,9},{6,10},{7,11},{8,12},{9,13},{1... | collective-permute-start | bytes 3145736 | tf_op jit(solution)/shard_map/ppermute | solution.py:21
  36.3 43.7 %collective-permute-start.7 = (bf16[2,1024,256]{2,1,0:T(8,128)(2,1)S(1)}, bf16[2,1024,256]{2,1,0:T(8,128)(2,1)}, u32[]{:S(2)}, u32[]{:S(2)}) collective-permute-start(bf16[2,1024,256]{2,1,0:T(8,128)(2,1)S(1)} %collective-permute-done.4.far4), channel_id=1, source_target_pairs={{4,0},{5,1},{6,2},{7,3},{8,4},{9,5},{10,6},{11,7},{12,8},{13,9},{1... | collective-permute-start | bytes 3145736 | tf_op jit(solution)/shard_map/ppermute | solution.py:21
  42.7 42.5 %copy-start.1 = (bf16[2,1024,256]{2,1,0:T(8,128)(2,1)S(1)}, bf16[2,1024,256]{2,1,0:T(8,128)(2,1)}, u32[]{:S(2)}) copy-start(bf16[2,1024,256]{2,1,0:T(8,128)(2,1)} %get-tuple-element.33.qg.own) | copy-start | bytes 3145732
  57.5 27.9 %collective-permute-start.5 = (bf16[2,1024,256]{2,1,0:T(8,128)(2,1)S(1)}, bf16[2,1024,256]{2,1,0:T(8,128)(2,1)S(1)}, u32[]{:S(2)}, u32[]{:S(2)}) collective-permute-start(bf16[2,1024,256]{2,1,0:T(8,128)(2,1)S(1)} %broadcast_select_fusion.2), channel_id=1, source_target_pairs={{0,2},{1,3},{2,0},{3,1},{4,6},{5,7},{6,4},{7,5},{8,10},{9,11},{10,... | collective-permute-start | bytes 3145736 | tf_op jit(solution)/shard_map/ppermute | solution.py:26
  80.0 5.4 %collective-permute-start.12 = (bf16[2,1024,256]{2,1,0:T(8,128)(2,1)S(1)}, bf16[2,1024,256]{2,1,0:T(8,128)(2,1)S(1)}, u32[]{:S(2)}, u32[]{:S(2)}) collective-permute-start(bf16[2,1024,256]{2,1,0:T(8,128)(2,1)S(1)} %broadcast_select_fusion), channel_id=1, source_target_pairs={{0,1},{1,0},{2,3},{3,2},{4,5},{5,4},{6,7},{7,6},{8,9},{9,8},{10,11... | collective-permute-start | bytes 3145736 | tf_op jit(solution)/shard_map/ppermute | solution.py:26
  81.9 24.9 %collective-permute-start.10 = (bf16[2,1024,256]{2,1,0:T(8,128)(2,1)}, bf16[2,1024,256]{2,1,0:T(8,128)(2,1)S(1)}, u32[]{:S(2)}, u32[]{:S(2)}) collective-permute-start(bf16[2,1024,256]{2,1,0:T(8,128)(2,1)} %collective-permute-done.2.far4), channel_id=1, source_target_pairs={{4,0},{5,1},{6,2},{7,3},{8,4},{9,5},{10,6},{11,7},{12,8},{13,9},{1... | collective-permute-start | bytes 3145736 | tf_op jit(solution)/shard_map/ppermute | solution.py:21
  83.9 26.6 %collective-permute-start.9 = (bf16[2,1024,256]{2,1,0:T(8,128)(2,1)}, bf16[2,1024,256]{2,1,0:T(8,128)(2,1)S(1)}, u32[]{:S(2)}, u32[]{:S(2)}) collective-permute-start(bf16[2,1024,256]{2,1,0:T(8,128)(2,1)} %collective-permute-done.1.far4), channel_id=1, source_target_pairs={{0,4},{1,5},{2,6},{3,7},{4,8},{5,9},{6,10},{7,11},{8,12},{9,13},{1... | collective-permute-start | bytes 3145736 | tf_op jit(solution)/shard_map/ppermute | solution.py:21
  85.6 26.1 %collective-permute-start.13 = (bf16[2,1024,256]{2,1,0:T(8,128)(2,1)S(1)}, bf16[2,1024,256]{2,1,0:T(8,128)(2,1)S(1)}, u32[]{:S(2)}, u32[]{:S(2)}) collective-permute-start(bf16[2,1024,256]{2,1,0:T(8,128)(2,1)S(1)} %select_select_fusion.1), channel_id=1, source_target_pairs={{0,1},{1,0},{2,3},{3,2},{4,5},{5,4},{6,7},{7,6},{8,9},{9,8},{10,11... | collective-permute-start | bytes 3145736 | tf_op jit(solution)/shard_map/ppermute | solution.py:26
  87.5 27.8 %collective-permute-start.8 = (bf16[2,1024,256]{2,1,0:T(8,128)(2,1)S(1)}, bf16[2,1024,256]{2,1,0:T(8,128)(2,1)S(1)}, u32[]{:S(2)}, u32[]{:S(2)}) collective-permute-start(bf16[2,1024,256]{2,1,0:T(8,128)(2,1)S(1)} %broadcast_select_fusion.3), channel_id=1, source_target_pairs={{0,2},{1,3},{2,0},{3,1},{4,6},{5,7},{6,4},{7,5},{8,10},{9,11},{10,... | collective-permute-start | bytes 3145736 | tf_op jit(solution)/shard_map/ppermute | solution.py:26
  110.5 4.7 %collective-permute-start.11 = (bf16[2,1024,256]{2,1,0:T(8,128)(2,1)S(1)}, bf16[2,1024,256]{2,1,0:T(8,128)(2,1)S(1)}, u32[]{:S(2)}, u32[]{:S(2)}) collective-permute-start(bf16[2,1024,256]{2,1,0:T(8,128)(2,1)S(1)} %broadcast_select_fusion.1), channel_id=1, source_target_pairs={{0,1},{1,0},{2,3},{3,2},{4,5},{5,4},{6,7},{7,6},{8,9},{9,8},{10,11... | collective-permute-start | bytes 3145736 | tf_op jit(solution)/shard_map/ppermute | solution.py:26
  115.4 9.4 %collective-permute-start.14 = (bf16[2,1024,256]{2,1,0:T(8,128)(2,1)S(1)}, bf16[2,1024,256]{2,1,0:T(8,128)(2,1)S(1)}, u32[]{:S(2)}, u32[]{:S(2)}) collective-permute-start(bf16[2,1024,256]{2,1,0:T(8,128)(2,1)S(1)} %select_select_fusion), channel_id=1, source_target_pairs={{0,1},{1,0},{2,3},{3,2},{4,5},{5,4},{6,7},{7,6},{8,9},{9,8},{10,11... | collective-permute-start | bytes 3145736 | tf_op jit(solution)/shard_map/ppermute | solution.py:26
  115.5 21.2 %collective-permute-start.22 = (f32[32,256]{1,0:T(8,128)S(1)}, f32[32,256]{1,0:T(8,128)S(1)}, u32[]{:S(2)}, u32[]{:S(2)}) collective-permute-start(f32[32,256]{1,0:T(8,128)S(1)} %get-tuple-element.47), channel_id=1, source_target_pairs={{8,0},{9,1},{10,2},{11,3},{12,4},{13,5},{14,6},{15,7},{24,16},{25,... | collective-permute-start | bytes 98312 | tf_op jit(solution)/shard_map/ppermute | solution.py:21
  117.3 12.2 %collective-permute-start.19 = (f32[32,256]{1,0:T(8,128)S(1)}, f32[32,256]{1,0:T(8,128)S(1)}, u32[]{:S(2)}, u32[]{:S(2)}) collective-permute-start(f32[32,256]{1,0:T(8,128)S(1)} %get-tuple-element.57), channel_id=1, source_target_pairs={{1,0},{2,1},{3,2},{4,3},{5,4},{6,5},{7,6},{8,7},{9,8},{10,9},{11,1... | collective-permute-start | bytes 98312 | tf_op jit(solution)/shard_map/ppermute | solution.py:21
  119.9 12.6 %collective-permute-start.20 = (f32[32,256]{1,0:T(8,128)S(1)}, f32[32,256]{1,0:T(8,128)S(1)}, u32[]{:S(2)}, u32[]{:S(2)}) collective-permute-start(f32[32,256]{1,0:T(8,128)S(1)} %get-tuple-element.58), channel_id=1, source_target_pairs={{2,0},{3,1},{4,2},{5,3},{6,4},{7,5},{8,6},{9,7},{10,8},{11,9},{12,... | collective-permute-start | bytes 98312 | tf_op jit(solution)/shard_map/ppermute | solution.py:21
  122.3 12.8 %collective-permute-start.21 = (f32[32,256]{1,0:T(8,128)S(1)}, f32[32,256]{1,0:T(8,128)S(1)}, u32[]{:S(2)}, u32[]{:S(2)}) collective-permute-start(f32[32,256]{1,0:T(8,128)S(1)} %get-tuple-element.59), channel_id=1, source_target_pairs={{4,0},{5,1},{6,2},{7,3},{8,4},{9,5},{10,6},{11,7},{12,8},{13,9},{1... | collective-permute-start | bytes 98312 | tf_op jit(solution)/shard_map/ppermute | solution.py:21
  128.3 13.8 %collective-permute-start.18 = (f32[32,256]{1,0:T(8,128)S(1)}, f32[32,256]{1,0:T(8,128)S(1)}, u32[]{:S(2)}, u32[]{:S(2)}) collective-permute-start(f32[32,256]{1,0:T(8,128)S(1)} %get-tuple-element.53), channel_id=1, source_target_pairs={{8,0},{9,1},{10,2},{11,3},{12,4},{13,5},{14,6},{15,7},{24,16},{25,... | collective-permute-start | bytes 98312 | tf_op jit(solution)/shard_map/ppermute | solution.py:21
  129.6 12.5 %collective-permute-start.15 = (f32[32,256]{1,0:T(8,128)S(1)}, f32[32,256]{1,0:T(8,128)S(1)}, u32[]{:S(2)}, u32[]{:S(2)}) collective-permute-start(f32[32,256]{1,0:T(8,128)S(1)} %get-tuple-element.50), channel_id=1, source_target_pairs={{1,0},{2,1},{3,2},{4,3},{5,4},{6,5},{7,6},{8,7},{9,8},{10,9},{11,1... | collective-permute-start | bytes 98312 | tf_op jit(solution)/shard_map/ppermute | solution.py:21
  132.5 9.6 %collective-permute-start.16 = (f32[32,256]{1,0:T(8,128)S(1)}, f32[32,256]{1,0:T(8,128)S(1)}, u32[]{:S(2)}, u32[]{:S(2)}) collective-permute-start(f32[32,256]{1,0:T(8,128)S(1)} %get-tuple-element.51), channel_id=1, source_target_pairs={{2,0},{3,1},{4,2},{5,3},{6,4},{7,5},{8,6},{9,7},{10,8},{11,9},{12,... | collective-permute-start | bytes 98312 | tf_op jit(solution)/shard_map/ppermute | solution.py:21
  135.1 7.0 %collective-permute-start.17 = (f32[32,256]{1,0:T(8,128)S(1)}, f32[32,256]{1,0:T(8,128)S(1)}, u32[]{:S(2)}, u32[]{:S(2)}) collective-permute-start(f32[32,256]{1,0:T(8,128)S(1)} %get-tuple-element.52), channel_id=1, source_target_pairs={{4,0},{5,1},{6,2},{7,3},{8,4},{9,5},{10,6},{11,7},{12,8},{13,9},{1... | collective-permute-start | bytes 98312 | tf_op jit(solution)/shard_map/ppermute | solution.py:21
  (7 other events, 153.5 us)

commit v4 on v3

--- a/solution.py
+++ b/solution.py
@@ -11,9 +11,8 @@
 NDIL = 4
 LANES = 128
 SUBLANES = 8
-UNIT = 256
+HEAVY = 48
 VMEM_BYTES = 32 * 2**20
-PACK_VMEM_BYTES = 60 * 2**20
 
 
 def shift(block, distance):
@@ -39,54 +38,68 @@
 PIN = False
 
 
-def columns(width, tile, offset=0):
-    return pl.BlockSpec((2, width, tile), lambda i: (0, 0, i + offset))
-
-
 def after(block, *done):
     return lax.optimization_barrier((block, *done))[0]
 
 
 def pack(queries, keys, values, grad_out):
     _, patches, width = queries.shape
-    tile = LANES
-    steps = patches // tile
-    half = steps // 2
-
-    def kernel(q_ref, k_ref, v_ref, g_ref, kv0, kv1, qg0, qg1, y_out):
-        step = pl.program_id(0)
-        unit = jnp.where(lax.broadcasted_iota(jnp.int32, (UNIT, UNIT), 0) == lax.broadcasted_iota(
-            jnp.int32, (UNIT, UNIT), 1), 1.0, 0.0).astype(jnp.bfloat16)
-
-        def turned(ref):
-            blocks = [lax.dot_general(unit, ref[0, :, i:i + UNIT], (((1,), (1,)), ((), ())),
-                                      preferred_element_type=jnp.float32) for i in range(0, width, UNIT)]
-            return jnp.concatenate([b.astype(jnp.bfloat16) for b in blocks], axis=0)
-
-        kv = [turned(r) for r in (k_ref, v_ref)]
-        qg = [turned(r) for r in (q_ref, g_ref)]
-        for kv_out, qg_out, mine in ((kv0, qg0, step < half), (kv1, qg1, step >= half)):
-            @pl.when(mine)
-            def _(kv_out=kv_out, qg_out=qg_out):
-                for part in range(2):
-                    kv_out[part] = kv[part]
-                    qg_out[part] = qg[part]
-        for part in range(2):
-            y_out[part] = jnp.where(place_bit(1) == 0, kv[part], qg[part])
-
-    first = pl.BlockSpec((2, width, tile), lambda i: (0, 0, jnp.minimum(i, half - 1)))
-    second = pl.BlockSpec((2, width, tile), lambda i: (0, 0, jnp.maximum(i - half, 0)))
-    half_shape = jax.ShapeDtypeStruct((2, width, patches // 2), jnp.bfloat16)
+    half = patches // 2
+
+    def kernel(q_hbm, k_hbm, v_hbm, g_hbm, kv0, kv1, qg0, qg1, y_out, q_ref, k_ref, v_ref, g_ref, sems):
+        pieces = []
+        for i in range(2):
+            rows = pl.ds(i * half, half)
+            for part, up, down in ((0, (k_hbm, k_ref), (q_hbm, q_ref)), (1, (v_hbm, v_ref), (g_hbm, g_ref))):
+                for (hbm, ref), out, bit in ((up, (kv0, kv1)[i], 0), (down, (qg0, qg1)[i], 1)):
+                    copy = pltpu.make_async_copy(hbm.at[0, rows, :], ref.at[rows, :], sems.at[len(pieces)])
+                    pieces.append((copy, ref, i * half, out, part, bit))
+        for piece in pieces:
+            piece[0].start()
+        for copy, ref, start, out, part, bit in pieces:
+            copy.wait()
+            for p in range(0, half, LANES):
+                turned = ref[start + p:start + p + LANES, :].T
+                out[part, :, p:p + LANES] = turned
+
+                @pl.when(place_bit(1) == bit)
+                def _():
+                    y_out[part, :, start + p:start + p + LANES] = turned
+
+    half_shape = jax.ShapeDtypeStruct((2, width, half), jnp.bfloat16)
     whole_shape = jax.ShapeDtypeStruct((2, width, patches), jnp.bfloat16)
     return pl.pallas_call(
         kernel,
-        grid=(steps,),
-        in_specs=[pl.BlockSpec((1, tile, width), lambda i: (0, i, 0))] * 4,
-        out_specs=[first, second] * 2 + [columns(width, tile)],
+        in_specs=[pl.BlockSpec(memory_space=pl.ANY)] * 4,
+        out_specs=[VMEM] * 5,
         out_shape=[half_shape] * 4 + [whole_shape],
-        compiler_params=pltpu.CompilerParams(vmem_limit_bytes=PACK_VMEM_BYTES),
+        scratch_shapes=[pltpu.VMEM((patches, width), jnp.bfloat16)] * 4 + [pltpu.SemaphoreType.DMA((8,))],
+        compiler_params=params(),
         name="pack",
-    )(queries, keys, values, grad_out)
+    )(*(pltpu.with_memory_space_constraint(a, pltpu.HBM) for a in (queries, keys, values, grad_out)))
+
+
+def pick(test, if_true, if_false, start=0, weight=1):
+    def kernel(a_ref, b_ref, out):
+        chosen = test()
+
+        @pl.when(chosen)
+        def _():
+            out[...] = a_ref[:, :, start:start + out.shape[2]]
+
+        @pl.when(jnp.logical_not(chosen))
+        def _():
+            out[...] = b_ref[...]
+
+    return pl.pallas_call(
+        kernel,
+        in_specs=[VMEM] * 2,
+        out_specs=VMEM,
+        out_shape=jax.ShapeDtypeStruct(if_false.shape, if_false.dtype),
+        compiler_params=params(),
+        cost_estimate=pl.CostEstimate(flops=0, bytes_accessed=weight * if_false.size, transcendentals=0),
+        name="pick",
+    )(if_true, if_false)
 
 
 def in_vmem(arrays):
@@ -158,7 +171,7 @@
             grad_query[rows, here] = functools.reduce(jnp.add, terms).astype(jnp.bfloat16)
 
 
-def scores_of(links, qg, own, two, one, far4, far8, start):
+def scores_of(links, qg, own, two, one, far4, far8, start, weight):
     _, width, rows = own.shape
     pair_shape = jax.ShapeDtypeStruct((2 * HEADS, rows), jnp.float32)
     return pl.pallas_call(
@@ -168,7 +181,7 @@
         out_shape=[pair_shape] * 5 + [jax.ShapeDtypeStruct((width, rows), jnp.bfloat16)],
         scratch_shapes=[pltpu.VMEM((NDIL + 1, HEADS * SUBLANES, LANES), jnp.float32)] * 2,
         compiler_params=params(),
-        cost_estimate=pl.CostEstimate(flops=rows * width * 100, bytes_accessed=rows * width * 36, transcendentals=0),
+        cost_estimate=pl.CostEstimate(flops=0, bytes_accessed=weight * rows * width, transcendentals=0),
         name="scores",
     )(links, *in_vmem([qg, own, *two, *one, far4, far8]))
 
@@ -240,38 +253,37 @@
 
 def per_device(queries, keys, values, grad_out, links, w_query, w_key, w_value):
     patches = queries.shape[1]
-    bit0, bit1 = place_bit(0), place_bit(1)
     half = patches // 2
 
-    def choose(bit, if_set, if_clear):
-        return jnp.where(bit == 1, if_set, if_clear)
+    def upper(bit):
+        return lambda: place_bit(bit) == 1
+
+    def same_bits():
+        return place_bit(0) == place_bit(1)
 
     kv0, kv1, qg0, qg1, y_own = pack(queries, keys, values, grad_out)
     y_own = swap(y_own, 2)
     up4_0, down4_0 = shift(kv0, 4), shift(qg0, -4)
     up4_1, down4_1 = shift(kv1, 4), shift(qg1, -4)
     up8_0, down8_0 = shift(after(up4_0, down4_0), 4), shift(after(down4_0, up4_0), -4)
-    y_far0 = swap(after(choose(bit1, up4_0, down4_0), up4_1, down4_1), 2)
+    y_far0 = swap(pick(upper(1), up4_0, down4_0), 2)
     up8_1, down8_1 = shift(after(up4_1, y_own), 4), shift(after(down4_1, y_own), -4)
-    y_far1 = swap(after(choose(bit1, up4_1, down4_1), y_far0, up8_0, down8_0), 2)
-    c_own0 = swap(after(choose(bit0, qg0, kv0), up8_0, down8_0), 1)
-    c_own1 = swap(after(choose(bit0, qg1, kv1), up8_1, down8_1), 1)
-
-    def near(y_own, y_far):
-        return choose(bit0, choose(bit1, y_own, y_far), choose(bit1, y_far, y_own))
+    y_far1 = swap(after(pick(upper(1), up4_1, down4_1), up8_0, down8_0), 2)
+    c_own0 = swap(after(pick(upper(0), qg0, kv0), up8_0, down8_0), 1)
+    c_own1 = swap(after(pick(upper(0), qg1, kv1), up8_1, down8_1), 1)
 
     def pairs_back(pair8, pair4, pair2, pair1):
         return [shift(p, -d) for p, d in ((pair8, 8), (pair4, 4), (pair2, 2), (pair1, 1))]
 
-    c_far0 = swap(near(y_own[:, :, :half], after(y_far0, c_own0)), 1)
+    c_far0 = swap(pick(same_bits, y_own, y_far0), 1)
     two, one = (y_own, y_far0), (c_own0, c_far0)
-    self0, pair1, pair2, pair4, pair8, grad_query0 = scores_of(links, qg0, kv0, two, one, up4_0, up8_0, 0)
+    self0, pair1, pair2, pair4, pair8, grad_query0 = scores_of(links, qg0, kv0, two, one, up4_0, up8_0, 0, 140)
     came0 = pairs_back(pair8, pair4, pair2, pair1)
     query_part0 = project(grad_query0, w_query)
-    c_far1 = swap(near(y_own[:, :, half:], after(y_far1, c_own1, pair8)), 1)
+    c_far1 = swap(after(pick(same_bits, y_own, after(y_far1, c_own1), half, HEAVY), pair8), 1)
     near0 = two, one
     two, one = (y_own, y_far1), (c_own1, c_far1)
-    self1, pair1, pair2, pair4, pair8, grad_query1 = scores_of(links, qg1, kv1, two, one, up4_1, up8_1, half)
+    self1, pair1, pair2, pair4, pair8, grad_query1 = scores_of(links, qg1, kv1, two, one, up4_1, up8_1, half, 1)
     came1 = pairs_back(pair8, pair4, pair2, pair1)
     out = sums_of(after(qg0, pair8), *near0, down4_0, down8_0, [self0, *came0[::-1]], query_part0, (w_key, w_value), None, 0,
                   patches)

time: 147 us -> 135 us (0.918)
  Pallas kernels: 24.7 us -> 17.2 us
  other arithmetic: 3.33 us -> 0 us
    select_n x6 -> x0, other arithmetic: 3.33 us -> none  [choose(): return jnp.where(bit == 1, if_set, if_clear)]
    pallas_call x1 -> x7, Pallas kernels: 6.99 us -> 3.89 us  [the longest x1 3.4 us: pack(): pl.pallas_call(kernel, in_specs=[pl.BlockSpec(memory_space=pl.ANY)] * 4,...]
    pallas_call x2, Pallas kernels: 9.22 us -> 6.72 us  [sums_of(): pl.pallas_call(functools.partial(sum_kernel, start), in_specs=specs, out_...]
    ppermute x16, waiting for transfers between devices: 74.7 us -> 72.2 us  [shift(): lax.ppermute(block, 'frame', [(i, i + distance) for i in range(n) if 0 <=...]
    ppermute x16, starting transfers between devices: 36.3 us -> 33.9 us  [shift(): lax.ppermute(block, 'frame', [(i, i + distance) for i in range(n) if 0 <=...]
    ppermute x7, starting transfers between devices: 7.28 us -> 9.33 us  [swap(): return lax.ppermute(block, 'frame', [(i, i ^ bit) for i in range(n)])]
    pallas_call x2, Pallas kernels: 7.03 us -> 5.23 us  [scores_of(): pl.pallas_call(functools.partial(score_kernel, start), in_specs=[SMEM] +...]
  transfers between devices with their start and end apart: 23 -> 23, of which waited for: 7 -> 8; matrix products, arithmetic and copies ran while one was open for 2% -> 0% of each run, Pallas kernels for 9% -> 8%
where the time goes in v4:
time: 135 us; the launch traced here: 134 us
  waiting for transfers between devices  73.4 us (54%)
  starting transfers between devices  43.3 us (32%)
  Pallas kernels  17.2 us (13%)
    ppermute x16, waiting for transfers between devices, shift(): lax.ppermute(block, 'frame', [(i, i + distance) for i in range(n) if 0 <=...  72.2 us
    ppermute x16, starting transfers between devices, shift(): lax.ppermute(block, 'frame', [(i, i + distance) for i in range(n) if 0 <=...  33.9 us
    ppermute x7, starting transfers between devices, swap(): return lax.ppermute(block, 'frame', [(i, i ^ bit) for i in range(n)])  9.33 us
    pallas_call x2, Pallas kernels, sums_of(): pl.pallas_call(functools.partial(sum_kernel, start), in_specs=specs, out_...  6.72 us
    pallas_call x2, Pallas kernels, scores_of(): pl.pallas_call(functools.partial(score_kernel, start), in_specs=[SMEM] +...  5.23 us
    pallas_call x1, Pallas kernels, pack(): pl.pallas_call(kernel, in_specs=[pl.BlockSpec(memory_space=pl.ANY)] * 4,...  3.4 us
  transfers between devices with their start and end apart: 23, of which 8 were waited for; matrix products, arithmetic and copies ran while one was open for 0% of the time, Pallas kernels for 8%

profile of v4, /device:TPU:27, one launch (start us, length us, event | category | flops | bytes accessed | tf_op | source)
XLA Modules:
  0.0 134.5 jit_solution(5236257654331378213)
XLA Ops:
  0.0 3.4 %pack.1 = (bf16[2,1024,256]{2,1,0:T(8,128)(2,1)S(1)}, bf16[2,1024,256]{2,1,0:T(8,128)(2,1)S(1)}, bf16[2,1024,256]{2,1,0:T(8,128)(2,1)S(1)}, bf16[2,1024,256]{2,1,0:T(8,128)(2,1)S(1)}, bf16[2,1024,512]{2,1,0:T(8,128)(2,1)S(1)}) custom-call(bf16[1,512,1024]{2,1,0:T(8,128)(2,1)} %q_hbm.1, bf16[1,512,1024]{2,1,0:T(8,128)(2,1)} %k_hbm.1, ...), custom_call_target="tpu_custom_call" | custom-call | tf_op jit(solution)/shard_map/pack/pallas_call | solution.py:71
  4.7 2.1 %collective-permute-start.4 = (bf16[2,1024,256]{2,1,0:T(8,128)(2,1)S(1)}, bf16[2,1024,256]{2,1,0:T(8,128)(2,1)S(1)}, u32[]{:S(2)}, u32[]{:S(2)}) collective-permute-start(bf16[2,1024,256]{2,1,0:T(8,128)(2,1)S(1)} %get-tuple-element.53.a_ref.qg.own), channel_id=1, source_target_pairs={{4,0},{5,1},{6,2},{7,3},{8,4},{9,5},{10,6},{11,7},{12,8},{13,9},{1... | collective-permute-start | bytes 3145736 | tf_op jit(solution)/shard_map/ppermute | solution.py:20
  8.2 4.1 %collective-permute-start.2 = (bf16[2,1024,256]{2,1,0:T(8,128)(2,1)S(1)}, bf16[2,1024,256]{2,1,0:T(8,128)(2,1)S(1)}, u32[]{:S(2)}, u32[]{:S(2)}) collective-permute-start(bf16[2,1024,256]{2,1,0:T(8,128)(2,1)S(1)} %get-tuple-element.32.a_ref.qg.own), channel_id=1, source_target_pairs={{4,0},{5,1},{6,2},{7,3},{8,4},{9,5},{10,6},{11,7},{12,8},{13,9},{1... | collective-permute-start | bytes 3145736 | tf_op jit(solution)/shard_map/ppermute | solution.py:20
  13.5 14.8 %collective-permute-done.4.b_ref.far4 = bf16[2,1024,256]{2,1,0:T(8,128)(2,1)S(1)} collective-permute-done((bf16[2,1024,256]{2,1,0:T(8,128)(2,1)S(1)}, bf16[2,1024,256]{2,1,0:T(8,128)(2,1)S(1)}, u32[]{:S(2)}, u32[]{:S(2)}) %collective-permute-start.4) | collective-permute-done | bytes 1048608 | tf_op jit(solution)/shard_map/ppermute | solution.py:20
  28.3 3.9 %collective-permute-done.3.a_ref.far4 = bf16[2,1024,256]{2,1,0:T(8,128)(2,1)S(1)} collective-permute-done((bf16[2,1024,256]{2,1,0:T(8,128)(2,1)S(1)}, bf16[2,1024,256]{2,1,0:T(8,128)(2,1)S(1)}, u32[]{:S(2)}, u32[]{:S(2)}) %collective-permute-start.3) | collective-permute-done | bytes 1048608 | tf_op jit(solution)/shard_map/ppermute | solution.py:20
  32.2 2.1 %collective-permute-start.6 = (bf16[2,1024,256]{2,1,0:T(8,128)(2,1)S(1)}, bf16[2,1024,256]{2,1,0:T(8,128)(2,1)S(1)}, u32[]{:S(2)}, u32[]{:S(2)}) collective-permute-start(bf16[2,1024,256]{2,1,0:T(8,128)(2,1)S(1)} %collective-permute-done.4.b_ref.far4), channel_id=1, source_target_pairs={{4,0},{5,1},{6,2},{7,3},{8,4},{9,5},{10,6},{11,7},{12,8},{13,9},{1... | collective-permute-start | bytes 3145736 | tf_op jit(solution)/shard_map/ppermute | solution.py:20
  35.6 15.1 %collective-permute-done.2.b_ref.far4 = bf16[2,1024,256]{2,1,0:T(8,128)(2,1)S(1)} collective-permute-done((bf16[2,1024,256]{2,1,0:T(8,128)(2,1)S(1)}, bf16[2,1024,256]{2,1,0:T(8,128)(2,1)S(1)}, u32[]{:S(2)}, u32[]{:S(2)}) %collective-permute-start.2) | collective-permute-done | bytes 1048608 | tf_op jit(solution)/shard_map/ppermute | solution.py:20
  51.0 4.2 %collective-permute-start.9 = (bf16[2,1024,256]{2,1,0:T(8,128)(2,1)S(1)}, bf16[2,1024,256]{2,1,0:T(8,128)(2,1)S(1)}, u32[]{:S(2)}, u32[]{:S(2)}) collective-permute-start(bf16[2,1024,256]{2,1,0:T(8,128)(2,1)S(1)} %collective-permute-done.2.b_ref.far4), channel_id=1, source_target_pairs={{4,0},{5,1},{6,2},{7,3},{8,4},{9,5},{10,6},{11,7},{12,8},{13,9},{1... | collective-permute-start | bytes 3145736 | tf_op jit(solution)/shard_map/ppermute | solution.py:20
  56.8 16.5 %collective-permute-done.6.far8 = bf16[2,1024,256]{2,1,0:T(8,128)(2,1)S(1)} collective-permute-done((bf16[2,1024,256]{2,1,0:T(8,128)(2,1)S(1)}, bf16[2,1024,256]{2,1,0:T(8,128)(2,1)S(1)}, u32[]{:S(2)}, u32[]{:S(2)}) %collective-permute-start.6) | collective-permute-done | bytes 1048608 | tf_op jit(solution)/shard_map/ppermute | solution.py:20
  73.2 3.9 %collective-permute-done.5.far8 = bf16[2,1024,256]{2,1,0:T(8,128)(2,1)S(1)} collective-permute-done((bf16[2,1024,256]{2,1,0:T(8,128)(2,1)S(1)}, bf16[2,1024,256]{2,1,0:T(8,128)(2,1)S(1)}, u32[]{:S(2)}, u32[]{:S(2)}) %collective-permute-start.5) | collective-permute-done | bytes 1048608 | tf_op jit(solution)/shard_map/ppermute | solution.py:20
  77.1 3.9 %collective-permute-start.12 = (bf16[2,1024,256]{2,1,0:T(8,128)(2,1)S(1)}, bf16[2,1024,256]{2,1,0:T(8,128)(2,1)S(1)}, u32[]{:S(2)}, u32[]{:S(2)}) collective-permute-start(bf16[2,1024,256]{2,1,0:T(8,128)(2,1)S(1)} %pick.10), channel_id=1, source_target_pairs={{0,1},{1,0},{2,3},{3,2},{4,5},{5,4},{6,7},{7,6},{8,9},{9,8},{10,11... | collective-permute-start | bytes 3145736 | tf_op jit(solution)/shard_map/ppermute | solution.py:25
  81.5 14.2 %collective-permute-done.9.far8 = bf16[2,1024,256]{2,1,0:T(8,128)(2,1)S(1)} collective-permute-done((bf16[2,1024,256]{2,1,0:T(8,128)(2,1)S(1)}, bf16[2,1024,256]{2,1,0:T(8,128)(2,1)S(1)}, u32[]{:S(2)}, u32[]{:S(2)}) %collective-permute-start.9) | collective-permute-done | bytes 1048608 | tf_op jit(solution)/shard_map/ppermute | solution.py:20
  95.7 3.9 %collective-permute-done.8.far8 = bf16[2,1024,256]{2,1,0:T(8,128)(2,1)S(1)} collective-permute-done((bf16[2,1024,256]{2,1,0:T(8,128)(2,1)S(1)}, bf16[2,1024,256]{2,1,0:T(8,128)(2,1)S(1)}, u32[]{:S(2)}, u32[]{:S(2)}) %collective-permute-start.8) | collective-permute-done | bytes 1048608 | tf_op jit(solution)/shard_map/ppermute | solution.py:20
  99.6 2.2 %collective-permute-start.10 = (bf16[2,1024,256]{2,1,0:T(8,128)(2,1)S(1)}, bf16[2,1024,256]{2,1,0:T(8,128)(2,1)S(1)}, u32[]{:S(2)}, u32[]{:S(2)}) collective-permute-start(bf16[2,1024,256]{2,1,0:T(8,128)(2,1)S(1)} %pick.7), channel_id=1, source_target_pairs={{0,1},{1,0},{2,3},{3,2},{4,5},{5,4},{6,7},{7,6},{8,9},{9,8},{10,11... | collective-permute-start | bytes 3145736 | tf_op jit(solution)/shard_map/ppermute | solution.py:25
  101.7 2.6 %scores.2 = (f32[32,256]{1,0:T(8,128)S(1)}, f32[32,256]{1,0:T(8,128)S(1)}, f32[32,256]{1,0:T(8,128)S(1)}, f32[32,256]{1,0:T(8,128)S(1)}, f32[32,256]{1,0:T(8,128)S(1)}, /*index=5*/bf16[1024,256]{1,0:T(8,128)(2,1)S(1)}) custom-call(s32[1,4]{1,0:T(1,128)S(1)} %copy-done.3, bf16[2,1024,256]{2,1,0:T(8,128)(2,1)S(1)} %get-tuple-element.53.a_ref.qg.own, ...), custom_call_target="tpu_custom_call" | custom-call | bytes 36700160 | tf_op jit(solution)/shard_map/scores/pallas_call | solution.py:177
  107.0 1.9 %collective-permute-start.22 = (f32[32,256]{1,0:T(8,128)S(1)}, f32[32,256]{1,0:T(8,128)S(1)}, u32[]{:S(2)}, u32[]{:S(2)}) collective-permute-start(f32[32,256]{1,0:T(8,128)S(1)} %get-tuple-element.45), channel_id=1, source_target_pairs={{8,0},{9,1},{10,2},{11,3},{12,4},{13,5},{14,6},{15,7},{24,16},{25,... | collective-permute-start | bytes 98312 | tf_op jit(solution)/shard_map/ppermute | solution.py:20
  108.9 2.2 %collective-permute-start.19 = (f32[32,256]{1,0:T(8,128)S(1)}, f32[32,256]{1,0:T(8,128)S(1)}, u32[]{:S(2)}, u32[]{:S(2)}) collective-permute-start(f32[32,256]{1,0:T(8,128)S(1)} %get-tuple-element.55), channel_id=1, source_target_pairs={{1,0},{2,1},{3,2},{4,3},{5,4},{6,5},{7,6},{8,7},{9,8},{10,9},{11,1... | collective-permute-start | bytes 98312 | tf_op jit(solution)/shard_map/ppermute | solution.py:20
  111.1 1.9 %collective-permute-start.20 = (f32[32,256]{1,0:T(8,128)S(1)}, f32[32,256]{1,0:T(8,128)S(1)}, u32[]{:S(2)}, u32[]{:S(2)}) collective-permute-start(f32[32,256]{1,0:T(8,128)S(1)} %get-tuple-element.56), channel_id=1, source_target_pairs={{2,0},{3,1},{4,2},{5,3},{6,4},{7,5},{8,6},{9,7},{10,8},{11,9},{12,... | collective-permute-start | bytes 98312 | tf_op jit(solution)/shard_map/ppermute | solution.py:20
  115.1 2.6 %scores.3 = (f32[32,256]{1,0:T(8,128)S(1)}, f32[32,256]{1,0:T(8,128)S(1)}, f32[32,256]{1,0:T(8,128)S(1)}, f32[32,256]{1,0:T(8,128)S(1)}, f32[32,256]{1,0:T(8,128)S(1)}, /*index=5*/bf16[1024,256]{1,0:T(8,128)(2,1)S(1)}) custom-call(s32[1,4]{1,0:T(1,128)S(1)} %copy-done.3, bf16[2,1024,256]{2,1,0:T(8,128)(2,1)S(1)} %get-tuple-element.32.a_ref.qg.own, ...), custom_call_target="tpu_custom_call" | custom-call | bytes 262144 | tf_op jit(solution)/shard_map/scores/pallas_call | solution.py:177
  119.3 3.7 %collective-permute-start.15 = (f32[32,256]{1,0:T(8,128)S(1)}, f32[32,256]{1,0:T(8,128)S(1)}, u32[]{:S(2)}, u32[]{:S(2)}) collective-permute-start(f32[32,256]{1,0:T(8,128)S(1)} %get-tuple-element.48), channel_id=1, source_target_pairs={{1,0},{2,1},{3,2},{4,3},{5,4},{6,5},{7,6},{8,7},{9,8},{10,9},{11,1... | collective-permute-start | bytes 98312 | tf_op jit(solution)/shard_map/ppermute | solution.py:20
  123.0 1.9 %collective-permute-start.16 = (f32[32,256]{1,0:T(8,128)S(1)}, f32[32,256]{1,0:T(8,128)S(1)}, u32[]{:S(2)}, u32[]{:S(2)}) collective-permute-start(f32[32,256]{1,0:T(8,128)S(1)} %get-tuple-element.49), channel_id=1, source_target_pairs={{2,0},{3,1},{4,2},{5,3},{6,4},{7,5},{8,6},{9,7},{10,8},{11,9},{12,... | collective-permute-start | bytes 98312 | tf_op jit(solution)/shard_map/ppermute | solution.py:20
  125.0 1.8 %collective-permute-start.17 = (f32[32,256]{1,0:T(8,128)S(1)}, f32[32,256]{1,0:T(8,128)S(1)}, u32[]{:S(2)}, u32[]{:S(2)}) collective-permute-start(f32[32,256]{1,0:T(8,128)S(1)} %get-tuple-element.50), channel_id=1, source_target_pairs={{4,0},{5,1},{6,2},{7,3},{8,4},{9,5},{10,6},{11,7},{12,8},{13,9},{1... | collective-permute-start | bytes 98312 | tf_op jit(solution)/shard_map/ppermute | solution.py:20
  126.8 3.3 %sums.2.rest_0_ = bf16[512,1024]{1,0:T(8,128)(2,1)} custom-call(bf16[2,1024,256]{2,1,0:T(8,128)(2,1)S(1)} %get-tuple-element.53.a_ref.qg.own, bf16[2,1024,512]{2,1,0:T(8,128)(2,1)S(1)} %collective-permute-done.a_ref.y_own, bf16[2,1024,256]{2,1,0:T(8,128)(2,1)S(1)} %collective-permute-done.11.b_ref.y_far, ...), custom_call_target="tpu_custom_call" | custom-call | flops 2097152000 | bytes 9437184 | tf_op jit(solution)/shard_map/sums/pallas_call | solution.py:240
  130.9 3.4 %sums.3 = bf16[512,1024]{1,0:T(8,128)(2,1)} custom-call(bf16[2,1024,256]{2,1,0:T(8,128)(2,1)S(1)} %get-tuple-element.32.a_ref.qg.own, bf16[2,1024,512]{2,1,0:T(8,128)(2,1)S(1)} %collective-permute-done.a_ref.y_own, bf16[2,1024,256]{2,1,0:T(8,128)(2,1)S(1)} %collective-permute-done.7.b_ref.y_far, ...), custom_call_target="tpu_custom_call", output_to_operand_aliasing={{}: (15, {})} | custom-call | flops 2097152000 | bytes 9437184 | tf_op jit(solution)/shard_map/sums/pallas_call | solution.py:240
  (43 shorter events, 14.5 us)
Async XLA Ops:
  3.4 47.6 %collective-permute-start = (bf16[2,1024,512]{2,1,0:T(8,128)(2,1)S(1)}, bf16[2,1024,512]{2,1,0:T(8,128)(2,1)S(1)}, u32[]{:S(2)}, u32[]{:S(2)}) collective-permute-start(bf16[2,1024,512]{2,1,0:T(8,128)(2,1)S(1)} %get-tuple-element.33), channel_id=1, source_target_pairs={{0,2},{1,3},{2,0},{3,1},{4,6},{5,7},{6,4},{7,5},{8,10},{9,11},{10,... | collective-permute-start | bytes 6291464 | tf_op jit(solution)/shard_map/ppermute | solution.py:25
  4.7 23.6 %collective-permute-start.4 = (bf16[2,1024,256]{2,1,0:T(8,128)(2,1)S(1)}, bf16[2,1024,256]{2,1,0:T(8,128)(2,1)S(1)}, u32[]{:S(2)}, u32[]{:S(2)}) collective-permute-start(bf16[2,1024,256]{2,1,0:T(8,128)(2,1)S(1)} %get-tuple-element.53.a_ref.qg.own), channel_id=1, source_target_pairs={{4,0},{5,1},{6,2},{7,3},{8,4},{9,5},{10,6},{11,7},{12,8},{13,9},{1... | collective-permute-start | bytes 3145736 | tf_op jit(solution)/shard_map/ppermute | solution.py:20
  6.8 25.3 %collective-permute-start.3 = (bf16[2,1024,256]{2,1,0:T(8,128)(2,1)S(1)}, bf16[2,1024,256]{2,1,0:T(8,128)(2,1)S(1)}, u32[]{:S(2)}, u32[]{:S(2)}) collective-permute-start(bf16[2,1024,256]{2,1,0:T(8,128)(2,1)S(1)} %get-tuple-element.35.b_ref.own), channel_id=1, source_target_pairs={{0,4},{1,5},{2,6},{3,7},{4,8},{5,9},{6,10},{7,11},{8,12},{9,13},{1... | collective-permute-start | bytes 3145736 | tf_op jit(solution)/shard_map/ppermute | solution.py:20
  8.2 42.6 %collective-permute-start.2 = (bf16[2,1024,256]{2,1,0:T(8,128)(2,1)S(1)}, bf16[2,1024,256]{2,1,0:T(8,128)(2,1)S(1)}, u32[]{:S(2)}, u32[]{:S(2)}) collective-permute-start(bf16[2,1024,256]{2,1,0:T(8,128)(2,1)S(1)} %get-tuple-element.32.a_ref.qg.own), channel_id=1, source_target_pairs={{4,0},{5,1},{6,2},{7,3},{8,4},{9,5},{10,6},{11,7},{12,8},{13,9},{1... | collective-permute-start | bytes 3145736 | tf_op jit(solution)/shard_map/ppermute | solution.py:20
  12.2 42.9 %collective-permute-start.1 = (bf16[2,1024,256]{2,1,0:T(8,128)(2,1)S(1)}, bf16[2,1024,256]{2,1,0:T(8,128)(2,1)S(1)}, u32[]{:S(2)}, u32[]{:S(2)}) collective-permute-start(bf16[2,1024,256]{2,1,0:T(8,128)(2,1)S(1)} %get-tuple-element.34.b_ref.own), channel_id=1, source_target_pairs={{0,4},{1,5},{2,6},{3,7},{4,8},{5,9},{6,10},{7,11},{8,12},{9,13},{1... | collective-permute-start | bytes 3145736 | tf_op jit(solution)/shard_map/ppermute | solution.py:20
  32.2 41.1 %collective-permute-start.6 = (bf16[2,1024,256]{2,1,0:T(8,128)(2,1)S(1)}, bf16[2,1024,256]{2,1,0:T(8,128)(2,1)S(1)}, u32[]{:S(2)}, u32[]{:S(2)}) collective-permute-start(bf16[2,1024,256]{2,1,0:T(8,128)(2,1)S(1)} %collective-permute-done.4.b_ref.far4), channel_id=1, source_target_pairs={{4,0},{5,1},{6,2},{7,3},{8,4},{9,5},{10,6},{11,7},{12,8},{13,9},{1... | collective-permute-start | bytes 3145736 | tf_op jit(solution)/shard_map/ppermute | solution.py:20
  34.2 42.9 %collective-permute-start.5 = (bf16[2,1024,256]{2,1,0:T(8,128)(2,1)S(1)}, bf16[2,1024,256]{2,1,0:T(8,128)(2,1)S(1)}, u32[]{:S(2)}, u32[]{:S(2)}) collective-permute-start(bf16[2,1024,256]{2,1,0:T(8,128)(2,1)S(1)} %collective-permute-done.3.a_ref.far4), channel_id=1, source_target_pairs={{0,4},{1,5},{2,6},{3,7},{4,8},{5,9},{6,10},{7,11},{8,12},{9,13},{1... | collective-permute-start | bytes 3145736 | tf_op jit(solution)/shard_map/ppermute | solution.py:20
  50.7 30.3 %collective-permute-start.11 = (bf16[2,1024,256]{2,1,0:T(8,128)(2,1)S(1)}, bf16[2,1024,256]{2,1,0:T(8,128)(2,1)S(1)}, u32[]{:S(2)}, u32[]{:S(2)}) collective-permute-start(bf16[2,1024,256]{2,1,0:T(8,128)(2,1)S(1)} %pick.9), channel_id=1, source_target_pairs={{0,2},{1,3},{2,0},{3,1},{4,6},{5,7},{6,4},{7,5},{8,10},{9,11},{10,... | collective-permute-start | bytes 3145736 | tf_op jit(solution)/shard_map/ppermute | solution.py:25
  51.0 44.7 %collective-permute-start.9 = (bf16[2,1024,256]{2,1,0:T(8,128)(2,1)S(1)}, bf16[2,1024,256]{2,1,0:T(8,128)(2,1)S(1)}, u32[]{:S(2)}, u32[]{:S(2)}) collective-permute-start(bf16[2,1024,256]{2,1,0:T(8,128)(2,1)S(1)} %collective-permute-done.2.b_ref.far4), channel_id=1, source_target_pairs={{4,0},{5,1},{6,2},{7,3},{8,4},{9,5},{10,6},{11,7},{12,8},{13,9},{1... | collective-permute-start | bytes 3145736 | tf_op jit(solution)/shard_map/ppermute | solution.py:20
  55.2 44.4 %collective-permute-start.8 = (bf16[2,1024,256]{2,1,0:T(8,128)(2,1)S(1)}, bf16[2,1024,256]{2,1,0:T(8,128)(2,1)S(1)}, u32[]{:S(2)}, u32[]{:S(2)}) collective-permute-start(bf16[2,1024,256]{2,1,0:T(8,128)(2,1)S(1)} %collective-permute-done.1.a_ref.far4), channel_id=1, source_target_pairs={{0,4},{1,5},{2,6},{3,7},{4,8},{5,9},{6,10},{7,11},{8,12},{9,13},{1... | collective-permute-start | bytes 3145736 | tf_op jit(solution)/shard_map/ppermute | solution.py:20
  56.7 45.0 %copy-start.3 = (s32[1,4]{1,0:T(1,128)S(1)}, s32[1,4]{1,0:T(1,128)}, u32[]{:S(2)}) copy-start(s32[1,4]{1,0:T(1,128)} %links.3) | copy-start | bytes 52
  77.1 24.6 %collective-permute-start.12 = (bf16[2,1024,256]{2,1,0:T(8,128)(2,1)S(1)}, bf16[2,1024,256]{2,1,0:T(8,128)(2,1)S(1)}, u32[]{:S(2)}, u32[]{:S(2)}) collective-permute-start(bf16[2,1024,256]{2,1,0:T(8,128)(2,1)S(1)} %pick.10), channel_id=1, source_target_pairs={{0,1},{1,0},{2,3},{3,2},{4,5},{5,4},{6,7},{7,6},{8,9},{9,8},{10,11... | collective-permute-start | bytes 3145736 | tf_op jit(solution)/shard_map/ppermute | solution.py:25
  81.1 20.6 %collective-permute-start.13 = (bf16[2,1024,256]{2,1,0:T(8,128)(2,1)S(1)}, bf16[2,1024,256]{2,1,0:T(8,128)(2,1)S(1)}, u32[]{:S(2)}, u32[]{:S(2)}) collective-permute-start(bf16[2,1024,256]{2,1,0:T(8,128)(2,1)S(1)} %pick.11), channel_id=1, source_target_pairs={{0,1},{1,0},{2,3},{3,2},{4,5},{5,4},{6,7},{7,6},{8,9},{9,8},{10,11... | collective-permute-start | bytes 3145736 | tf_op jit(solution)/shard_map/ppermute | solution.py:25
  81.2 24.4 %collective-permute-start.7 = (bf16[2,1024,256]{2,1,0:T(8,128)(2,1)S(1)}, bf16[2,1024,256]{2,1,0:T(8,128)(2,1)S(1)}, u32[]{:S(2)}, u32[]{:S(2)}) collective-permute-start(bf16[2,1024,256]{2,1,0:T(8,128)(2,1)S(1)} %pick.6), channel_id=1, source_target_pairs={{0,2},{1,3},{2,0},{3,1},{4,6},{5,7},{6,4},{7,5},{8,10},{9,11},{10,... | collective-permute-start | bytes 3145736 | tf_op jit(solution)/shard_map/ppermute | solution.py:25
  99.6 6.0 %collective-permute-start.10 = (bf16[2,1024,256]{2,1,0:T(8,128)(2,1)S(1)}, bf16[2,1024,256]{2,1,0:T(8,128)(2,1)S(1)}, u32[]{:S(2)}, u32[]{:S(2)}) collective-permute-start(bf16[2,1024,256]{2,1,0:T(8,128)(2,1)S(1)} %pick.7), channel_id=1, source_target_pairs={{0,1},{1,0},{2,3},{3,2},{4,5},{5,4},{6,7},{7,6},{8,9},{9,8},{10,11... | collective-permute-start | bytes 3145736 | tf_op jit(solution)/shard_map/ppermute | solution.py:25
  105.6 9.4 %collective-permute-start.14 = (bf16[2,1024,256]{2,1,0:T(8,128)(2,1)S(1)}, bf16[2,1024,256]{2,1,0:T(8,128)(2,1)S(1)}, u32[]{:S(2)}, u32[]{:S(2)}) collective-permute-start(bf16[2,1024,256]{2,1,0:T(8,128)(2,1)S(1)} %pick.8), channel_id=1, source_target_pairs={{0,1},{1,0},{2,3},{3,2},{4,5},{5,4},{6,7},{7,6},{8,9},{9,8},{10,11... | collective-permute-start | bytes 3145736 | tf_op jit(solution)/shard_map/ppermute | solution.py:25
  107.0 19.8 %collective-permute-start.22 = (f32[32,256]{1,0:T(8,128)S(1)}, f32[32,256]{1,0:T(8,128)S(1)}, u32[]{:S(2)}, u32[]{:S(2)}) collective-permute-start(f32[32,256]{1,0:T(8,128)S(1)} %get-tuple-element.45), channel_id=1, source_target_pairs={{8,0},{9,1},{10,2},{11,3},{12,4},{13,5},{14,6},{15,7},{24,16},{25,... | collective-permute-start | bytes 98312 | tf_op jit(solution)/shard_map/ppermute | solution.py:20
  108.9 10.5 %collective-permute-start.19 = (f32[32,256]{1,0:T(8,128)S(1)}, f32[32,256]{1,0:T(8,128)S(1)}, u32[]{:S(2)}, u32[]{:S(2)}) collective-permute-start(f32[32,256]{1,0:T(8,128)S(1)} %get-tuple-element.55), channel_id=1, source_target_pairs={{1,0},{2,1},{3,2},{4,3},{5,4},{6,5},{7,6},{8,7},{9,8},{10,9},{11,1... | collective-permute-start | bytes 98312 | tf_op jit(solution)/shard_map/ppermute | solution.py:20
  111.1 11.9 %collective-permute-start.20 = (f32[32,256]{1,0:T(8,128)S(1)}, f32[32,256]{1,0:T(8,128)S(1)}, u32[]{:S(2)}, u32[]{:S(2)}) collective-permute-start(f32[32,256]{1,0:T(8,128)S(1)} %get-tuple-element.56), channel_id=1, source_target_pairs={{2,0},{3,1},{4,2},{5,3},{6,4},{7,5},{8,6},{9,7},{10,8},{11,9},{12,... | collective-permute-start | bytes 98312 | tf_op jit(solution)/shard_map/ppermute | solution.py:20
  113.0 11.9 %collective-permute-start.21 = (f32[32,256]{1,0:T(8,128)S(1)}, f32[32,256]{1,0:T(8,128)S(1)}, u32[]{:S(2)}, u32[]{:S(2)}) collective-permute-start(f32[32,256]{1,0:T(8,128)S(1)} %get-tuple-element.57), channel_id=1, source_target_pairs={{4,0},{5,1},{6,2},{7,3},{8,4},{9,5},{10,6},{11,7},{12,8},{13,9},{1... | collective-permute-start | bytes 98312 | tf_op jit(solution)/shard_map/ppermute | solution.py:20
  117.7 13.2 %collective-permute-start.18 = (f32[32,256]{1,0:T(8,128)S(1)}, f32[32,256]{1,0:T(8,128)S(1)}, u32[]{:S(2)}, u32[]{:S(2)}) collective-permute-start(f32[32,256]{1,0:T(8,128)S(1)} %get-tuple-element.51), channel_id=1, source_target_pairs={{8,0},{9,1},{10,2},{11,3},{12,4},{13,5},{14,6},{15,7},{24,16},{25,... | collective-permute-start | bytes 98312 | tf_op jit(solution)/shard_map/ppermute | solution.py:20
  119.3 11.5 %collective-permute-start.15 = (f32[32,256]{1,0:T(8,128)S(1)}, f32[32,256]{1,0:T(8,128)S(1)}, u32[]{:S(2)}, u32[]{:S(2)}) collective-permute-start(f32[32,256]{1,0:T(8,128)S(1)} %get-tuple-element.48), channel_id=1, source_target_pairs={{1,0},{2,1},{3,2},{4,3},{5,4},{6,5},{7,6},{8,7},{9,8},{10,9},{11,1... | collective-permute-start | bytes 98312 | tf_op jit(solution)/shard_map/ppermute | solution.py:20
  123.0 7.9 %collective-permute-start.16 = (f32[32,256]{1,0:T(8,128)S(1)}, f32[32,256]{1,0:T(8,128)S(1)}, u32[]{:S(2)}, u32[]{:S(2)}) collective-permute-start(f32[32,256]{1,0:T(8,128)S(1)} %get-tuple-element.49), channel_id=1, source_target_pairs={{2,0},{3,1},{4,2},{5,3},{6,4},{7,5},{8,6},{9,7},{10,8},{11,9},{12,... | collective-permute-start | bytes 98312 | tf_op jit(solution)/shard_map/ppermute | solution.py:20
  125.0 5.9 %collective-permute-start.17 = (f32[32,256]{1,0:T(8,128)S(1)}, f32[32,256]{1,0:T(8,128)S(1)}, u32[]{:S(2)}, u32[]{:S(2)}) collective-permute-start(f32[32,256]{1,0:T(8,128)S(1)} %get-tuple-element.50), channel_id=1, source_target_pairs={{4,0},{5,1},{6,2},{7,3},{8,4},{9,5},{10,6},{11,7},{12,8},{13,9},{1... | collective-permute-start | bytes 98312 | tf_op jit(solution)/shard_map/ppermute | solution.py:20
  (3 other events, 33.5 us)

commit v5 on v4

v5 whole, which is shorter than its diff:
```python
import functools

import jax
import jax.numpy as jnp
from jax import lax
from jax.experimental import pallas as pl
from jax.experimental.pallas import tpu as pltpu
from jax.sharding import PartitionSpec as P

HEADS = 16
NDIL = 4
LANES = 128
SUBLANES = 8
PIECE = 256
US = 3.69e6
BY_BIT0, BY_BIT1 = (0, 1, 0, 1), (0, 0, 1, 1)
VMEM_BYTES = 32 * 2**20


def shift(block, distance):
    n = lax.axis_size("frame")
    return lax.ppermute(block, "frame", [(i, i + distance) for i in range(n) if 0 <= i + distance < n])


def swap(block, bit):
    n = lax.axis_size("frame")
    return lax.ppermute(block, "frame", [(i, i ^ bit) for i in range(n)])


def place_bit(bit):
    return lax.rem(lax.axis_index("frame") // 2**bit, 2)


def params():
    return pltpu.CompilerParams(vmem_limit_bytes=VMEM_BYTES)


SMEM = pl.BlockSpec(memory_space=pltpu.SMEM)
VMEM = pl.BlockSpec(memory_space=pltpu.VMEM)


def after(block, *done):
    return lax.optimization_barrier((block, *done))[0] if done else block


def pack(queries, keys, values, grad_out):
    _, patches, width = queries.shape
    half = patches // 2

    def kernel(q_hbm, k_hbm, v_hbm, g_hbm, kv0, kv1, qg0, qg1, y_out, q_ref, k_ref, v_ref, g_ref, sems):
        pieces = []
        for i in range(2):
            rows = pl.ds(i * half, half)
            for part, up, down in ((0, (k_hbm, k_ref), (q_hbm, q_ref)), (1, (v_hbm, v_ref), (g_hbm, g_ref))):
                for (hbm, ref), out, bit in ((up, (kv0, kv1)[i], 0), (down, (qg0, qg1)[i], 1)):
                    copy = pltpu.make_async_copy(hbm.at[0, rows, :], ref.at[rows, :], sems.at[len(pieces)])
                    pieces.append((copy, ref, i * half, out, part, bit))
        for piece in pieces:
            piece[0].start()
        for copy, ref, start, out, part, bit in pieces:
            copy.wait()
            for p in range(0, half, LANES):
                turned = ref[start + p:start + p + LANES, :].T
                out[part, :, p:p + LANES] = turned

                if start == 0:
                    @pl.when(place_bit(1) == bit)
                    def _():
                        y_out[part, :, p:p + LANES] = turned

    half_shape = jax.ShapeDtypeStruct((2, width, half), jnp.bfloat16)
    return pl.pallas_call(
        kernel,
        in_specs=[pl.BlockSpec(memory_space=pl.ANY)] * 4,
        out_specs=[VMEM] * 5,
        out_shape=[half_shape] * 5,
        scratch_shapes=[pltpu.VMEM((patches, width), jnp.bfloat16)] * 4 + [pltpu.SemaphoreType.DMA((8,))],
        compiler_params=params(),
        name="pack",
    )(*(pltpu.with_memory_space_constraint(a, pltpu.HBM) for a in (queries, keys, values, grad_out)))


def pick(blocks, which, weight=1):
    def kernel(*refs):
        place = 2 * place_bit(1) + place_bit(0)
        for number, ref in enumerate(refs[:-1]):
            mine = [place == p for p in range(4) if which[p] == number]

            @pl.when(functools.reduce(jnp.logical_or, mine))
            def _(ref=ref):
                refs[-1][...] = ref[...]

    size = blocks[0].size
    return pl.pallas_call(
        kernel,
        in_specs=[VMEM] * len(blocks),
        out_specs=VMEM,
        out_shape=jax.ShapeDtypeStruct(blocks[0].shape, blocks[0].dtype),
        compiler_params=params(),
        cost_estimate=pl.CostEstimate(flops=0, bytes_accessed=int(weight * US), transcendentals=0),
        name="pick",
    )(*blocks)


def choose(blocks, bit, wanted, here):
    if len(blocks) == 1:
        return lambda i, rows: blocks[0][i, rows, here]
    use_first = place_bit(bit) == wanted
    return lambda i, rows: jnp.where(use_first, blocks[0][i, rows, here], blocks[1][i, rows, here])


def source_getters(own, two, one, far4, far8, wanted, here):
    return (
        choose([own], 0, wanted, here),
        choose(one, 0, wanted, here),
        choose(two, 1, wanted, here),
        choose([far4], 0, wanted, here),
        choose([far8], 0, wanted, here),
    )


def head_slices(width):
    size = width // HEADS
    return [slice(h * size, (h + 1) * size) for h in range(HEADS)]


def lanes(step):
    return pl.ds(pl.multiple_of(step * LANES, LANES), LANES)


def head_products(mine, other, part, here, into):
    for h, rows in enumerate(head_slices(mine.shape[1])):
        left = mine[part, rows, here].astype(jnp.float32)
        for slot, get in enumerate(other):
            product = left * get(part, rows).astype(jnp.float32)
            into[slot, h * SUBLANES:(h + 1) * SUBLANES, :] = jnp.sum(product.reshape(-1, SUBLANES, LANES), axis=0)


def sublane_total(ref, slot):
    parts = [ref[slot, pl.ds(i, HEADS, stride=SUBLANES), :] for i in range(SUBLANES)]
    while len(parts) > 1:
        parts = [a + b for a, b in zip(parts[::2], parts[1::2])]
    return parts[0]


def product_kernel(n_two, n_one, n_other, qg, *rest):
    *sources, out, work = rest
    others = sources[:n_other]
    two, one = sources[n_other:n_other + n_two], sources[n_other + n_two:]

    @pl.loop(0, qg.shape[2] // LANES)
    def _(step):
        here = lanes(step)
        getters = [choose([o], 0, 1, here) for o in others]
        getters += [choose(blocks, bit, 1, here) for blocks, bit in ((one, 0), (two, 1)) if blocks]
        for part in range(2):
            head_products(qg, getters, part, here, work)
            for slot in range(len(getters)):
                out[part, slot, :, here] = sublane_total(work, slot)


def products_of(qg, others, two, one, weight):
    rows = qg.shape[2]
    slots = len(others) + bool(two) + bool(one)
    return pl.pallas_call(
        functools.partial(product_kernel, len(two), len(one), len(others)),
        in_specs=[VMEM] * (1 + len(others) + len(two) + len(one)),
        out_specs=VMEM,
        out_shape=jax.ShapeDtypeStruct((2, slots, HEADS, rows), jnp.float32),
        scratch_shapes=[pltpu.VMEM((slots, HEADS * SUBLANES, LANES), jnp.float32)],
        compiler_params=params(),
        cost_estimate=pl.CostEstimate(flops=0, bytes_accessed=int(weight * US), transcendentals=0),
        name="products",
    )(qg, *others, *two, *one)


def score_kernel(head_size, links, near0, near1, far0, far1, self_pair, pair1, pair2, pair4, pair8):
    scale = head_size ** (-0.5)
    half = far0.shape[-1]
    for start, near, far in ((0, near0, far0), (half, near1, far1)):
        here = slice(start, start + half)
        products = [[near[part, 0], near[part, 2], near[part, 3], near[part, 1], far[part, 0]] for part in range(2)]
        scores = [p * scale for p in products[0]]
        scores = scores[:1] + [jnp.where(links[0, j] > 0, s, -1e30) for j, s in enumerate(scores[1:])]
        highest = functools.reduce(jnp.maximum, scores)
        raw = [jnp.exp(s - highest) for s in scores]
        raw = raw[:1] + [jnp.where(links[0, j] > 0, r, 0.0) for j, r in enumerate(raw[1:])]
        total = functools.reduce(jnp.add, raw)
        probability = [r / total for r in raw]
        inner = functools.reduce(jnp.add, [p * g for p, g in zip(probability, products[1])])
        for pair, p, g in zip((self_pair, pair1, pair2, pair4, pair8), probability, products[1]):
            pair[:HEADS, here] = p * (g - inner) * scale
            pair[HEADS:, here] = p


def scores_of(links, near0, near1, far0, far1, head_size, weight):
    pair = jax.ShapeDtypeStruct((2 * HEADS, 2 * far0.shape[-1]), jnp.float32)
    return pl.pallas_call(
        functools.partial(score_kernel, head_size),
        in_specs=[SMEM] + [VMEM] * 4,
        out_specs=[VMEM] * 5,
        out_shape=[pair] * 5,
        compiler_params=params(),
        cost_estimate=pl.CostEstimate(flops=0, bytes_accessed=int(weight * US), transcendentals=0),
        name="scores",
    )(links, near0, near1, far0, far1)


def query_kernel(start, own, two_a, two_b, one_a, one_b, far4, far8, self_pair, pair1, pair2, pair4, pair8, w_query, out,
                 grad_query):
    _, width, patches = own.shape
    pairs = (self_pair, pair1, pair2, pair4, pair8)

    @pl.loop(0, patches // LANES)
    def _(step):
        here = lanes(step)
        there = lanes(step + start // LANES)
        getters = source_getters(own, (two_a, two_b), (one_a, one_b), far4, far8, 1, here)
        for h, rows in enumerate(head_slices(width)):
            terms = [pairs[s][h:h + 1, there] * get(0, rows).astype(jnp.float32) for s, get in enumerate(getters)]
            grad_query[rows, here] = functools.reduce(jnp.add, terms).astype(jnp.bfloat16)

    out[...] = jnp.dot(w_query[...], grad_query[...], preferred_element_type=jnp.float32)


def query_part_of(own, two, one, far4, far8, pairs, w_query, start, weight):
    _, width, rows = own.shape
    return pl.pallas_call(
        functools.partial(query_kernel, start),
        in_specs=[VMEM] * 13,
        out_specs=VMEM,
        out_shape=jax.ShapeDtypeStruct((w_query.shape[0], rows), jnp.float32),
        scratch_shapes=[pltpu.VMEM((width, rows), jnp.bfloat16)],
        compiler_params=params(),
        cost_estimate=pl.CostEstimate(flops=0, bytes_accessed=int(weight * US), transcendentals=0),
        name="query_part",
    )(own, *two, *one, far4, far8, *pairs, w_query)


def sum_kernel(shapes, self_pair, pair8, pair4, pair2, pair1, w_key, w_value, *rest):
    out, key_ref, value_ref, result, sems = rest[-5:]
    rest = rest[:-5]
    pairs = (self_pair, pair1, pair2, pair4, pair8)
    copies = []
    for i, (n_two, n_one) in enumerate(shapes):
        own, query_part, far4, far8 = rest[:4]
        two, one, rest = rest[4:4 + n_two], rest[4 + n_two:4 + n_two + n_one], rest[4 + n_two + n_one:]
        _, width, patches = own.shape

        @pl.loop(0, patches // LANES)
        def _(step):
            here = lanes(step)
            there = lanes(step + i * (patches // LANES))
            getters = source_getters(own, two, one, far4, far8, 0, here)
            for h, rows in enumerate(head_slices(width)):
                for part, into in ((0, key_ref), (1, value_ref)):
                    row = part * HEADS + h
                    terms = [pairs[s][row:row + 1, there] * get(part, rows).astype(jnp.float32)
                             for s, get in enumerate(getters)]
                    into[rows, there] = functools.reduce(jnp.add, terms).astype(jnp.bfloat16)

        columns = pl.ds(i * patches, patches)
        for o in range(0, width, PIECE):
            piece = slice(o, o + PIECE)
            total = query_part[piece, :] + jnp.dot(
                w_key[piece, :], key_ref[:, columns], preferred_element_type=jnp.float32)
            total = total + jnp.dot(w_value[piece, :], value_ref[:, columns], preferred_element_type=jnp.float32)
            result[columns, piece] = total.astype(jnp.bfloat16).T
        copies.append(pltpu.make_async_copy(result.at[columns, :], out.at[columns, :], sems.at[i]))
        copies[-1].start()
    for copy in copies:
        copy.wait()


def sums_of(halves, pairs, weights, weight):
    _, width, rows = halves[0][0].shape
    operands = [*pairs, *weights]
    for own, query_part, two, one, far4, far8 in halves:
        operands += [own, query_part, far4, far8, *two, *one]
    return pl.pallas_call(
        functools.partial(sum_kernel, [(len(h[2]), len(h[3])) for h in halves]),
        in_specs=[VMEM] * len(operands),
        out_specs=pl.BlockSpec(memory_space=pl.ANY),
        out_shape=jax.ShapeDtypeStruct((2 * rows, width), jnp.bfloat16),
        scratch_shapes=[pltpu.VMEM((width, 2 * rows), jnp.bfloat16)] * 2
        + [pltpu.VMEM((2 * rows, width), jnp.bfloat16), pltpu.SemaphoreType.DMA((2,))],
        compiler_params=params(),
        cost_estimate=pl.CostEstimate(flops=0, bytes_accessed=int(weight * US), transcendentals=0),
        name="sums",
    )(*operands)


def per_device(queries, keys, values, grad_out, links, w_query, w_key, w_value):
    patches = queries.shape[1]
    half = patches // 2
    head_size = keys.shape[2] // HEADS
    kv0, kv1, qg0, qg1, owed = pack(queries, keys, values, grad_out)
    up4_0 = shift(kv0, 4)
    down4_0 = shift(qg0, -4)
    y_a = swap(owed, 2)
    up4_1 = shift(kv1, 4)
    down4_1 = shift(qg1, -4)
    y_b = swap(after(pick((kv1, up4_0), BY_BIT1, 0), y_a, down4_0), 2)
    up8_0 = shift(after(up4_0, down4_0), 4)
    down8_0 = shift(after(down4_0, up4_0), -4)
    c_a = swap(pick((after(kv0, up4_1, down4_1), qg0), BY_BIT0, 2.8), 1)
    y_c = swap(pick((down4_0, up4_1), BY_BIT1, 0), 2)
    up8_1 = shift(after(up4_1, y_b), 4)
    down8_1 = shift(after(down4_1, up8_0, down8_0), -4)
    c_b = swap(pick((kv1, y_b, y_a), (0, 1, 0, 2), 0), 1)
    far0 = products_of(after(qg0, down8_0), [up8_0], (), (), 5.7)
    near0 = products_of(qg0, [kv0, up4_0], (y_a, y_b), (c_a, c_b), 0)
    y_d = swap(after(pick((down4_1, qg1), BY_BIT1, 0), up8_0, down8_0), 2)
    c_c = swap(after(pick((y_a, y_c, y_b), (0, 1, 1, 2), 0), near0, far0), 1)
    near1 = products_of(qg1, [kv1, up4_1], (y_b, y_c), (c_b, c_c), 0)
    far1 = products_of(qg1, [up8_1], (), (), 10)
    pairs = scores_of(links, near0, near1, far0, far1, head_size, 0)
    self_pair, pair1, pair2, pair4, pair8 = pairs
    came8 = shift(pair8, -8)
    came4 = shift(pair4, -4)
    came2 = shift(pair2, -2)
    came1 = shift(pair1, -1)
    query_part0 = query_part_of(kv0, (y_a, y_b), (c_a, c_b), up4_0, up8_0, pairs, w_query, 0, 0)
    query_part1 = query_part_of(kv1, (y_b, y_c), (c_b, c_c), up4_1, up8_1, pairs, w_query, half, 0)
    c_d = swap(pick((y_d, qg1), BY_BIT0, 0), 1)
    halves = (
        (qg0, query_part0, (y_a, y_c), (c_a, c_c), down4_0, down8_0),
        (qg1, query_part1, (y_d,), (c_d,), down4_1, down8_1),
    )
    out = sums_of(halves, (self_pair, came8, came4, came2, came1), (w_key, w_value), 3)
    return out[None]


def solution(mesh):
    by_frame = P(("dom", "frame"), None, None)
    return jax.shard_map(
        per_device,
        mesh=mesh,
        in_specs=(by_frame,) * 4 + (P(("dom", "frame"), None), P(), P(), P()),
        out_specs=by_frame,
        check_vma=False,
    )
```

time: 135 us -> 126 us (0.933)
  waiting for transfers between devices: 73.4 us -> 62.5 us
  starting transfers between devices: 43.3 us -> 46.2 us
  Pallas kernels: 17.2 us -> 15.4 us
    ppermute x16 -> x12, waiting for transfers between devices: 72.2 us -> 46 us  [shift(): lax.ppermute(block, 'frame', [(i, i + distance) for i in range(n) if 0 <=...]
    ppermute x7 -> x8, waiting for transfers between devices: 1.18 us -> 16.5 us  [swap(): return lax.ppermute(block, 'frame', [(i, i ^ bit) for i in range(n)])]
    ppermute x7 -> x8, starting transfers between devices: 9.33 us -> 17.5 us  [swap(): return lax.ppermute(block, 'frame', [(i, i ^ bit) for i in range(n)])]
    ppermute x16 -> x12, starting transfers between devices: 33.9 us -> 28.7 us  [shift(): lax.ppermute(block, 'frame', [(i, i + distance) for i in range(n) if 0 <=...]
    pallas_call x12 -> x15, Pallas kernels: 13.8 us -> 12.3 us  [the longest x1 5.7 us: sums_of(): pl.pallas_call(functools.partial(sum_kernel, [(len(h[2]), len(h[3])) for...]
  transfers between devices with their start and end apart: 23 -> 20, of which waited for: 8 -> 9; matrix products, arithmetic and copies ran while one was open for 0% -> 0% of each run, Pallas kernels for 8% -> 5%
where the time goes in v5:
time: 126 us; the launch traced here: 125 us
  waiting for transfers between devices  62.5 us (50%)
  starting transfers between devices  46.2 us (37%)
  Pallas kernels  15.4 us (12%)
    ppermute x12, waiting for transfers between devices, shift(): lax.ppermute(block, 'frame', [(i, i + distance) for i in range(n) if 0 <=...  46 us
    ppermute x12, starting transfers between devices, shift(): lax.ppermute(block, 'frame', [(i, i + distance) for i in range(n) if 0 <=...  28.7 us
    ppermute x8, starting transfers between devices, swap(): return lax.ppermute(block, 'frame', [(i, i ^ bit) for i in range(n)])  17.5 us
    ppermute x8, waiting for transfers between devices, swap(): return lax.ppermute(block, 'frame', [(i, i ^ bit) for i in range(n)])  16.5 us
    pallas_call x1, Pallas kernels, sums_of(): pl.pallas_call(functools.partial(sum_kernel, [(len(h[2]), len(h[3])) for...  5.7 us
    pallas_call x1, Pallas kernels, pack(): pl.pallas_call(kernel, in_specs=[pl.BlockSpec(memory_space=pl.ANY)] * 4,...  3.02 us
    pallas_call x4, Pallas kernels, products_of(): pl.pallas_call(functools.partial(product_kernel, len(two), len(one), len(...  2.87 us
    pallas_call x2, Pallas kernels, query_part_of(): pl.pallas_call(functools.partial(query_kernel, start), in_specs=[VMEM] *...  2.65 us
  transfers between devices with their start and end apart: 20, of which 9 were waited for; matrix products, arithmetic and copies ran while one was open for 0% of the time, Pallas kernels for 5%

profile of v5, /device:TPU:27, one launch (start us, length us, event | category | flops | bytes accessed | tf_op | source)
XLA Modules:
  0.0 125.1 jit_solution(17857529885168155888)
XLA Ops:
  0.0 3.0 %pack.1 = (bf16[2,1024,256]{2,1,0:T(8,128)(2,1)S(1)}, bf16[2,1024,256]{2,1,0:T(8,128)(2,1)S(1)}, bf16[2,1024,256]{2,1,0:T(8,128)(2,1)S(1)}, bf16[2,1024,256]{2,1,0:T(8,128)(2,1)S(1)}, bf16[2,1024,256]{2,1,0:T(8,128)(2,1)S(1)}) custom-call(bf16[1,512,1024]{2,1,0:T(8,128)(2,1)} %q_hbm.1, bf16[1,512,1024]{2,1,0:T(8,128)(2,1)} %k_hbm.1, ...), custom_call_target="tpu_custom_call" | custom-call | tf_op jit(solution)/shard_map/pack/pallas_call | solution.py:72
  3.0 1.3 %collective-permute-start = (bf16[2,1024,256]{2,1,0:T(8,128)(2,1)S(1)}, bf16[2,1024,256]{2,1,0:T(8,128)(2,1)S(1)}, u32[]{:S(2)}, u32[]{:S(2)}) collective-permute-start(bf16[2,1024,256]{2,1,0:T(8,128)(2,1)S(1)} %get-tuple-element.30.refs_0_.rest_0_.own), channel_id=1, source_target_pairs={{0,4},{1,5},{2,6},{3,7},{4,8},{5,9},{6,10},{7,11},{8,12},{9,13},{1... | collective-permute-start | bytes 3145736 | tf_op jit(solution)/shard_map/ppermute | solution.py:22
  4.3 4.1 %collective-permute-start.2 = (bf16[2,1024,256]{2,1,0:T(8,128)(2,1)S(1)}, bf16[2,1024,256]{2,1,0:T(8,128)(2,1)S(1)}, u32[]{:S(2)}, u32[]{:S(2)}) collective-permute-start(bf16[2,1024,256]{2,1,0:T(8,128)(2,1)S(1)} %get-tuple-element.32.refs_1_.qg.rest_0_), channel_id=1, source_target_pairs={{4,0},{5,1},{6,2},{7,3},{8,4},{9,5},{10,6},{11,7},{12,8},{13,9},{1... | collective-permute-start | bytes 3145736 | tf_op jit(solution)/shard_map/ppermute | solution.py:22
  8.4 1.3 %collective-permute-start.1 = (bf16[2,1024,256]{2,1,0:T(8,128)(2,1)S(1)}, bf16[2,1024,256]{2,1,0:T(8,128)(2,1)S(1)}, u32[]{:S(2)}, u32[]{:S(2)}) collective-permute-start(bf16[2,1024,256]{2,1,0:T(8,128)(2,1)S(1)} %get-tuple-element.26), channel_id=1, source_target_pairs={{0,2},{1,3},{2,0},{3,1},{4,6},{5,7},{6,4},{7,5},{8,10},{9,11},{10,... | collective-permute-start | bytes 3145736 | tf_op jit(solution)/shard_map/ppermute | solution.py:27
  11.0 4.1 %collective-permute-start.5 = (bf16[2,1024,256]{2,1,0:T(8,128)(2,1)S(1)}, bf16[2,1024,256]{2,1,0:T(8,128)(2,1)S(1)}, u32[]{:S(2)}, u32[]{:S(2)}) collective-permute-start(bf16[2,1024,256]{2,1,0:T(8,128)(2,1)S(1)} %get-tuple-element.29.qg.refs_1_.rest_8_), channel_id=1, source_target_pairs={{4,0},{5,1},{6,2},{7,3},{8,4},{9,5},{10,6},{11,7},{12,8},{13,9},{1... | collective-permute-start | bytes 3145736 | tf_op jit(solution)/shard_map/ppermute | solution.py:22
  15.0 13.9 %collective-permute-done.refs_1_.rest_1_.far4 = bf16[2,1024,256]{2,1,0:T(8,128)(2,1)S(1)} collective-permute-done((bf16[2,1024,256]{2,1,0:T(8,128)(2,1)S(1)}, bf16[2,1024,256]{2,1,0:T(8,128)(2,1)S(1)}, u32[]{:S(2)}, u32[]{:S(2)}) %collective-permute-start) | collective-permute-done | bytes 1048608 | tf_op jit(solution)/shard_map/ppermute | solution.py:22
  29.8 2.1 %collective-permute-done.1.refs_2_.rest_2_.refs_0_.two_a.rest_4_ = bf16[2,1024,256]{2,1,0:T(8,128)(2,1)S(1)} collective-permute-done((bf16[2,1024,256]{2,1,0:T(8,128)(2,1)S(1)}, bf16[2,1024,256]{2,1,0:T(8,128)(2,1)S(1)}, u32[]{:S(2)}, u32[]{:S(2)}) %collective-permute-start.1) | collective-permute-done | bytes 1048608 | tf_op jit(solution)/shard_map/ppermute | solution.py:27
  33.1 2.1 %collective-permute-start.9 = (bf16[2,1024,256]{2,1,0:T(8,128)(2,1)S(1)}, bf16[2,1024,256]{2,1,0:T(8,128)(2,1)S(1)}, u32[]{:S(2)}, u32[]{:S(2)}) collective-permute-start(bf16[2,1024,256]{2,1,0:T(8,128)(2,1)S(1)} %collective-permute-done.2.refs_0_.rest_2_), channel_id=1, source_target_pairs={{4,0},{5,1},{6,2},{7,3},{8,4},{9,5},{10,6},{11,7},{12,8},{13,9},{1... | collective-permute-start | bytes 3145736 | tf_op jit(solution)/shard_map/ppermute | solution.py:22
  36.5 14.9 %collective-permute-done.4.refs_1_.rest_1_.far4 = bf16[2,1024,256]{2,1,0:T(8,128)(2,1)S(1)} collective-permute-done((bf16[2,1024,256]{2,1,0:T(8,128)(2,1)S(1)}, bf16[2,1024,256]{2,1,0:T(8,128)(2,1)S(1)}, u32[]{:S(2)}, u32[]{:S(2)}) %collective-permute-start.4) | collective-permute-done | bytes 1048608 | tf_op jit(solution)/shard_map/ppermute | solution.py:22
  52.4 1.3 %collective-permute-start.8 = (bf16[2,1024,256]{2,1,0:T(8,128)(2,1)S(1)}, bf16[2,1024,256]{2,1,0:T(8,128)(2,1)S(1)}, u32[]{:S(2)}, u32[]{:S(2)}) collective-permute-start(bf16[2,1024,256]{2,1,0:T(8,128)(2,1)S(1)} %pick.10), channel_id=1, source_target_pairs={{0,2},{1,3},{2,0},{3,1},{4,6},{5,7},{6,4},{7,5},{8,10},{9,11},{10,... | collective-permute-start | bytes 3145736 | tf_op jit(solution)/shard_map/ppermute | solution.py:27
  53.7 3.7 %collective-permute-start.6 = (bf16[2,1024,256]{2,1,0:T(8,128)(2,1)S(1)}, bf16[2,1024,256]{2,1,0:T(8,128)(2,1)S(1)}, u32[]{:S(2)}, u32[]{:S(2)}) collective-permute-start(bf16[2,1024,256]{2,1,0:T(8,128)(2,1)S(1)} %pick.8), channel_id=1, source_target_pairs={{0,1},{1,0},{2,3},{3,2},{4,5},{5,4},{6,7},{7,6},{8,9},{9,8},{10,11... | collective-permute-start | bytes 3145736 | tf_op jit(solution)/shard_map/ppermute | solution.py:27
  57.5 1.9 %collective-permute-start.7 = (bf16[2,1024,256]{2,1,0:T(8,128)(2,1)S(1)}, bf16[2,1024,256]{2,1,0:T(8,128)(2,1)S(1)}, u32[]{:S(2)}, u32[]{:S(2)}) collective-permute-start(bf16[2,1024,256]{2,1,0:T(8,128)(2,1)S(1)} %pick.9), channel_id=1, source_target_pairs={{0,1},{1,0},{2,3},{3,2},{4,5},{5,4},{6,7},{7,6},{8,9},{9,8},{10,11... | collective-permute-start | bytes 3145736 | tf_op jit(solution)/shard_map/ppermute | solution.py:27
  59.5 15.2 %collective-permute-done.9.rest_3_ = bf16[2,1024,256]{2,1,0:T(8,128)(2,1)S(1)} collective-permute-done((bf16[2,1024,256]{2,1,0:T(8,128)(2,1)S(1)}, bf16[2,1024,256]{2,1,0:T(8,128)(2,1)S(1)}, u32[]{:S(2)}, u32[]{:S(2)}) %collective-permute-start.9) | collective-permute-done | bytes 1048608 | tf_op jit(solution)/shard_map/ppermute | solution.py:22
  79.1 4.4 %collective-permute-start.11 = (bf16[2,1024,256]{2,1,0:T(8,128)(2,1)S(1)}, bf16[2,1024,256]{2,1,0:T(8,128)(2,1)S(1)}, u32[]{:S(2)}, u32[]{:S(2)}) collective-permute-start(bf16[2,1024,256]{2,1,0:T(8,128)(2,1)S(1)} %pick.11), channel_id=1, source_target_pairs={{0,1},{1,0},{2,3},{3,2},{4,5},{5,4},{6,7},{7,6},{8,9},{9,8},{10,11... | collective-permute-start | bytes 3145736 | tf_op jit(solution)/shard_map/ppermute | solution.py:27
  83.5 2.4 %collective-permute-start.17 = (bf16[2,1024,256]{2,1,0:T(8,128)(2,1)S(1)}, bf16[2,1024,256]{2,1,0:T(8,128)(2,1)S(1)}, u32[]{:S(2)}, u32[]{:S(2)}) collective-permute-start(bf16[2,1024,256]{2,1,0:T(8,128)(2,1)S(1)} %collective-permute-done.5.refs_0_.rest_10_), channel_id=1, source_target_pairs={{4,0},{5,1},{6,2},{7,3},{8,4},{9,5},{10,6},{11,7},{12,8},{13,9},{1... | collective-permute-start | bytes 3145736 | tf_op jit(solution)/shard_map/ppermute | solution.py:22
  85.9 14.2 %collective-permute-done.18.refs_0_.rest_12_ = bf16[2,1024,256]{2,1,0:T(8,128)(2,1)S(1)} collective-permute-done((bf16[2,1024,256]{2,1,0:T(8,128)(2,1)S(1)}, bf16[2,1024,256]{2,1,0:T(8,128)(2,1)S(1)}, u32[]{:S(2)}, u32[]{:S(2)}) %collective-permute-start.18) | collective-permute-done | bytes 1048608 | tf_op jit(solution)/shard_map/ppermute | solution.py:27
  100.1 2.4 %collective-permute-start.19 = (bf16[2,1024,256]{2,1,0:T(8,128)(2,1)S(1)}, bf16[2,1024,256]{2,1,0:T(8,128)(2,1)S(1)}, u32[]{:S(2)}, u32[]{:S(2)}) collective-permute-start(bf16[2,1024,256]{2,1,0:T(8,128)(2,1)S(1)} %pick.13), channel_id=1, source_target_pairs={{0,1},{1,0},{2,3},{3,2},{4,5},{5,4},{6,7},{7,6},{8,9},{9,8},{10,11... | collective-permute-start | bytes 3145736 | tf_op jit(solution)/shard_map/ppermute | solution.py:27
  104.7 2.1 %collective-permute-start.13 = (f32[32,512]{1,0:T(8,128)S(1)}, f32[32,512]{1,0:T(8,128)S(1)}, u32[]{:S(2)}, u32[]{:S(2)}) collective-permute-start(f32[32,512]{1,0:T(8,128)S(1)} %get-tuple-element.37.pair8), channel_id=1, source_target_pairs={{8,0},{9,1},{10,2},{11,3},{12,4},{13,5},{14,6},{15,7},{24,16},{25,... | collective-permute-start | bytes 196616 | tf_op jit(solution)/shard_map/ppermute | solution.py:22
  106.7 2.1 %collective-permute-start.14 = (f32[32,512]{1,0:T(8,128)S(1)}, f32[32,512]{1,0:T(8,128)S(1)}, u32[]{:S(2)}, u32[]{:S(2)}) collective-permute-start(f32[32,512]{1,0:T(8,128)S(1)} %get-tuple-element.38.pair4), channel_id=1, source_target_pairs={{4,0},{5,1},{6,2},{7,3},{8,4},{9,5},{10,6},{11,7},{12,8},{13,9},{1... | collective-permute-start | bytes 196616 | tf_op jit(solution)/shard_map/ppermute | solution.py:22
  108.9 2.9 %collective-permute-start.15 = (f32[32,512]{1,0:T(8,128)S(1)}, f32[32,512]{1,0:T(8,128)S(1)}, u32[]{:S(2)}, u32[]{:S(2)}) collective-permute-start(f32[32,512]{1,0:T(8,128)S(1)} %get-tuple-element.39.pair2), channel_id=1, source_target_pairs={{2,0},{3,1},{4,2},{5,3},{6,4},{7,5},{8,6},{9,7},{10,8},{11,9},{12,... | collective-permute-start | bytes 196616 | tf_op jit(solution)/shard_map/ppermute | solution.py:22
  111.8 3.9 %collective-permute-start.16 = (f32[32,512]{1,0:T(8,128)S(1)}, f32[32,512]{1,0:T(8,128)S(1)}, u32[]{:S(2)}, u32[]{:S(2)}) collective-permute-start(f32[32,512]{1,0:T(8,128)S(1)} %get-tuple-element.40.pair1), channel_id=1, source_target_pairs={{1,0},{2,1},{3,2},{4,3},{5,4},{6,5},{7,6},{8,7},{9,8},{10,9},{11,1... | collective-permute-start | bytes 196616 | tf_op jit(solution)/shard_map/ppermute | solution.py:22
  115.7 1.3 %query_part.3.rest_9_ = f32[1024,256]{1,0:T(8,128)S(1)} custom-call(bf16[2,1024,256]{2,1,0:T(8,128)(2,1)S(1)} %get-tuple-element.27.refs_0_.rest_0_.own, bf16[2,1024,256]{2,1,0:T(8,128)(2,1)S(1)} %collective-permute-done.3.refs_1_.rest_3_.refs_2_.rest_2_.two_b.two_a, bf16[2,1024,256]{2,1,0:T(8,128)(2,1)S(1)} %collective-permute-done.8.refs_1_.rest_3_.two_b.rest_5_, ...), custom_call_target="tpu_custom_call" | custom-call | tf_op jit(solution)/shard_map/query_part/pallas_call | solution.py:228
  117.1 1.3 %query_part.2.rest_1_ = f32[1024,256]{1,0:T(8,128)S(1)} custom-call(bf16[2,1024,256]{2,1,0:T(8,128)(2,1)S(1)} %get-tuple-element.30.refs_0_.rest_0_.own, bf16[2,1024,256]{2,1,0:T(8,128)(2,1)S(1)} %collective-permute-done.1.refs_2_.rest_2_.refs_0_.two_a.rest_4_, bf16[2,1024,256]{2,1,0:T(8,128)(2,1)S(1)} %collective-permute-done.3.refs_1_.rest_3_.refs_2_.rest_2_.two_b.two_a, ...), custom_call_target="tpu_custom_call" | custom-call | tf_op jit(solution)/shard_map/query_part/pallas_call | solution.py:228
  119.3 5.7 %sums.1 = bf16[512,1024]{1,0:T(8,128)(2,1)} custom-call(f32[32,512]{1,0:T(8,128)S(1)} %get-tuple-element.36.self_pair, f32[32,512]{1,0:T(8,128)S(1)} %collective-permute-done.13.pair8, f32[32,512]{1,0:T(8,128)S(1)} %collective-permute-done.14.pair4, f32[32,512]{1,0:T(8,128)S(1)} %collective-permute-done.15.pair2, ...), custom_call_target="tpu_custom_call" | custom-call | bytes 11070000 | tf_op jit(solution)/shard_map/sums/pallas_call | solution.py:280
  (40 shorter events, 13.1 us)
Async XLA Ops:
  3.0 25.9 %collective-permute-start = (bf16[2,1024,256]{2,1,0:T(8,128)(2,1)S(1)}, bf16[2,1024,256]{2,1,0:T(8,128)(2,1)S(1)}, u32[]{:S(2)}, u32[]{:S(2)}) collective-permute-start(bf16[2,1024,256]{2,1,0:T(8,128)(2,1)S(1)} %get-tuple-element.30.refs_0_.rest_0_.own), channel_id=1, source_target_pairs={{0,4},{1,5},{2,6},{3,7},{4,8},{5,9},{6,10},{7,11},{8,12},{9,13},{1... | collective-permute-start | bytes 3145736 | tf_op jit(solution)/shard_map/ppermute | solution.py:22
  4.3 25.5 %collective-permute-start.2 = (bf16[2,1024,256]{2,1,0:T(8,128)(2,1)S(1)}, bf16[2,1024,256]{2,1,0:T(8,128)(2,1)S(1)}, u32[]{:S(2)}, u32[]{:S(2)}) collective-permute-start(bf16[2,1024,256]{2,1,0:T(8,128)(2,1)S(1)} %get-tuple-element.32.refs_1_.qg.rest_0_), channel_id=1, source_target_pairs={{4,0},{5,1},{6,2},{7,3},{8,4},{9,5},{10,6},{11,7},{12,8},{13,9},{1... | collective-permute-start | bytes 3145736 | tf_op jit(solution)/shard_map/ppermute | solution.py:22
  8.4 23.5 %collective-permute-start.1 = (bf16[2,1024,256]{2,1,0:T(8,128)(2,1)S(1)}, bf16[2,1024,256]{2,1,0:T(8,128)(2,1)S(1)}, u32[]{:S(2)}, u32[]{:S(2)}) collective-permute-start(bf16[2,1024,256]{2,1,0:T(8,128)(2,1)S(1)} %get-tuple-element.26), channel_id=1, source_target_pairs={{0,2},{1,3},{2,0},{3,1},{4,6},{5,7},{6,4},{7,5},{8,10},{9,11},{10,... | collective-permute-start | bytes 3145736 | tf_op jit(solution)/shard_map/ppermute | solution.py:27
  9.7 41.7 %collective-permute-start.4 = (bf16[2,1024,256]{2,1,0:T(8,128)(2,1)S(1)}, bf16[2,1024,256]{2,1,0:T(8,128)(2,1)S(1)}, u32[]{:S(2)}, u32[]{:S(2)}) collective-permute-start(bf16[2,1024,256]{2,1,0:T(8,128)(2,1)S(1)} %get-tuple-element.27.refs_0_.rest_0_.own), channel_id=1, source_target_pairs={{0,4},{1,5},{2,6},{3,7},{4,8},{5,9},{6,10},{7,11},{8,12},{9,13},{1... | collective-permute-start | bytes 3145736 | tf_op jit(solution)/shard_map/ppermute | solution.py:22
  11.0 41.3 %collective-permute-start.5 = (bf16[2,1024,256]{2,1,0:T(8,128)(2,1)S(1)}, bf16[2,1024,256]{2,1,0:T(8,128)(2,1)S(1)}, u32[]{:S(2)}, u32[]{:S(2)}) collective-permute-start(bf16[2,1024,256]{2,1,0:T(8,128)(2,1)S(1)} %get-tuple-element.29.qg.refs_1_.rest_8_), channel_id=1, source_target_pairs={{4,0},{5,1},{6,2},{7,3},{8,4},{9,5},{10,6},{11,7},{12,8},{13,9},{1... | collective-permute-start | bytes 3145736 | tf_op jit(solution)/shard_map/ppermute | solution.py:22
  31.9 25.5 %collective-permute-start.3 = (bf16[2,1024,256]{2,1,0:T(8,128)(2,1)S(1)}, bf16[2,1024,256]{2,1,0:T(8,128)(2,1)S(1)}, u32[]{:S(2)}, u32[]{:S(2)}) collective-permute-start(bf16[2,1024,256]{2,1,0:T(8,128)(2,1)S(1)} %pick.7), channel_id=1, source_target_pairs={{0,2},{1,3},{2,0},{3,1},{4,6},{5,7},{6,4},{7,5},{8,10},{9,11},{10,... | collective-permute-start | bytes 3145736 | tf_op jit(solution)/shard_map/ppermute | solution.py:27
  33.1 41.6 %collective-permute-start.9 = (bf16[2,1024,256]{2,1,0:T(8,128)(2,1)S(1)}, bf16[2,1024,256]{2,1,0:T(8,128)(2,1)S(1)}, u32[]{:S(2)}, u32[]{:S(2)}) collective-permute-start(bf16[2,1024,256]{2,1,0:T(8,128)(2,1)S(1)} %collective-permute-done.2.refs_0_.rest_2_), channel_id=1, source_target_pairs={{4,0},{5,1},{6,2},{7,3},{8,4},{9,5},{10,6},{11,7},{12,8},{13,9},{1... | collective-permute-start | bytes 3145736 | tf_op jit(solution)/shard_map/ppermute | solution.py:22
  35.2 39.5 %collective-permute-start.10 = (bf16[2,1024,256]{2,1,0:T(8,128)(2,1)S(1)}, bf16[2,1024,256]{2,1,0:T(8,128)(2,1)S(1)}, u32[]{:S(2)}, u32[]{:S(2)}) collective-permute-start(bf16[2,1024,256]{2,1,0:T(8,128)(2,1)S(1)} %collective-permute-done.refs_1_.rest_1_.far4), channel_id=1, source_target_pairs={{0,4},{1,5},{2,6},{3,7},{4,8},{5,9},{6,10},{7,11},{8,12},{9,13},{1... | collective-permute-start | bytes 3145736 | tf_op jit(solution)/shard_map/ppermute | solution.py:22
  52.4 25.2 %collective-permute-start.8 = (bf16[2,1024,256]{2,1,0:T(8,128)(2,1)S(1)}, bf16[2,1024,256]{2,1,0:T(8,128)(2,1)S(1)}, u32[]{:S(2)}, u32[]{:S(2)}) collective-permute-start(bf16[2,1024,256]{2,1,0:T(8,128)(2,1)S(1)} %pick.10), channel_id=1, source_target_pairs={{0,2},{1,3},{2,0},{3,1},{4,6},{5,7},{6,4},{7,5},{8,10},{9,11},{10,... | collective-permute-start | bytes 3145736 | tf_op jit(solution)/shard_map/ppermute | solution.py:27
  53.7 24.2 %collective-permute-start.6 = (bf16[2,1024,256]{2,1,0:T(8,128)(2,1)S(1)}, bf16[2,1024,256]{2,1,0:T(8,128)(2,1)S(1)}, u32[]{:S(2)}, u32[]{:S(2)}) collective-permute-start(bf16[2,1024,256]{2,1,0:T(8,128)(2,1)S(1)} %pick.8), channel_id=1, source_target_pairs={{0,1},{1,0},{2,3},{3,2},{4,5},{5,4},{6,7},{7,6},{8,9},{9,8},{10,11... | collective-permute-start | bytes 3145736 | tf_op jit(solution)/shard_map/ppermute | solution.py:27
  57.5 20.5 %collective-permute-start.7 = (bf16[2,1024,256]{2,1,0:T(8,128)(2,1)S(1)}, bf16[2,1024,256]{2,1,0:T(8,128)(2,1)S(1)}, u32[]{:S(2)}, u32[]{:S(2)}) collective-permute-start(bf16[2,1024,256]{2,1,0:T(8,128)(2,1)S(1)} %pick.9), channel_id=1, source_target_pairs={{0,1},{1,0},{2,3},{3,2},{4,5},{5,4},{6,7},{7,6},{8,9},{9,8},{10,11... | collective-permute-start | bytes 3145736 | tf_op jit(solution)/shard_map/ppermute | solution.py:27
  74.8 25.3 %collective-permute-start.18 = (bf16[2,1024,256]{2,1,0:T(8,128)(2,1)S(1)}, bf16[2,1024,256]{2,1,0:T(8,128)(2,1)S(1)}, u32[]{:S(2)}, u32[]{:S(2)}) collective-permute-start(bf16[2,1024,256]{2,1,0:T(8,128)(2,1)S(1)} %pick.12), channel_id=1, source_target_pairs={{0,2},{1,3},{2,0},{3,1},{4,6},{5,7},{6,4},{7,5},{8,10},{9,11},{10,... | collective-permute-start | bytes 3145736 | tf_op jit(solution)/shard_map/ppermute | solution.py:27
  76.0 26.5 %collective-permute-start.12 = (bf16[2,1024,256]{2,1,0:T(8,128)(2,1)S(1)}, bf16[2,1024,256]{2,1,0:T(8,128)(2,1)S(1)}, u32[]{:S(2)}, u32[]{:S(2)}) collective-permute-start(bf16[2,1024,256]{2,1,0:T(8,128)(2,1)S(1)} %collective-permute-done.4.refs_1_.rest_1_.far4), channel_id=1, source_target_pairs={{0,4},{1,5},{2,6},{3,7},{4,8},{5,9},{6,10},{7,11},{8,12},{9,13},{1... | collective-permute-start | bytes 3145736 | tf_op jit(solution)/shard_map/ppermute | solution.py:22
  79.1 23.8 %collective-permute-start.11 = (bf16[2,1024,256]{2,1,0:T(8,128)(2,1)S(1)}, bf16[2,1024,256]{2,1,0:T(8,128)(2,1)S(1)}, u32[]{:S(2)}, u32[]{:S(2)}) collective-permute-start(bf16[2,1024,256]{2,1,0:T(8,128)(2,1)S(1)} %pick.11), channel_id=1, source_target_pairs={{0,1},{1,0},{2,3},{3,2},{4,5},{5,4},{6,7},{7,6},{8,9},{9,8},{10,11... | collective-permute-start | bytes 3145736 | tf_op jit(solution)/shard_map/ppermute | solution.py:27
  83.5 28.3 %collective-permute-start.17 = (bf16[2,1024,256]{2,1,0:T(8,128)(2,1)S(1)}, bf16[2,1024,256]{2,1,0:T(8,128)(2,1)S(1)}, u32[]{:S(2)}, u32[]{:S(2)}) collective-permute-start(bf16[2,1024,256]{2,1,0:T(8,128)(2,1)S(1)} %collective-permute-done.5.refs_0_.rest_10_), channel_id=1, source_target_pairs={{4,0},{5,1},{6,2},{7,3},{8,4},{9,5},{10,6},{11,7},{12,8},{13,9},{1... | collective-permute-start | bytes 3145736 | tf_op jit(solution)/shard_map/ppermute | solution.py:22
  100.1 18.3 %collective-permute-start.19 = (bf16[2,1024,256]{2,1,0:T(8,128)(2,1)S(1)}, bf16[2,1024,256]{2,1,0:T(8,128)(2,1)S(1)}, u32[]{:S(2)}, u32[]{:S(2)}) collective-permute-start(bf16[2,1024,256]{2,1,0:T(8,128)(2,1)S(1)} %pick.13), channel_id=1, source_target_pairs={{0,1},{1,0},{2,3},{3,2},{4,5},{5,4},{6,7},{7,6},{8,9},{9,8},{10,11... | collective-permute-start | bytes 3145736 | tf_op jit(solution)/shard_map/ppermute | solution.py:27
  102.8 1.2 copy-start.3
  102.9 12.8 %copy-start = (bf16[1024,1024]{1,0:T(8,128)(2,1)S(1)}, bf16[1024,1024]{1,0:T(8,128)(2,1)}, u32[]{:S(2)}) copy-start(bf16[1024,1024]{1,0:T(8,128)(2,1)} %w_query.3) | copy-start | bytes 6291460
  104.7 13.7 %collective-permute-start.13 = (f32[32,512]{1,0:T(8,128)S(1)}, f32[32,512]{1,0:T(8,128)S(1)}, u32[]{:S(2)}, u32[]{:S(2)}) collective-permute-start(f32[32,512]{1,0:T(8,128)S(1)} %get-tuple-element.37.pair8), channel_id=1, source_target_pairs={{8,0},{9,1},{10,2},{11,3},{12,4},{13,5},{14,6},{15,7},{24,16},{25,... | collective-permute-start | bytes 196616 | tf_op jit(solution)/shard_map/ppermute | solution.py:22
  106.7 11.7 %collective-permute-start.14 = (f32[32,512]{1,0:T(8,128)S(1)}, f32[32,512]{1,0:T(8,128)S(1)}, u32[]{:S(2)}, u32[]{:S(2)}) collective-permute-start(f32[32,512]{1,0:T(8,128)S(1)} %get-tuple-element.38.pair4), channel_id=1, source_target_pairs={{4,0},{5,1},{6,2},{7,3},{8,4},{9,5},{10,6},{11,7},{12,8},{13,9},{1... | collective-permute-start | bytes 196616 | tf_op jit(solution)/shard_map/ppermute | solution.py:22
  108.9 9.5 %collective-permute-start.15 = (f32[32,512]{1,0:T(8,128)S(1)}, f32[32,512]{1,0:T(8,128)S(1)}, u32[]{:S(2)}, u32[]{:S(2)}) collective-permute-start(f32[32,512]{1,0:T(8,128)S(1)} %get-tuple-element.39.pair2), channel_id=1, source_target_pairs={{2,0},{3,1},{4,2},{5,3},{6,4},{7,5},{8,6},{9,7},{10,8},{11,9},{12,... | collective-permute-start | bytes 196616 | tf_op jit(solution)/shard_map/ppermute | solution.py:22
  111.8 6.9 %collective-permute-start.16 = (f32[32,512]{1,0:T(8,128)S(1)}, f32[32,512]{1,0:T(8,128)S(1)}, u32[]{:S(2)}, u32[]{:S(2)}) collective-permute-start(f32[32,512]{1,0:T(8,128)S(1)} %get-tuple-element.40.pair1), channel_id=1, source_target_pairs={{1,0},{2,1},{3,2},{4,3},{5,4},{6,5},{7,6},{8,7},{9,8},{10,9},{11,1... | collective-permute-start | bytes 196616 | tf_op jit(solution)/shard_map/ppermute | solution.py:22
  117.0 1.7 %copy-start.1 = (bf16[1024,1024]{1,0:T(8,128)(2,1)S(1)}, bf16[1024,1024]{1,0:T(8,128)(2,1)}, u32[]{:S(2)}) copy-start(bf16[1024,1024]{1,0:T(8,128)(2,1)} %w_key.1) | copy-start | bytes 6291460
  117.0 2.2 %copy-start.2 = (bf16[1024,1024]{1,0:T(8,128)(2,1)S(1)}, bf16[1024,1024]{1,0:T(8,128)(2,1)}, u32[]{:S(2)}) copy-start(bf16[1024,1024]{1,0:T(8,128)(2,1)} %w_value.1) | copy-start | bytes 6291460

commit v6 on v5

--- a/solution.py
+++ b/solution.py
@@ -13,6 +13,7 @@
 SUBLANES = 8
 PIECE = 256
 US = 3.69e6
+US_FLOPS = 1.15e9
 BY_BIT0, BY_BIT1 = (0, 1, 0, 1), (0, 0, 1, 1)
 VMEM_BYTES = 32 * 2**20
 
@@ -43,38 +44,36 @@
     return lax.optimization_barrier((block, *done))[0] if done else block
 
 
-def pack(queries, keys, values, grad_out):
-    _, patches, width = queries.shape
-    half = patches // 2
-
-    def kernel(q_hbm, k_hbm, v_hbm, g_hbm, kv0, kv1, qg0, qg1, y_out, q_ref, k_ref, v_ref, g_ref, sems):
+def pack(queries, keys, values, grad_out, start, rows, with_owed):
+    width = queries.shape[2]
+
+    def kernel(q_hbm, k_hbm, v_hbm, g_hbm, kv_out, qg_out, *rest):
+        owed, (q_ref, k_ref, v_ref, g_ref, sems) = rest[:-5], rest[-5:]
         pieces = []
-        for i in range(2):
-            rows = pl.ds(i * half, half)
-            for part, up, down in ((0, (k_hbm, k_ref), (q_hbm, q_ref)), (1, (v_hbm, v_ref), (g_hbm, g_ref))):
-                for (hbm, ref), out, bit in ((up, (kv0, kv1)[i], 0), (down, (qg0, qg1)[i], 1)):
-                    copy = pltpu.make_async_copy(hbm.at[0, rows, :], ref.at[rows, :], sems.at[len(pieces)])
-                    pieces.append((copy, ref, i * half, out, part, bit))
+        for part, up, down in ((0, (k_hbm, k_ref), (q_hbm, q_ref)), (1, (v_hbm, v_ref), (g_hbm, g_ref))):
+            for (hbm, ref), out, bit in ((up, kv_out, 0), (down, qg_out, 1)):
+                copy = pltpu.make_async_copy(hbm.at[0, pl.ds(start, rows), :], ref, sems.at[len(pieces)])
+                pieces.append((copy, ref, out, part, bit))
         for piece in pieces:
             piece[0].start()
-        for copy, ref, start, out, part, bit in pieces:
+        for copy, ref, out, part, bit in pieces:
             copy.wait()
-            for p in range(0, half, LANES):
-                turned = ref[start + p:start + p + LANES, :].T
+            for p in range(0, rows, LANES):
+                turned = ref[p:p + LANES, :].T
                 out[part, :, p:p + LANES] = turned
-
-                if start == 0:
+                for y_out in owed:
                     @pl.when(place_bit(1) == bit)
                     def _():
                         y_out[part, :, p:p + LANES] = turned
 
-    half_shape = jax.ShapeDtypeStruct((2, width, half), jnp.bfloat16)
+    shape = jax.ShapeDtypeStruct((2, width, rows), jnp.bfloat16)
+    n_out = 3 if with_owed else 2
     return pl.pallas_call(
         kernel,
         in_specs=[pl.BlockSpec(memory_space=pl.ANY)] * 4,
-        out_specs=[VMEM] * 5,
-        out_shape=[half_shape] * 5,
-        scratch_shapes=[pltpu.VMEM((patches, width), jnp.bfloat16)] * 4 + [pltpu.SemaphoreType.DMA((8,))],
+        out_specs=[VMEM] * n_out,
+        out_shape=[shape] * n_out,
+        scratch_shapes=[pltpu.VMEM((rows, width), jnp.bfloat16)] * 4 + [pltpu.SemaphoreType.DMA((4,))],
         compiler_params=params(),
         name="pack",
     )(*(pltpu.with_memory_space_constraint(a, pltpu.HBM) for a in (queries, keys, values, grad_out)))
@@ -97,7 +96,7 @@
         out_specs=VMEM,
         out_shape=jax.ShapeDtypeStruct(blocks[0].shape, blocks[0].dtype),
         compiler_params=params(),
-        cost_estimate=pl.CostEstimate(flops=0, bytes_accessed=int(weight * US), transcendentals=0),
+        cost_estimate=pl.CostEstimate(flops=int(weight * US_FLOPS), bytes_accessed=int(weight * US), transcendentals=0),
         name="pick",
     )(*blocks)
 
@@ -169,7 +168,7 @@
         out_shape=jax.ShapeDtypeStruct((2, slots, HEADS, rows), jnp.float32),
         scratch_shapes=[pltpu.VMEM((slots, HEADS * SUBLANES, LANES), jnp.float32)],
         compiler_params=params(),
-        cost_estimate=pl.CostEstimate(flops=0, bytes_accessed=int(weight * US), transcendentals=0),
+        cost_estimate=pl.CostEstimate(flops=int(weight * US_FLOPS), bytes_accessed=int(weight * US), transcendentals=0),
         name="products",
     )(qg, *others, *two, *one)
 
@@ -201,7 +200,7 @@
         out_specs=[VMEM] * 5,
         out_shape=[pair] * 5,
         compiler_params=params(),
-        cost_estimate=pl.CostEstimate(flops=0, bytes_accessed=int(weight * US), transcendentals=0),
+        cost_estimate=pl.CostEstimate(flops=int(weight * US_FLOPS), bytes_accessed=int(weight * US), transcendentals=0),
         name="scores",
     )(links, near0, near1, far0, far1)
 
@@ -232,7 +231,7 @@
         out_shape=jax.ShapeDtypeStruct((w_query.shape[0], rows), jnp.float32),
         scratch_shapes=[pltpu.VMEM((width, rows), jnp.bfloat16)],
         compiler_params=params(),
-        cost_estimate=pl.CostEstimate(flops=0, bytes_accessed=int(weight * US), transcendentals=0),
+        cost_estimate=pl.CostEstimate(flops=int(weight * US_FLOPS), bytes_accessed=int(weight * US), transcendentals=0),
         name="query_part",
     )(own, *two, *one, far4, far8, *pairs, w_query)
 
@@ -285,7 +284,7 @@
         scratch_shapes=[pltpu.VMEM((width, 2 * rows), jnp.bfloat16)] * 2
         + [pltpu.VMEM((2 * rows, width), jnp.bfloat16), pltpu.SemaphoreType.DMA((2,))],
         compiler_params=params(),
-        cost_estimate=pl.CostEstimate(flops=0, bytes_accessed=int(weight * US), transcendentals=0),
+        cost_estimate=pl.CostEstimate(flops=int(weight * US_FLOPS), bytes_accessed=int(weight * US), transcendentals=0),
         name="sums",
     )(*operands)
 
@@ -294,7 +293,8 @@
     patches = queries.shape[1]
     half = patches // 2
     head_size = keys.shape[2] // HEADS
-    kv0, kv1, qg0, qg1, owed = pack(queries, keys, values, grad_out)
+    kv0, qg0, owed = pack(queries, keys, values, grad_out, 0, half, True)
+    kv1, qg1 = pack(after(queries, kv0), keys, values, grad_out, half, half, False)
     up4_0 = shift(kv0, 4)
     down4_0 = shift(qg0, -4)
     y_a = swap(owed, 2)
@@ -304,17 +304,17 @@
     up8_0 = shift(after(up4_0, down4_0), 4)
     down8_0 = shift(after(down4_0, up4_0), -4)
     c_a = swap(pick((after(kv0, up4_1, down4_1), qg0), BY_BIT0, 2.8), 1)
-    y_c = swap(pick((down4_0, up4_1), BY_BIT1, 0), 2)
+    y_c = swap(pick((down4_0, up4_1), BY_BIT1, 3), 2)
     up8_1 = shift(after(up4_1, y_b), 4)
     down8_1 = shift(after(down4_1, up8_0, down8_0), -4)
     c_b = swap(pick((kv1, y_b, y_a), (0, 1, 0, 2), 0), 1)
+    near0 = products_of(qg0, [kv0, up4_0], (y_a, y_b), (c_a, c_b), 4)
     far0 = products_of(after(qg0, down8_0), [up8_0], (), (), 5.7)
-    near0 = products_of(qg0, [kv0, up4_0], (y_a, y_b), (c_a, c_b), 0)
-    y_d = swap(after(pick((down4_1, qg1), BY_BIT1, 0), up8_0, down8_0), 2)
     c_c = swap(after(pick((y_a, y_c, y_b), (0, 1, 1, 2), 0), near0, far0), 1)
     near1 = products_of(qg1, [kv1, up4_1], (y_b, y_c), (c_b, c_c), 0)
-    far1 = products_of(qg1, [up8_1], (), (), 10)
-    pairs = scores_of(links, near0, near1, far0, far1, head_size, 0)
+    y_d = swap(after(pick((down4_1, qg1), BY_BIT1, 0), up8_0, down8_0), 2)
+    far1 = products_of(after(qg1, c_b), [up8_1], (), (), 10)
+    pairs = scores_of(links, after(near0, down8_0), near1, far0, far1, head_size, 0)
     self_pair, pair1, pair2, pair4, pair8 = pairs
     came8 = shift(pair8, -8)
     came4 = shift(pair4, -4)

time: 126 us -> 125 us (level)
  waiting for transfers between devices: 62.5 us -> 59.7 us
    ppermute x12, waiting for transfers between devices: 46 us -> 42.3 us  [shift(): lax.ppermute(block, 'frame', [(i, i + distance) for i in range(n) if 0 <=...]
    ppermute x12, starting transfers between devices: 28.7 us -> 31.2 us  [shift(): lax.ppermute(block, 'frame', [(i, i + distance) for i in range(n) if 0 <=...]
    ppermute x8, starting transfers between devices: 17.5 us -> 16 us  [swap(): return lax.ppermute(block, 'frame', [(i, i ^ bit) for i in range(n)])]
    pallas_call x1 -> x2, Pallas kernels: 3.02 us -> 4.06 us  [pack(): pl.pallas_call(kernel, in_specs=[pl.BlockSpec(memory_space=pl.ANY)] * 4,...]
  transfers between devices with their start and end apart: 20 -> 20, of which waited for: 9 -> 8; matrix products, arithmetic and copies ran while one was open for 0% -> 0% of each run, Pallas kernels for 5% -> 7%
where the time goes in v6:
time: 125 us; the launch traced here: 124 us
  waiting for transfers between devices  59.7 us (48%)
  starting transfers between devices  47.1 us (38%)
  Pallas kernels  16.4 us (13%)
    ppermute x12, waiting for transfers between devices, shift(): lax.ppermute(block, 'frame', [(i, i + distance) for i in range(n) if 0 <=...  42.3 us
    ppermute x12, starting transfers between devices, shift(): lax.ppermute(block, 'frame', [(i, i + distance) for i in range(n) if 0 <=...  31.2 us
    ppermute x8, waiting for transfers between devices, swap(): return lax.ppermute(block, 'frame', [(i, i ^ bit) for i in range(n)])  17.5 us
    ppermute x8, starting transfers between devices, swap(): return lax.ppermute(block, 'frame', [(i, i ^ bit) for i in range(n)])  16 us
    pallas_call x1, Pallas kernels, sums_of(): pl.pallas_call(functools.partial(sum_kernel, [(len(h[2]), len(h[3])) for...  5.71 us
    pallas_call x2, Pallas kernels, pack(): pl.pallas_call(kernel, in_specs=[pl.BlockSpec(memory_space=pl.ANY)] * 4,...  4.06 us
    pallas_call x4, Pallas kernels, products_of(): pl.pallas_call(functools.partial(product_kernel, len(two), len(one), len(...  2.87 us
    pallas_call x2, Pallas kernels, query_part_of(): pl.pallas_call(functools.partial(query_kernel, start), in_specs=[VMEM] *...  2.65 us
  transfers between devices with their start and end apart: 20, of which 8 were waited for; matrix products, arithmetic and copies ran while one was open for 0% of the time, Pallas kernels for 7%

profile of v6, /device:TPU:27, one launch (start us, length us, event | category | flops | bytes accessed | tf_op | source)
XLA Modules:
  0.0 124.3 jit_solution(4719101295716428335)
XLA Ops:
  0.0 2.2 %pack.2 = (bf16[2,1024,256]{2,1,0:T(8,128)(2,1)S(1)}, bf16[2,1024,256]{2,1,0:T(8,128)(2,1)S(1)}, bf16[2,1024,256]{2,1,0:T(8,128)(2,1)S(1)}) custom-call(bf16[1,512,1024]{2,1,0:T(8,128)(2,1)} %q_hbm.2, bf16[1,512,1024]{2,1,0:T(8,128)(2,1)} %k_hbm.3, bf16[1,512,1024]{2,1,0:T(8,128)(2,1)} %v_hbm.3, bf16[1,512,1024]{2,1,0:T(8,128)(2,1)} %g_hbm.3), custom_call_target="tpu_custom_call" | custom-call | tf_op jit(solution)/shard_map/pack/pallas_call | solution.py:71
  3.5 4.1 %collective-permute-start.2 = (bf16[2,1024,256]{2,1,0:T(8,128)(2,1)S(1)}, bf16[2,1024,256]{2,1,0:T(8,128)(2,1)S(1)}, u32[]{:S(2)}, u32[]{:S(2)}) collective-permute-start(bf16[2,1024,256]{2,1,0:T(8,128)(2,1)S(1)} %get-tuple-element.37.refs_1_.qg.rest_0_), channel_id=1, source_target_pairs={{4,0},{5,1},{6,2},{7,3},{8,4},{9,5},{10,6},{11,7},{12,8},{13,9},{1... | collective-permute-start | bytes 3145736 | tf_op jit(solution)/shard_map/ppermute | solution.py:23
  7.6 1.3 %collective-permute-start.1 = (bf16[2,1024,256]{2,1,0:T(8,128)(2,1)S(1)}, bf16[2,1024,256]{2,1,0:T(8,128)(2,1)S(1)}, u32[]{:S(2)}, u32[]{:S(2)}) collective-permute-start(bf16[2,1024,256]{2,1,0:T(8,128)(2,1)S(1)} %get-tuple-element.29), channel_id=1, source_target_pairs={{0,2},{1,3},{2,0},{3,1},{4,6},{5,7},{6,4},{7,5},{8,10},{9,11},{10,... | collective-permute-start | bytes 3145736 | tf_op jit(solution)/shard_map/ppermute | solution.py:28
  8.9 1.8 %pack.3 = (bf16[2,1024,256]{2,1,0:T(8,128)(2,1)S(1)}, bf16[2,1024,256]{2,1,0:T(8,128)(2,1)S(1)}) custom-call(bf16[1,512,1024]{2,1,0:T(8,128)(2,1)} %q_hbm.2, bf16[1,512,1024]{2,1,0:T(8,128)(2,1)} %k_hbm.3, bf16[1,512,1024]{2,1,0:T(8,128)(2,1)} %v_hbm.3, bf16[1,512,1024]{2,1,0:T(8,128)(2,1)} %g_hbm.3), custom_call_target="tpu_custom_call" | custom-call | tf_op jit(solution)/shard_map/pack/pallas_call | solution.py:71
  12.0 4.1 %collective-permute-start.5 = (bf16[2,1024,256]{2,1,0:T(8,128)(2,1)S(1)}, bf16[2,1024,256]{2,1,0:T(8,128)(2,1)S(1)}, u32[]{:S(2)}, u32[]{:S(2)}) collective-permute-start(bf16[2,1024,256]{2,1,0:T(8,128)(2,1)S(1)} %get-tuple-element.40.qg.refs_1_.rest_8_), channel_id=1, source_target_pairs={{4,0},{5,1},{6,2},{7,3},{8,4},{9,5},{10,6},{11,7},{12,8},{13,9},{1... | collective-permute-start | bytes 3145736 | tf_op jit(solution)/shard_map/ppermute | solution.py:23
  16.1 12.0 %collective-permute-done.refs_1_.rest_1_.far4 = bf16[2,1024,256]{2,1,0:T(8,128)(2,1)S(1)} collective-permute-done((bf16[2,1024,256]{2,1,0:T(8,128)(2,1)S(1)}, bf16[2,1024,256]{2,1,0:T(8,128)(2,1)S(1)}, u32[]{:S(2)}, u32[]{:S(2)}) %collective-permute-start) | collective-permute-done | bytes 1048608 | tf_op jit(solution)/shard_map/ppermute | solution.py:23
  29.0 2.1 %collective-permute-done.1.refs_2_.rest_2_.refs_0_.two_a.rest_4_ = bf16[2,1024,256]{2,1,0:T(8,128)(2,1)S(1)} collective-permute-done((bf16[2,1024,256]{2,1,0:T(8,128)(2,1)S(1)}, bf16[2,1024,256]{2,1,0:T(8,128)(2,1)S(1)}, u32[]{:S(2)}, u32[]{:S(2)}) %collective-permute-start.1) | collective-permute-done | bytes 1048608 | tf_op jit(solution)/shard_map/ppermute | solution.py:28
  32.3 2.1 %collective-permute-start.8 = (bf16[2,1024,256]{2,1,0:T(8,128)(2,1)S(1)}, bf16[2,1024,256]{2,1,0:T(8,128)(2,1)S(1)}, u32[]{:S(2)}, u32[]{:S(2)}) collective-permute-start(bf16[2,1024,256]{2,1,0:T(8,128)(2,1)S(1)} %collective-permute-done.2.refs_0_.rest_2_), channel_id=1, source_target_pairs={{4,0},{5,1},{6,2},{7,3},{8,4},{9,5},{10,6},{11,7},{12,8},{13,9},{1... | collective-permute-start | bytes 3145736 | tf_op jit(solution)/shard_map/ppermute | solution.py:23
  35.7 14.9 %collective-permute-done.4.refs_1_.rest_1_.far4 = bf16[2,1024,256]{2,1,0:T(8,128)(2,1)S(1)} collective-permute-done((bf16[2,1024,256]{2,1,0:T(8,128)(2,1)S(1)}, bf16[2,1024,256]{2,1,0:T(8,128)(2,1)S(1)}, u32[]{:S(2)}, u32[]{:S(2)}) %collective-permute-start.4) | collective-permute-done | bytes 1048608 | tf_op jit(solution)/shard_map/ppermute | solution.py:23
  50.7 1.3 %collective-permute-start.9 = (bf16[2,1024,256]{2,1,0:T(8,128)(2,1)S(1)}, bf16[2,1024,256]{2,1,0:T(8,128)(2,1)S(1)}, u32[]{:S(2)}, u32[]{:S(2)}) collective-permute-start(bf16[2,1024,256]{2,1,0:T(8,128)(2,1)S(1)} %pick.10), channel_id=1, source_target_pairs={{0,2},{1,3},{2,0},{3,1},{4,6},{5,7},{6,4},{7,5},{8,10},{9,11},{10,... | collective-permute-start | bytes 3145736 | tf_op jit(solution)/shard_map/ppermute | solution.py:28
  52.0 1.6 %collective-permute-done.3.refs_1_.rest_3_.refs_2_.rest_2_.two_b.two_a = bf16[2,1024,256]{2,1,0:T(8,128)(2,1)S(1)} collective-permute-done((bf16[2,1024,256]{2,1,0:T(8,128)(2,1)S(1)}, bf16[2,1024,256]{2,1,0:T(8,128)(2,1)S(1)}, u32[]{:S(2)}, u32[]{:S(2)}) %collective-permute-start.3) | collective-permute-done | bytes 1048608 | tf_op jit(solution)/shard_map/ppermute | solution.py:28
  53.6 5.8 %collective-permute-start.7 = (bf16[2,1024,256]{2,1,0:T(8,128)(2,1)S(1)}, bf16[2,1024,256]{2,1,0:T(8,128)(2,1)S(1)}, u32[]{:S(2)}, u32[]{:S(2)}) collective-permute-start(bf16[2,1024,256]{2,1,0:T(8,128)(2,1)S(1)} %pick.9), channel_id=1, source_target_pairs={{0,1},{1,0},{2,3},{3,2},{4,5},{5,4},{6,7},{7,6},{8,9},{9,8},{10,11... | collective-permute-start | bytes 3145736 | tf_op jit(solution)/shard_map/ppermute | solution.py:28
  59.7 14.2 %collective-permute-done.8.rest_3_ = bf16[2,1024,256]{2,1,0:T(8,128)(2,1)S(1)} collective-permute-done((bf16[2,1024,256]{2,1,0:T(8,128)(2,1)S(1)}, bf16[2,1024,256]{2,1,0:T(8,128)(2,1)S(1)}, u32[]{:S(2)}, u32[]{:S(2)}) %collective-permute-start.8) | collective-permute-done | bytes 1048608 | tf_op jit(solution)/shard_map/ppermute | solution.py:23
  76.5 4.8 %collective-permute-start.17 = (bf16[2,1024,256]{2,1,0:T(8,128)(2,1)S(1)}, bf16[2,1024,256]{2,1,0:T(8,128)(2,1)S(1)}, u32[]{:S(2)}, u32[]{:S(2)}) collective-permute-start(bf16[2,1024,256]{2,1,0:T(8,128)(2,1)S(1)} %collective-permute-done.5.refs_0_.rest_10_), channel_id=1, source_target_pairs={{4,0},{5,1},{6,2},{7,3},{8,4},{9,5},{10,6},{11,7},{12,8},{13,9},{1... | collective-permute-start | bytes 3145736 | tf_op jit(solution)/shard_map/ppermute | solution.py:23
  82.9 2.5 %collective-permute-start.11 = (bf16[2,1024,256]{2,1,0:T(8,128)(2,1)S(1)}, bf16[2,1024,256]{2,1,0:T(8,128)(2,1)S(1)}, u32[]{:S(2)}, u32[]{:S(2)}) collective-permute-start(bf16[2,1024,256]{2,1,0:T(8,128)(2,1)S(1)} %pick.11), channel_id=1, source_target_pairs={{0,1},{1,0},{2,3},{3,2},{4,5},{5,4},{6,7},{7,6},{8,9},{9,8},{10,11... | collective-permute-start | bytes 3145736 | tf_op jit(solution)/shard_map/ppermute | solution.py:28
  85.4 13.8 %collective-permute-done.18.refs_0_.rest_12_ = bf16[2,1024,256]{2,1,0:T(8,128)(2,1)S(1)} collective-permute-done((bf16[2,1024,256]{2,1,0:T(8,128)(2,1)S(1)}, bf16[2,1024,256]{2,1,0:T(8,128)(2,1)S(1)}, u32[]{:S(2)}, u32[]{:S(2)}) %collective-permute-start.18) | collective-permute-done | bytes 1048608 | tf_op jit(solution)/shard_map/ppermute | solution.py:28
  99.3 2.5 %collective-permute-start.19 = (bf16[2,1024,256]{2,1,0:T(8,128)(2,1)S(1)}, bf16[2,1024,256]{2,1,0:T(8,128)(2,1)S(1)}, u32[]{:S(2)}, u32[]{:S(2)}) collective-permute-start(bf16[2,1024,256]{2,1,0:T(8,128)(2,1)S(1)} %pick.13), channel_id=1, source_target_pairs={{0,1},{1,0},{2,3},{3,2},{4,5},{5,4},{6,7},{7,6},{8,9},{9,8},{10,11... | collective-permute-start | bytes 3145736 | tf_op jit(solution)/shard_map/ppermute | solution.py:28
  103.9 2.0 %collective-permute-start.13 = (f32[32,512]{1,0:T(8,128)S(1)}, f32[32,512]{1,0:T(8,128)S(1)}, u32[]{:S(2)}, u32[]{:S(2)}) collective-permute-start(f32[32,512]{1,0:T(8,128)S(1)} %get-tuple-element.43.pair8), channel_id=1, source_target_pairs={{8,0},{9,1},{10,2},{11,3},{12,4},{13,5},{14,6},{15,7},{24,16},{25,... | collective-permute-start | bytes 196616 | tf_op jit(solution)/shard_map/ppermute | solution.py:23
  105.8 2.1 %collective-permute-start.14 = (f32[32,512]{1,0:T(8,128)S(1)}, f32[32,512]{1,0:T(8,128)S(1)}, u32[]{:S(2)}, u32[]{:S(2)}) collective-permute-start(f32[32,512]{1,0:T(8,128)S(1)} %get-tuple-element.44.pair4), channel_id=1, source_target_pairs={{4,0},{5,1},{6,2},{7,3},{8,4},{9,5},{10,6},{11,7},{12,8},{13,9},{1... | collective-permute-start | bytes 196616 | tf_op jit(solution)/shard_map/ppermute | solution.py:23
  108.0 2.9 %collective-permute-start.15 = (f32[32,512]{1,0:T(8,128)S(1)}, f32[32,512]{1,0:T(8,128)S(1)}, u32[]{:S(2)}, u32[]{:S(2)}) collective-permute-start(f32[32,512]{1,0:T(8,128)S(1)} %get-tuple-element.45.pair2), channel_id=1, source_target_pairs={{2,0},{3,1},{4,2},{5,3},{6,4},{7,5},{8,6},{9,7},{10,8},{11,9},{12,... | collective-permute-start | bytes 196616 | tf_op jit(solution)/shard_map/ppermute | solution.py:23
  110.8 4.0 %collective-permute-start.16 = (f32[32,512]{1,0:T(8,128)S(1)}, f32[32,512]{1,0:T(8,128)S(1)}, u32[]{:S(2)}, u32[]{:S(2)}) collective-permute-start(f32[32,512]{1,0:T(8,128)S(1)} %get-tuple-element.46.pair1), channel_id=1, source_target_pairs={{1,0},{2,1},{3,2},{4,3},{5,4},{6,5},{7,6},{8,7},{9,8},{10,9},{11,1... | collective-permute-start | bytes 196616 | tf_op jit(solution)/shard_map/ppermute | solution.py:23
  114.9 1.3 %query_part.3.rest_9_ = f32[1024,256]{1,0:T(8,128)S(1)} custom-call(bf16[2,1024,256]{2,1,0:T(8,128)(2,1)S(1)} %get-tuple-element.31.refs_0_.rest_0_.own, bf16[2,1024,256]{2,1,0:T(8,128)(2,1)S(1)} %collective-permute-done.3.refs_1_.rest_3_.refs_2_.rest_2_.two_b.two_a, bf16[2,1024,256]{2,1,0:T(8,128)(2,1)S(1)} %collective-permute-done.9.refs_1_.rest_3_.two_b.rest_5_, ...), custom_call_target="tpu_custom_call" | custom-call | tf_op jit(solution)/shard_map/query_part/pallas_call | solution.py:227
  116.3 1.3 %query_part.2.rest_1_ = f32[1024,256]{1,0:T(8,128)S(1)} custom-call(bf16[2,1024,256]{2,1,0:T(8,128)(2,1)S(1)} %get-tuple-element.34.refs_0_.rest_0_.own, bf16[2,1024,256]{2,1,0:T(8,128)(2,1)S(1)} %collective-permute-done.1.refs_2_.rest_2_.refs_0_.two_a.rest_4_, bf16[2,1024,256]{2,1,0:T(8,128)(2,1)S(1)} %collective-permute-done.3.refs_1_.rest_3_.refs_2_.rest_2_.two_b.two_a, ...), custom_call_target="tpu_custom_call" | custom-call | tf_op jit(solution)/shard_map/query_part/pallas_call | solution.py:227
  118.5 5.7 %sums.1 = bf16[512,1024]{1,0:T(8,128)(2,1)} custom-call(f32[32,512]{1,0:T(8,128)S(1)} %get-tuple-element.42.self_pair, f32[32,512]{1,0:T(8,128)S(1)} %collective-permute-done.13.pair8, f32[32,512]{1,0:T(8,128)S(1)} %collective-permute-done.14.pair4, f32[32,512]{1,0:T(8,128)S(1)} %collective-permute-done.15.pair2, ...), custom_call_target="tpu_custom_call" | custom-call | flops 3449999872 | bytes 11070000 | tf_op jit(solution)/shard_map/sums/pallas_call | solution.py:279
  (41 shorter events, 13.4 us)
Async XLA Ops:
  2.2 25.9 %collective-permute-start = (bf16[2,1024,256]{2,1,0:T(8,128)(2,1)S(1)}, bf16[2,1024,256]{2,1,0:T(8,128)(2,1)S(1)}, u32[]{:S(2)}, u32[]{:S(2)}) collective-permute-start(bf16[2,1024,256]{2,1,0:T(8,128)(2,1)S(1)} %get-tuple-element.34.refs_0_.rest_0_.own), channel_id=1, source_target_pairs={{0,4},{1,5},{2,6},{3,7},{4,8},{5,9},{6,10},{7,11},{8,12},{9,13},{1... | collective-permute-start | bytes 3145736 | tf_op jit(solution)/shard_map/ppermute | solution.py:23
  3.5 25.5 %collective-permute-start.2 = (bf16[2,1024,256]{2,1,0:T(8,128)(2,1)S(1)}, bf16[2,1024,256]{2,1,0:T(8,128)(2,1)S(1)}, u32[]{:S(2)}, u32[]{:S(2)}) collective-permute-start(bf16[2,1024,256]{2,1,0:T(8,128)(2,1)S(1)} %get-tuple-element.37.refs_1_.qg.rest_0_), channel_id=1, source_target_pairs={{4,0},{5,1},{6,2},{7,3},{8,4},{9,5},{10,6},{11,7},{12,8},{13,9},{1... | collective-permute-start | bytes 3145736 | tf_op jit(solution)/shard_map/ppermute | solution.py:23
  7.6 23.5 %collective-permute-start.1 = (bf16[2,1024,256]{2,1,0:T(8,128)(2,1)S(1)}, bf16[2,1024,256]{2,1,0:T(8,128)(2,1)S(1)}, u32[]{:S(2)}, u32[]{:S(2)}) collective-permute-start(bf16[2,1024,256]{2,1,0:T(8,128)(2,1)S(1)} %get-tuple-element.29), channel_id=1, source_target_pairs={{0,2},{1,3},{2,0},{3,1},{4,6},{5,7},{6,4},{7,5},{8,10},{9,11},{10,... | collective-permute-start | bytes 3145736 | tf_op jit(solution)/shard_map/ppermute | solution.py:28
  10.7 39.9 %collective-permute-start.4 = (bf16[2,1024,256]{2,1,0:T(8,128)(2,1)S(1)}, bf16[2,1024,256]{2,1,0:T(8,128)(2,1)S(1)}, u32[]{:S(2)}, u32[]{:S(2)}) collective-permute-start(bf16[2,1024,256]{2,1,0:T(8,128)(2,1)S(1)} %get-tuple-element.31.refs_0_.rest_0_.own), channel_id=1, source_target_pairs={{0,4},{1,5},{2,6},{3,7},{4,8},{5,9},{6,10},{7,11},{8,12},{9,13},{1... | collective-permute-start | bytes 3145736 | tf_op jit(solution)/shard_map/ppermute | solution.py:23
  12.0 40.0 %collective-permute-start.5 = (bf16[2,1024,256]{2,1,0:T(8,128)(2,1)S(1)}, bf16[2,1024,256]{2,1,0:T(8,128)(2,1)S(1)}, u32[]{:S(2)}, u32[]{:S(2)}) collective-permute-start(bf16[2,1024,256]{2,1,0:T(8,128)(2,1)S(1)} %get-tuple-element.40.qg.refs_1_.rest_8_), channel_id=1, source_target_pairs={{4,0},{5,1},{6,2},{7,3},{8,4},{9,5},{10,6},{11,7},{12,8},{13,9},{1... | collective-permute-start | bytes 3145736 | tf_op jit(solution)/shard_map/ppermute | solution.py:23
  31.1 22.5 %collective-permute-start.3 = (bf16[2,1024,256]{2,1,0:T(8,128)(2,1)S(1)}, bf16[2,1024,256]{2,1,0:T(8,128)(2,1)S(1)}, u32[]{:S(2)}, u32[]{:S(2)}) collective-permute-start(bf16[2,1024,256]{2,1,0:T(8,128)(2,1)S(1)} %pick.7), channel_id=1, source_target_pairs={{0,2},{1,3},{2,0},{3,1},{4,6},{5,7},{6,4},{7,5},{8,10},{9,11},{10,... | collective-permute-start | bytes 3145736 | tf_op jit(solution)/shard_map/ppermute | solution.py:28
  32.3 41.6 %collective-permute-start.8 = (bf16[2,1024,256]{2,1,0:T(8,128)(2,1)S(1)}, bf16[2,1024,256]{2,1,0:T(8,128)(2,1)S(1)}, u32[]{:S(2)}, u32[]{:S(2)}) collective-permute-start(bf16[2,1024,256]{2,1,0:T(8,128)(2,1)S(1)} %collective-permute-done.2.refs_0_.rest_2_), channel_id=1, source_target_pairs={{4,0},{5,1},{6,2},{7,3},{8,4},{9,5},{10,6},{11,7},{12,8},{13,9},{1... | collective-permute-start | bytes 3145736 | tf_op jit(solution)/shard_map/ppermute | solution.py:23
  34.4 39.5 %collective-permute-start.10 = (bf16[2,1024,256]{2,1,0:T(8,128)(2,1)S(1)}, bf16[2,1024,256]{2,1,0:T(8,128)(2,1)S(1)}, u32[]{:S(2)}, u32[]{:S(2)}) collective-permute-start(bf16[2,1024,256]{2,1,0:T(8,128)(2,1)S(1)} %collective-permute-done.refs_1_.rest_1_.far4), channel_id=1, source_target_pairs={{0,4},{1,5},{2,6},{3,7},{4,8},{5,9},{6,10},{7,11},{8,12},{9,13},{1... | collective-permute-start | bytes 3145736 | tf_op jit(solution)/shard_map/ppermute | solution.py:23
  50.7 25.8 %collective-permute-start.9 = (bf16[2,1024,256]{2,1,0:T(8,128)(2,1)S(1)}, bf16[2,1024,256]{2,1,0:T(8,128)(2,1)S(1)}, u32[]{:S(2)}, u32[]{:S(2)}) collective-permute-start(bf16[2,1024,256]{2,1,0:T(8,128)(2,1)S(1)} %pick.10), channel_id=1, source_target_pairs={{0,2},{1,3},{2,0},{3,1},{4,6},{5,7},{6,4},{7,5},{8,10},{9,11},{10,... | collective-permute-start | bytes 3145736 | tf_op jit(solution)/shard_map/ppermute | solution.py:28
  53.6 28.1 %collective-permute-start.7 = (bf16[2,1024,256]{2,1,0:T(8,128)(2,1)S(1)}, bf16[2,1024,256]{2,1,0:T(8,128)(2,1)S(1)}, u32[]{:S(2)}, u32[]{:S(2)}) collective-permute-start(bf16[2,1024,256]{2,1,0:T(8,128)(2,1)S(1)} %pick.9), channel_id=1, source_target_pairs={{0,1},{1,0},{2,3},{3,2},{4,5},{5,4},{6,7},{7,6},{8,9},{9,8},{10,11... | collective-permute-start | bytes 3145736 | tf_op jit(solution)/shard_map/ppermute | solution.py:28
  59.5 22.2 %collective-permute-start.6 = (bf16[2,1024,256]{2,1,0:T(8,128)(2,1)S(1)}, bf16[2,1024,256]{2,1,0:T(8,128)(2,1)S(1)}, u32[]{:S(2)}, u32[]{:S(2)}) collective-permute-start(bf16[2,1024,256]{2,1,0:T(8,128)(2,1)S(1)} %pick.8), channel_id=1, source_target_pairs={{0,1},{1,0},{2,3},{3,2},{4,5},{5,4},{6,7},{7,6},{8,9},{9,8},{10,11... | collective-permute-start | bytes 3145736 | tf_op jit(solution)/shard_map/ppermute | solution.py:28
  74.0 25.2 %collective-permute-start.18 = (bf16[2,1024,256]{2,1,0:T(8,128)(2,1)S(1)}, bf16[2,1024,256]{2,1,0:T(8,128)(2,1)S(1)}, u32[]{:S(2)}, u32[]{:S(2)}) collective-permute-start(bf16[2,1024,256]{2,1,0:T(8,128)(2,1)S(1)} %pick.12), channel_id=1, source_target_pairs={{0,2},{1,3},{2,0},{3,1},{4,6},{5,7},{6,4},{7,5},{8,10},{9,11},{10,... | collective-permute-start | bytes 3145736 | tf_op jit(solution)/shard_map/ppermute | solution.py:28
  75.2 26.5 %collective-permute-start.12 = (bf16[2,1024,256]{2,1,0:T(8,128)(2,1)S(1)}, bf16[2,1024,256]{2,1,0:T(8,128)(2,1)S(1)}, u32[]{:S(2)}, u32[]{:S(2)}) collective-permute-start(bf16[2,1024,256]{2,1,0:T(8,128)(2,1)S(1)} %collective-permute-done.4.refs_1_.rest_1_.far4), channel_id=1, source_target_pairs={{0,4},{1,5},{2,6},{3,7},{4,8},{5,9},{6,10},{7,11},{8,12},{9,13},{1... | collective-permute-start | bytes 3145736 | tf_op jit(solution)/shard_map/ppermute | solution.py:23
  76.5 34.3 %collective-permute-start.17 = (bf16[2,1024,256]{2,1,0:T(8,128)(2,1)S(1)}, bf16[2,1024,256]{2,1,0:T(8,128)(2,1)S(1)}, u32[]{:S(2)}, u32[]{:S(2)}) collective-permute-start(bf16[2,1024,256]{2,1,0:T(8,128)(2,1)S(1)} %collective-permute-done.5.refs_0_.rest_10_), channel_id=1, source_target_pairs={{4,0},{5,1},{6,2},{7,3},{8,4},{9,5},{10,6},{11,7},{12,8},{13,9},{1... | collective-permute-start | bytes 3145736 | tf_op jit(solution)/shard_map/ppermute | solution.py:23
  82.9 19.2 %collective-permute-start.11 = (bf16[2,1024,256]{2,1,0:T(8,128)(2,1)S(1)}, bf16[2,1024,256]{2,1,0:T(8,128)(2,1)S(1)}, u32[]{:S(2)}, u32[]{:S(2)}) collective-permute-start(bf16[2,1024,256]{2,1,0:T(8,128)(2,1)S(1)} %pick.11), channel_id=1, source_target_pairs={{0,1},{1,0},{2,3},{3,2},{4,5},{5,4},{6,7},{7,6},{8,9},{9,8},{10,11... | collective-permute-start | bytes 3145736 | tf_op jit(solution)/shard_map/ppermute | solution.py:28
  99.3 18.3 %collective-permute-start.19 = (bf16[2,1024,256]{2,1,0:T(8,128)(2,1)S(1)}, bf16[2,1024,256]{2,1,0:T(8,128)(2,1)S(1)}, u32[]{:S(2)}, u32[]{:S(2)}) collective-permute-start(bf16[2,1024,256]{2,1,0:T(8,128)(2,1)S(1)} %pick.13), channel_id=1, source_target_pairs={{0,1},{1,0},{2,3},{3,2},{4,5},{5,4},{6,7},{7,6},{8,9},{9,8},{10,11... | collective-permute-start | bytes 3145736 | tf_op jit(solution)/shard_map/ppermute | solution.py:28
  102.0 1.2 copy-start.3
  102.1 12.8 %copy-start = (bf16[1024,1024]{1,0:T(8,128)(2,1)S(1)}, bf16[1024,1024]{1,0:T(8,128)(2,1)}, u32[]{:S(2)}) copy-start(bf16[1024,1024]{1,0:T(8,128)(2,1)} %w_query.3) | copy-start | bytes 6291460
  103.9 13.7 %collective-permute-start.13 = (f32[32,512]{1,0:T(8,128)S(1)}, f32[32,512]{1,0:T(8,128)S(1)}, u32[]{:S(2)}, u32[]{:S(2)}) collective-permute-start(f32[32,512]{1,0:T(8,128)S(1)} %get-tuple-element.43.pair8), channel_id=1, source_target_pairs={{8,0},{9,1},{10,2},{11,3},{12,4},{13,5},{14,6},{15,7},{24,16},{25,... | collective-permute-start | bytes 196616 | tf_op jit(solution)/shard_map/ppermute | solution.py:23
  105.8 11.8 %collective-permute-start.14 = (f32[32,512]{1,0:T(8,128)S(1)}, f32[32,512]{1,0:T(8,128)S(1)}, u32[]{:S(2)}, u32[]{:S(2)}) collective-permute-start(f32[32,512]{1,0:T(8,128)S(1)} %get-tuple-element.44.pair4), channel_id=1, source_target_pairs={{4,0},{5,1},{6,2},{7,3},{8,4},{9,5},{10,6},{11,7},{12,8},{13,9},{1... | collective-permute-start | bytes 196616 | tf_op jit(solution)/shard_map/ppermute | solution.py:23
  108.0 9.7 %collective-permute-start.15 = (f32[32,512]{1,0:T(8,128)S(1)}, f32[32,512]{1,0:T(8,128)S(1)}, u32[]{:S(2)}, u32[]{:S(2)}) collective-permute-start(f32[32,512]{1,0:T(8,128)S(1)} %get-tuple-element.45.pair2), channel_id=1, source_target_pairs={{2,0},{3,1},{4,2},{5,3},{6,4},{7,5},{8,6},{9,7},{10,8},{11,9},{12,... | collective-permute-start | bytes 196616 | tf_op jit(solution)/shard_map/ppermute | solution.py:23
  110.8 7.1 %collective-permute-start.16 = (f32[32,512]{1,0:T(8,128)S(1)}, f32[32,512]{1,0:T(8,128)S(1)}, u32[]{:S(2)}, u32[]{:S(2)}) collective-permute-start(f32[32,512]{1,0:T(8,128)S(1)} %get-tuple-element.46.pair1), channel_id=1, source_target_pairs={{1,0},{2,1},{3,2},{4,3},{5,4},{6,5},{7,6},{8,7},{9,8},{10,9},{11,1... | collective-permute-start | bytes 196616 | tf_op jit(solution)/shard_map/ppermute | solution.py:23
  116.2 1.7 %copy-start.1 = (bf16[1024,1024]{1,0:T(8,128)(2,1)S(1)}, bf16[1024,1024]{1,0:T(8,128)(2,1)}, u32[]{:S(2)}) copy-start(bf16[1024,1024]{1,0:T(8,128)(2,1)} %w_key.1) | copy-start | bytes 6291460
  116.2 2.2 %copy-start.2 = (bf16[1024,1024]{1,0:T(8,128)(2,1)S(1)}, bf16[1024,1024]{1,0:T(8,128)(2,1)}, u32[]{:S(2)}) copy-start(bf16[1024,1024]{1,0:T(8,128)(2,1)} %w_value.1) | copy-start | bytes 6291460

commit v7 on v6

--- a/solution.py
+++ b/solution.py
@@ -246,10 +246,9 @@
         two, one, rest = rest[4:4 + n_two], rest[4 + n_two:4 + n_two + n_one], rest[4 + n_two + n_one:]
         _, width, patches = own.shape
 
-        @pl.loop(0, patches // LANES)
-        def _(step):
-            here = lanes(step)
-            there = lanes(step + i * (patches // LANES))
+        for step in range(patches // LANES):
+            here = slice(step * LANES, (step + 1) * LANES)
+            there = slice(i * patches + step * LANES, i * patches + (step + 1) * LANES)
             getters = source_getters(own, two, one, far4, far8, 0, here)
             for h, rows in enumerate(head_slices(width)):
                 for part, into in ((0, key_ref), (1, value_ref)):
@@ -258,7 +257,7 @@
                              for s, get in enumerate(getters)]
                     into[rows, there] = functools.reduce(jnp.add, terms).astype(jnp.bfloat16)
 
-        columns = pl.ds(i * patches, patches)
+        columns = slice(i * patches, (i + 1) * patches)
         for o in range(0, width, PIECE):
             piece = slice(o, o + PIECE)
             total = query_part[piece, :] + jnp.dot(

time: 125 us -> 124 us (level)
  no operation moved by 1% of the time
where the time goes in v7:
time: 124 us
  waiting for transfers between devices  59.7 us (48%)
  starting transfers between devices  47.1 us (38%)
  Pallas kernels  15.8 us (13%)
    ppermute x12, waiting for transfers between devices, shift(): lax.ppermute(block, 'frame', [(i, i + distance) for i in range(n) if 0 <=...  42.3 us
    ppermute x12, starting transfers between devices, shift(): lax.ppermute(block, 'frame', [(i, i + distance) for i in range(n) if 0 <=...  31.2 us
    ppermute x8, waiting for transfers between devices, swap(): return lax.ppermute(block, 'frame', [(i, i ^ bit) for i in range(n)])  17.5 us
    ppermute x8, starting transfers between devices, swap(): return lax.ppermute(block, 'frame', [(i, i ^ bit) for i in range(n)])  16 us
    pallas_call x1, Pallas kernels, sums_of(): pl.pallas_call(functools.partial(sum_kernel, [(len(h[2]), len(h[3])) for...  5.05 us
    pallas_call x2, Pallas kernels, pack(): pl.pallas_call(kernel, in_specs=[pl.BlockSpec(memory_space=pl.ANY)] * 4,...  4.06 us
    pallas_call x4, Pallas kernels, products_of(): pl.pallas_call(functools.partial(product_kernel, len(two), len(one), len(...  2.87 us
    pallas_call x2, Pallas kernels, query_part_of(): pl.pallas_call(functools.partial(query_kernel, start), in_specs=[VMEM] *...  2.65 us
  transfers between devices with their start and end apart: 20, of which 8 were waited for; matrix products, arithmetic and copies ran while one was open for 0% of the time, Pallas kernels for 7%

profile of v7, /device:TPU:27, one launch (start us, length us, event | category | flops | bytes accessed | tf_op | source)
XLA Modules:
  0.0 123.7 jit_solution(2051113537741320329)
XLA Ops:
  0.0 2.2 %pack.2 = (bf16[2,1024,256]{2,1,0:T(8,128)(2,1)S(1)}, bf16[2,1024,256]{2,1,0:T(8,128)(2,1)S(1)}, bf16[2,1024,256]{2,1,0:T(8,128)(2,1)S(1)}) custom-call(bf16[1,512,1024]{2,1,0:T(8,128)(2,1)} %q_hbm.2, bf16[1,512,1024]{2,1,0:T(8,128)(2,1)} %k_hbm.3, bf16[1,512,1024]{2,1,0:T(8,128)(2,1)} %v_hbm.3, bf16[1,512,1024]{2,1,0:T(8,128)(2,1)} %g_hbm.3), custom_call_target="tpu_custom_call" | custom-call | tf_op jit(solution)/shard_map/pack/pallas_call | solution.py:71
  3.5 4.1 %collective-permute-start.2 = (bf16[2,1024,256]{2,1,0:T(8,128)(2,1)S(1)}, bf16[2,1024,256]{2,1,0:T(8,128)(2,1)S(1)}, u32[]{:S(2)}, u32[]{:S(2)}) collective-permute-start(bf16[2,1024,256]{2,1,0:T(8,128)(2,1)S(1)} %get-tuple-element.37.refs_1_.qg.rest_0_), channel_id=1, source_target_pairs={{4,0},{5,1},{6,2},{7,3},{8,4},{9,5},{10,6},{11,7},{12,8},{13,9},{1... | collective-permute-start | bytes 3145736 | tf_op jit(solution)/shard_map/ppermute | solution.py:23
  7.6 1.3 %collective-permute-start.1 = (bf16[2,1024,256]{2,1,0:T(8,128)(2,1)S(1)}, bf16[2,1024,256]{2,1,0:T(8,128)(2,1)S(1)}, u32[]{:S(2)}, u32[]{:S(2)}) collective-permute-start(bf16[2,1024,256]{2,1,0:T(8,128)(2,1)S(1)} %get-tuple-element.29), channel_id=1, source_target_pairs={{0,2},{1,3},{2,0},{3,1},{4,6},{5,7},{6,4},{7,5},{8,10},{9,11},{10,... | collective-permute-start | bytes 3145736 | tf_op jit(solution)/shard_map/ppermute | solution.py:28
  8.9 1.8 %pack.3 = (bf16[2,1024,256]{2,1,0:T(8,128)(2,1)S(1)}, bf16[2,1024,256]{2,1,0:T(8,128)(2,1)S(1)}) custom-call(bf16[1,512,1024]{2,1,0:T(8,128)(2,1)} %q_hbm.2, bf16[1,512,1024]{2,1,0:T(8,128)(2,1)} %k_hbm.3, bf16[1,512,1024]{2,1,0:T(8,128)(2,1)} %v_hbm.3, bf16[1,512,1024]{2,1,0:T(8,128)(2,1)} %g_hbm.3), custom_call_target="tpu_custom_call" | custom-call | tf_op jit(solution)/shard_map/pack/pallas_call | solution.py:71
  12.0 4.1 %collective-permute-start.5 = (bf16[2,1024,256]{2,1,0:T(8,128)(2,1)S(1)}, bf16[2,1024,256]{2,1,0:T(8,128)(2,1)S(1)}, u32[]{:S(2)}, u32[]{:S(2)}) collective-permute-start(bf16[2,1024,256]{2,1,0:T(8,128)(2,1)S(1)} %get-tuple-element.40.qg.refs_1_.rest_8_), channel_id=1, source_target_pairs={{4,0},{5,1},{6,2},{7,3},{8,4},{9,5},{10,6},{11,7},{12,8},{13,9},{1... | collective-permute-start | bytes 3145736 | tf_op jit(solution)/shard_map/ppermute | solution.py:23
  16.1 12.0 %collective-permute-done.refs_1_.rest_1_.far4 = bf16[2,1024,256]{2,1,0:T(8,128)(2,1)S(1)} collective-permute-done((bf16[2,1024,256]{2,1,0:T(8,128)(2,1)S(1)}, bf16[2,1024,256]{2,1,0:T(8,128)(2,1)S(1)}, u32[]{:S(2)}, u32[]{:S(2)}) %collective-permute-start) | collective-permute-done | bytes 1048608 | tf_op jit(solution)/shard_map/ppermute | solution.py:23
  29.0 2.1 %collective-permute-done.1.refs_2_.rest_2_.refs_0_.two_a.rest_4_ = bf16[2,1024,256]{2,1,0:T(8,128)(2,1)S(1)} collective-permute-done((bf16[2,1024,256]{2,1,0:T(8,128)(2,1)S(1)}, bf16[2,1024,256]{2,1,0:T(8,128)(2,1)S(1)}, u32[]{:S(2)}, u32[]{:S(2)}) %collective-permute-start.1) | collective-permute-done | bytes 1048608 | tf_op jit(solution)/shard_map/ppermute | solution.py:28
  32.3 2.1 %collective-permute-start.8 = (bf16[2,1024,256]{2,1,0:T(8,128)(2,1)S(1)}, bf16[2,1024,256]{2,1,0:T(8,128)(2,1)S(1)}, u32[]{:S(2)}, u32[]{:S(2)}) collective-permute-start(bf16[2,1024,256]{2,1,0:T(8,128)(2,1)S(1)} %collective-permute-done.2.refs_0_.rest_2_), channel_id=1, source_target_pairs={{4,0},{5,1},{6,2},{7,3},{8,4},{9,5},{10,6},{11,7},{12,8},{13,9},{1... | collective-permute-start | bytes 3145736 | tf_op jit(solution)/shard_map/ppermute | solution.py:23
  35.7 14.9 %collective-permute-done.4.refs_1_.rest_1_.far4 = bf16[2,1024,256]{2,1,0:T(8,128)(2,1)S(1)} collective-permute-done((bf16[2,1024,256]{2,1,0:T(8,128)(2,1)S(1)}, bf16[2,1024,256]{2,1,0:T(8,128)(2,1)S(1)}, u32[]{:S(2)}, u32[]{:S(2)}) %collective-permute-start.4) | collective-permute-done | bytes 1048608 | tf_op jit(solution)/shard_map/ppermute | solution.py:23
  50.7 1.3 %collective-permute-start.9 = (bf16[2,1024,256]{2,1,0:T(8,128)(2,1)S(1)}, bf16[2,1024,256]{2,1,0:T(8,128)(2,1)S(1)}, u32[]{:S(2)}, u32[]{:S(2)}) collective-permute-start(bf16[2,1024,256]{2,1,0:T(8,128)(2,1)S(1)} %pick.10), channel_id=1, source_target_pairs={{0,2},{1,3},{2,0},{3,1},{4,6},{5,7},{6,4},{7,5},{8,10},{9,11},{10,... | collective-permute-start | bytes 3145736 | tf_op jit(solution)/shard_map/ppermute | solution.py:28
  52.0 1.6 %collective-permute-done.3.refs_1_.rest_3_.refs_2_.rest_2_.two_b.two_a = bf16[2,1024,256]{2,1,0:T(8,128)(2,1)S(1)} collective-permute-done((bf16[2,1024,256]{2,1,0:T(8,128)(2,1)S(1)}, bf16[2,1024,256]{2,1,0:T(8,128)(2,1)S(1)}, u32[]{:S(2)}, u32[]{:S(2)}) %collective-permute-start.3) | collective-permute-done | bytes 1048608 | tf_op jit(solution)/shard_map/ppermute | solution.py:28
  53.6 5.8 %collective-permute-start.7 = (bf16[2,1024,256]{2,1,0:T(8,128)(2,1)S(1)}, bf16[2,1024,256]{2,1,0:T(8,128)(2,1)S(1)}, u32[]{:S(2)}, u32[]{:S(2)}) collective-permute-start(bf16[2,1024,256]{2,1,0:T(8,128)(2,1)S(1)} %pick.9), channel_id=1, source_target_pairs={{0,1},{1,0},{2,3},{3,2},{4,5},{5,4},{6,7},{7,6},{8,9},{9,8},{10,11... | collective-permute-start | bytes 3145736 | tf_op jit(solution)/shard_map/ppermute | solution.py:28
  59.7 14.2 %collective-permute-done.8.rest_3_ = bf16[2,1024,256]{2,1,0:T(8,128)(2,1)S(1)} collective-permute-done((bf16[2,1024,256]{2,1,0:T(8,128)(2,1)S(1)}, bf16[2,1024,256]{2,1,0:T(8,128)(2,1)S(1)}, u32[]{:S(2)}, u32[]{:S(2)}) %collective-permute-start.8) | collective-permute-done | bytes 1048608 | tf_op jit(solution)/shard_map/ppermute | solution.py:23
  76.5 4.8 %collective-permute-start.17 = (bf16[2,1024,256]{2,1,0:T(8,128)(2,1)S(1)}, bf16[2,1024,256]{2,1,0:T(8,128)(2,1)S(1)}, u32[]{:S(2)}, u32[]{:S(2)}) collective-permute-start(bf16[2,1024,256]{2,1,0:T(8,128)(2,1)S(1)} %collective-permute-done.5.refs_0_.rest_10_), channel_id=1, source_target_pairs={{4,0},{5,1},{6,2},{7,3},{8,4},{9,5},{10,6},{11,7},{12,8},{13,9},{1... | collective-permute-start | bytes 3145736 | tf_op jit(solution)/shard_map/ppermute | solution.py:23
  82.9 2.5 %collective-permute-start.11 = (bf16[2,1024,256]{2,1,0:T(8,128)(2,1)S(1)}, bf16[2,1024,256]{2,1,0:T(8,128)(2,1)S(1)}, u32[]{:S(2)}, u32[]{:S(2)}) collective-permute-start(bf16[2,1024,256]{2,1,0:T(8,128)(2,1)S(1)} %pick.11), channel_id=1, source_target_pairs={{0,1},{1,0},{2,3},{3,2},{4,5},{5,4},{6,7},{7,6},{8,9},{9,8},{10,11... | collective-permute-start | bytes 3145736 | tf_op jit(solution)/shard_map/ppermute | solution.py:28
  85.4 13.8 %collective-permute-done.18.refs_0_.rest_12_ = bf16[2,1024,256]{2,1,0:T(8,128)(2,1)S(1)} collective-permute-done((bf16[2,1024,256]{2,1,0:T(8,128)(2,1)S(1)}, bf16[2,1024,256]{2,1,0:T(8,128)(2,1)S(1)}, u32[]{:S(2)}, u32[]{:S(2)}) %collective-permute-start.18) | collective-permute-done | bytes 1048608 | tf_op jit(solution)/shard_map/ppermute | solution.py:28
  99.3 2.5 %collective-permute-start.19 = (bf16[2,1024,256]{2,1,0:T(8,128)(2,1)S(1)}, bf16[2,1024,256]{2,1,0:T(8,128)(2,1)S(1)}, u32[]{:S(2)}, u32[]{:S(2)}) collective-permute-start(bf16[2,1024,256]{2,1,0:T(8,128)(2,1)S(1)} %pick.13), channel_id=1, source_target_pairs={{0,1},{1,0},{2,3},{3,2},{4,5},{5,4},{6,7},{7,6},{8,9},{9,8},{10,11... | collective-permute-start | bytes 3145736 | tf_op jit(solution)/shard_map/ppermute | solution.py:28
  103.9 2.0 %collective-permute-start.13 = (f32[32,512]{1,0:T(8,128)S(1)}, f32[32,512]{1,0:T(8,128)S(1)}, u32[]{:S(2)}, u32[]{:S(2)}) collective-permute-start(f32[32,512]{1,0:T(8,128)S(1)} %get-tuple-element.43.pair8), channel_id=1, source_target_pairs={{8,0},{9,1},{10,2},{11,3},{12,4},{13,5},{14,6},{15,7},{24,16},{25,... | collective-permute-start | bytes 196616 | tf_op jit(solution)/shard_map/ppermute | solution.py:23
  105.8 2.1 %collective-permute-start.14 = (f32[32,512]{1,0:T(8,128)S(1)}, f32[32,512]{1,0:T(8,128)S(1)}, u32[]{:S(2)}, u32[]{:S(2)}) collective-permute-start(f32[32,512]{1,0:T(8,128)S(1)} %get-tuple-element.44.pair4), channel_id=1, source_target_pairs={{4,0},{5,1},{6,2},{7,3},{8,4},{9,5},{10,6},{11,7},{12,8},{13,9},{1... | collective-permute-start | bytes 196616 | tf_op jit(solution)/shard_map/ppermute | solution.py:23
  108.0 2.9 %collective-permute-start.15 = (f32[32,512]{1,0:T(8,128)S(1)}, f32[32,512]{1,0:T(8,128)S(1)}, u32[]{:S(2)}, u32[]{:S(2)}) collective-permute-start(f32[32,512]{1,0:T(8,128)S(1)} %get-tuple-element.45.pair2), channel_id=1, source_target_pairs={{2,0},{3,1},{4,2},{5,3},{6,4},{7,5},{8,6},{9,7},{10,8},{11,9},{12,... | collective-permute-start | bytes 196616 | tf_op jit(solution)/shard_map/ppermute | solution.py:23
  110.8 4.0 %collective-permute-start.16 = (f32[32,512]{1,0:T(8,128)S(1)}, f32[32,512]{1,0:T(8,128)S(1)}, u32[]{:S(2)}, u32[]{:S(2)}) collective-permute-start(f32[32,512]{1,0:T(8,128)S(1)} %get-tuple-element.46.pair1), channel_id=1, source_target_pairs={{1,0},{2,1},{3,2},{4,3},{5,4},{6,5},{7,6},{8,7},{9,8},{10,9},{11,1... | collective-permute-start | bytes 196616 | tf_op jit(solution)/shard_map/ppermute | solution.py:23
  114.9 1.3 %query_part.3.rest_9_ = f32[1024,256]{1,0:T(8,128)S(1)} custom-call(bf16[2,1024,256]{2,1,0:T(8,128)(2,1)S(1)} %get-tuple-element.31.refs_0_.rest_0_.own, bf16[2,1024,256]{2,1,0:T(8,128)(2,1)S(1)} %collective-permute-done.3.refs_1_.rest_3_.refs_2_.rest_2_.two_b.two_a, bf16[2,1024,256]{2,1,0:T(8,128)(2,1)S(1)} %collective-permute-done.9.refs_1_.rest_3_.two_b.rest_5_, ...), custom_call_target="tpu_custom_call" | custom-call | tf_op jit(solution)/shard_map/query_part/pallas_call | solution.py:227
  116.3 1.3 %query_part.2.rest_1_ = f32[1024,256]{1,0:T(8,128)S(1)} custom-call(bf16[2,1024,256]{2,1,0:T(8,128)(2,1)S(1)} %get-tuple-element.34.refs_0_.rest_0_.own, bf16[2,1024,256]{2,1,0:T(8,128)(2,1)S(1)} %collective-permute-done.1.refs_2_.rest_2_.refs_0_.two_a.rest_4_, bf16[2,1024,256]{2,1,0:T(8,128)(2,1)S(1)} %collective-permute-done.3.refs_1_.rest_3_.refs_2_.rest_2_.two_b.two_a, ...), custom_call_target="tpu_custom_call" | custom-call | tf_op jit(solution)/shard_map/query_part/pallas_call | solution.py:227
  118.5 5.0 %sums.1 = bf16[512,1024]{1,0:T(8,128)(2,1)} custom-call(f32[32,512]{1,0:T(8,128)S(1)} %get-tuple-element.42.self_pair, f32[32,512]{1,0:T(8,128)S(1)} %collective-permute-done.13.pair8, f32[32,512]{1,0:T(8,128)S(1)} %collective-permute-done.14.pair4, f32[32,512]{1,0:T(8,128)S(1)} %collective-permute-done.15.pair2, ...), custom_call_target="tpu_custom_call" | custom-call | flops 3449999872 | bytes 11070000 | tf_op jit(solution)/shard_map/sums/pallas_call | solution.py:278
  (41 shorter events, 13.4 us)
Async XLA Ops:
  2.2 25.9 %collective-permute-start = (bf16[2,1024,256]{2,1,0:T(8,128)(2,1)S(1)}, bf16[2,1024,256]{2,1,0:T(8,128)(2,1)S(1)}, u32[]{:S(2)}, u32[]{:S(2)}) collective-permute-start(bf16[2,1024,256]{2,1,0:T(8,128)(2,1)S(1)} %get-tuple-element.34.refs_0_.rest_0_.own), channel_id=1, source_target_pairs={{0,4},{1,5},{2,6},{3,7},{4,8},{5,9},{6,10},{7,11},{8,12},{9,13},{1... | collective-permute-start | bytes 3145736 | tf_op jit(solution)/shard_map/ppermute | solution.py:23
  3.5 25.5 %collective-permute-start.2 = (bf16[2,1024,256]{2,1,0:T(8,128)(2,1)S(1)}, bf16[2,1024,256]{2,1,0:T(8,128)(2,1)S(1)}, u32[]{:S(2)}, u32[]{:S(2)}) collective-permute-start(bf16[2,1024,256]{2,1,0:T(8,128)(2,1)S(1)} %get-tuple-element.37.refs_1_.qg.rest_0_), channel_id=1, source_target_pairs={{4,0},{5,1},{6,2},{7,3},{8,4},{9,5},{10,6},{11,7},{12,8},{13,9},{1... | collective-permute-start | bytes 3145736 | tf_op jit(solution)/shard_map/ppermute | solution.py:23
  7.6 23.5 %collective-permute-start.1 = (bf16[2,1024,256]{2,1,0:T(8,128)(2,1)S(1)}, bf16[2,1024,256]{2,1,0:T(8,128)(2,1)S(1)}, u32[]{:S(2)}, u32[]{:S(2)}) collective-permute-start(bf16[2,1024,256]{2,1,0:T(8,128)(2,1)S(1)} %get-tuple-element.29), channel_id=1, source_target_pairs={{0,2},{1,3},{2,0},{3,1},{4,6},{5,7},{6,4},{7,5},{8,10},{9,11},{10,... | collective-permute-start | bytes 3145736 | tf_op jit(solution)/shard_map/ppermute | solution.py:28
  10.7 39.9 %collective-permute-start.4 = (bf16[2,1024,256]{2,1,0:T(8,128)(2,1)S(1)}, bf16[2,1024,256]{2,1,0:T(8,128)(2,1)S(1)}, u32[]{:S(2)}, u32[]{:S(2)}) collective-permute-start(bf16[2,1024,256]{2,1,0:T(8,128)(2,1)S(1)} %get-tuple-element.31.refs_0_.rest_0_.own), channel_id=1, source_target_pairs={{0,4},{1,5},{2,6},{3,7},{4,8},{5,9},{6,10},{7,11},{8,12},{9,13},{1... | collective-permute-start | bytes 3145736 | tf_op jit(solution)/shard_map/ppermute | solution.py:23
  12.0 40.0 %collective-permute-start.5 = (bf16[2,1024,256]{2,1,0:T(8,128)(2,1)S(1)}, bf16[2,1024,256]{2,1,0:T(8,128)(2,1)S(1)}, u32[]{:S(2)}, u32[]{:S(2)}) collective-permute-start(bf16[2,1024,256]{2,1,0:T(8,128)(2,1)S(1)} %get-tuple-element.40.qg.refs_1_.rest_8_), channel_id=1, source_target_pairs={{4,0},{5,1},{6,2},{7,3},{8,4},{9,5},{10,6},{11,7},{12,8},{13,9},{1... | collective-permute-start | bytes 3145736 | tf_op jit(solution)/shard_map/ppermute | solution.py:23
  31.1 22.5 %collective-permute-start.3 = (bf16[2,1024,256]{2,1,0:T(8,128)(2,1)S(1)}, bf16[2,1024,256]{2,1,0:T(8,128)(2,1)S(1)}, u32[]{:S(2)}, u32[]{:S(2)}) collective-permute-start(bf16[2,1024,256]{2,1,0:T(8,128)(2,1)S(1)} %pick.7), channel_id=1, source_target_pairs={{0,2},{1,3},{2,0},{3,1},{4,6},{5,7},{6,4},{7,5},{8,10},{9,11},{10,... | collective-permute-start | bytes 3145736 | tf_op jit(solution)/shard_map/ppermute | solution.py:28
  32.3 41.6 %collective-permute-start.8 = (bf16[2,1024,256]{2,1,0:T(8,128)(2,1)S(1)}, bf16[2,1024,256]{2,1,0:T(8,128)(2,1)S(1)}, u32[]{:S(2)}, u32[]{:S(2)}) collective-permute-start(bf16[2,1024,256]{2,1,0:T(8,128)(2,1)S(1)} %collective-permute-done.2.refs_0_.rest_2_), channel_id=1, source_target_pairs={{4,0},{5,1},{6,2},{7,3},{8,4},{9,5},{10,6},{11,7},{12,8},{13,9},{1... | collective-permute-start | bytes 3145736 | tf_op jit(solution)/shard_map/ppermute | solution.py:23
  34.4 39.5 %collective-permute-start.10 = (bf16[2,1024,256]{2,1,0:T(8,128)(2,1)S(1)}, bf16[2,1024,256]{2,1,0:T(8,128)(2,1)S(1)}, u32[]{:S(2)}, u32[]{:S(2)}) collective-permute-start(bf16[2,1024,256]{2,1,0:T(8,128)(2,1)S(1)} %collective-permute-done.refs_1_.rest_1_.far4), channel_id=1, source_target_pairs={{0,4},{1,5},{2,6},{3,7},{4,8},{5,9},{6,10},{7,11},{8,12},{9,13},{1... | collective-permute-start | bytes 3145736 | tf_op jit(solution)/shard_map/ppermute | solution.py:23
  50.7 25.8 %collective-permute-start.9 = (bf16[2,1024,256]{2,1,0:T(8,128)(2,1)S(1)}, bf16[2,1024,256]{2,1,0:T(8,128)(2,1)S(1)}, u32[]{:S(2)}, u32[]{:S(2)}) collective-permute-start(bf16[2,1024,256]{2,1,0:T(8,128)(2,1)S(1)} %pick.10), channel_id=1, source_target_pairs={{0,2},{1,3},{2,0},{3,1},{4,6},{5,7},{6,4},{7,5},{8,10},{9,11},{10,... | collective-permute-start | bytes 3145736 | tf_op jit(solution)/shard_map/ppermute | solution.py:28
  53.6 28.1 %collective-permute-start.7 = (bf16[2,1024,256]{2,1,0:T(8,128)(2,1)S(1)}, bf16[2,1024,256]{2,1,0:T(8,128)(2,1)S(1)}, u32[]{:S(2)}, u32[]{:S(2)}) collective-permute-start(bf16[2,1024,256]{2,1,0:T(8,128)(2,1)S(1)} %pick.9), channel_id=1, source_target_pairs={{0,1},{1,0},{2,3},{3,2},{4,5},{5,4},{6,7},{7,6},{8,9},{9,8},{10,11... | collective-permute-start | bytes 3145736 | tf_op jit(solution)/shard_map/ppermute | solution.py:28
  59.5 22.2 %collective-permute-start.6 = (bf16[2,1024,256]{2,1,0:T(8,128)(2,1)S(1)}, bf16[2,1024,256]{2,1,0:T(8,128)(2,1)S(1)}, u32[]{:S(2)}, u32[]{:S(2)}) collective-permute-start(bf16[2,1024,256]{2,1,0:T(8,128)(2,1)S(1)} %pick.8), channel_id=1, source_target_pairs={{0,1},{1,0},{2,3},{3,2},{4,5},{5,4},{6,7},{7,6},{8,9},{9,8},{10,11... | collective-permute-start | bytes 3145736 | tf_op jit(solution)/shard_map/ppermute | solution.py:28
  74.0 25.2 %collective-permute-start.18 = (bf16[2,1024,256]{2,1,0:T(8,128)(2,1)S(1)}, bf16[2,1024,256]{2,1,0:T(8,128)(2,1)S(1)}, u32[]{:S(2)}, u32[]{:S(2)}) collective-permute-start(bf16[2,1024,256]{2,1,0:T(8,128)(2,1)S(1)} %pick.12), channel_id=1, source_target_pairs={{0,2},{1,3},{2,0},{3,1},{4,6},{5,7},{6,4},{7,5},{8,10},{9,11},{10,... | collective-permute-start | bytes 3145736 | tf_op jit(solution)/shard_map/ppermute | solution.py:28
  75.2 26.5 %collective-permute-start.12 = (bf16[2,1024,256]{2,1,0:T(8,128)(2,1)S(1)}, bf16[2,1024,256]{2,1,0:T(8,128)(2,1)S(1)}, u32[]{:S(2)}, u32[]{:S(2)}) collective-permute-start(bf16[2,1024,256]{2,1,0:T(8,128)(2,1)S(1)} %collective-permute-done.4.refs_1_.rest_1_.far4), channel_id=1, source_target_pairs={{0,4},{1,5},{2,6},{3,7},{4,8},{5,9},{6,10},{7,11},{8,12},{9,13},{1... | collective-permute-start | bytes 3145736 | tf_op jit(solution)/shard_map/ppermute | solution.py:23
  76.5 34.3 %collective-permute-start.17 = (bf16[2,1024,256]{2,1,0:T(8,128)(2,1)S(1)}, bf16[2,1024,256]{2,1,0:T(8,128)(2,1)S(1)}, u32[]{:S(2)}, u32[]{:S(2)}) collective-permute-start(bf16[2,1024,256]{2,1,0:T(8,128)(2,1)S(1)} %collective-permute-done.5.refs_0_.rest_10_), channel_id=1, source_target_pairs={{4,0},{5,1},{6,2},{7,3},{8,4},{9,5},{10,6},{11,7},{12,8},{13,9},{1... | collective-permute-start | bytes 3145736 | tf_op jit(solution)/shard_map/ppermute | solution.py:23
  82.9 19.2 %collective-permute-start.11 = (bf16[2,1024,256]{2,1,0:T(8,128)(2,1)S(1)}, bf16[2,1024,256]{2,1,0:T(8,128)(2,1)S(1)}, u32[]{:S(2)}, u32[]{:S(2)}) collective-permute-start(bf16[2,1024,256]{2,1,0:T(8,128)(2,1)S(1)} %pick.11), channel_id=1, source_target_pairs={{0,1},{1,0},{2,3},{3,2},{4,5},{5,4},{6,7},{7,6},{8,9},{9,8},{10,11... | collective-permute-start | bytes 3145736 | tf_op jit(solution)/shard_map/ppermute | solution.py:28
  99.3 18.3 %collective-permute-start.19 = (bf16[2,1024,256]{2,1,0:T(8,128)(2,1)S(1)}, bf16[2,1024,256]{2,1,0:T(8,128)(2,1)S(1)}, u32[]{:S(2)}, u32[]{:S(2)}) collective-permute-start(bf16[2,1024,256]{2,1,0:T(8,128)(2,1)S(1)} %pick.13), channel_id=1, source_target_pairs={{0,1},{1,0},{2,3},{3,2},{4,5},{5,4},{6,7},{7,6},{8,9},{9,8},{10,11... | collective-permute-start | bytes 3145736 | tf_op jit(solution)/shard_map/ppermute | solution.py:28
  102.0 1.2 copy-start.3
  102.1 12.8 %copy-start = (bf16[1024,1024]{1,0:T(8,128)(2,1)S(1)}, bf16[1024,1024]{1,0:T(8,128)(2,1)}, u32[]{:S(2)}) copy-start(bf16[1024,1024]{1,0:T(8,128)(2,1)} %w_query.3) | copy-start | bytes 6291460
  103.9 13.7 %collective-permute-start.13 = (f32[32,512]{1,0:T(8,128)S(1)}, f32[32,512]{1,0:T(8,128)S(1)}, u32[]{:S(2)}, u32[]{:S(2)}) collective-permute-start(f32[32,512]{1,0:T(8,128)S(1)} %get-tuple-element.43.pair8), channel_id=1, source_target_pairs={{8,0},{9,1},{10,2},{11,3},{12,4},{13,5},{14,6},{15,7},{24,16},{25,... | collective-permute-start | bytes 196616 | tf_op jit(solution)/shard_map/ppermute | solution.py:23
  105.8 11.8 %collective-permute-start.14 = (f32[32,512]{1,0:T(8,128)S(1)}, f32[32,512]{1,0:T(8,128)S(1)}, u32[]{:S(2)}, u32[]{:S(2)}) collective-permute-start(f32[32,512]{1,0:T(8,128)S(1)} %get-tuple-element.44.pair4), channel_id=1, source_target_pairs={{4,0},{5,1},{6,2},{7,3},{8,4},{9,5},{10,6},{11,7},{12,8},{13,9},{1... | collective-permute-start | bytes 196616 | tf_op jit(solution)/shard_map/ppermute | solution.py:23
  108.0 9.7 %collective-permute-start.15 = (f32[32,512]{1,0:T(8,128)S(1)}, f32[32,512]{1,0:T(8,128)S(1)}, u32[]{:S(2)}, u32[]{:S(2)}) collective-permute-start(f32[32,512]{1,0:T(8,128)S(1)} %get-tuple-element.45.pair2), channel_id=1, source_target_pairs={{2,0},{3,1},{4,2},{5,3},{6,4},{7,5},{8,6},{9,7},{10,8},{11,9},{12,... | collective-permute-start | bytes 196616 | tf_op jit(solution)/shard_map/ppermute | solution.py:23
  110.8 7.1 %collective-permute-start.16 = (f32[32,512]{1,0:T(8,128)S(1)}, f32[32,512]{1,0:T(8,128)S(1)}, u32[]{:S(2)}, u32[]{:S(2)}) collective-permute-start(f32[32,512]{1,0:T(8,128)S(1)} %get-tuple-element.46.pair1), channel_id=1, source_target_pairs={{1,0},{2,1},{3,2},{4,3},{5,4},{6,5},{7,6},{8,7},{9,8},{10,9},{11,1... | collective-permute-start | bytes 196616 | tf_op jit(solution)/shard_map/ppermute | solution.py:23
  116.2 1.7 %copy-start.1 = (bf16[1024,1024]{1,0:T(8,128)(2,1)S(1)}, bf16[1024,1024]{1,0:T(8,128)(2,1)}, u32[]{:S(2)}) copy-start(bf16[1024,1024]{1,0:T(8,128)(2,1)} %w_key.1) | copy-start | bytes 6291460
  116.2 2.2 %copy-start.2 = (bf16[1024,1024]{1,0:T(8,128)(2,1)S(1)}, bf16[1024,1024]{1,0:T(8,128)(2,1)}, u32[]{:S(2)}) copy-start(bf16[1024,1024]{1,0:T(8,128)(2,1)} %w_value.1) | copy-start | bytes 6291460

commit v8 on v7

--- a/solution.py
+++ b/solution.py
@@ -210,10 +210,9 @@
     _, width, patches = own.shape
     pairs = (self_pair, pair1, pair2, pair4, pair8)
 
-    @pl.loop(0, patches // LANES)
-    def _(step):
-        here = lanes(step)
-        there = lanes(step + start // LANES)
+    for step in range(patches // LANES):
+        here = slice(step * LANES, (step + 1) * LANES)
+        there = slice(start + step * LANES, start + (step + 1) * LANES)
         getters = source_getters(own, (two_a, two_b), (one_a, one_b), far4, far8, 1, here)
         for h, rows in enumerate(head_slices(width)):
             terms = [pairs[s][h:h + 1, there] * get(0, rows).astype(jnp.float32) for s, get in enumerate(getters)]

time: 124 us -> 124 us (level)
  no operation moved by 1% of the time
where the time goes in v8:
time: 124 us
  waiting for transfers between devices  60 us (48%)
  starting transfers between devices  47.1 us (38%)
  Pallas kernels  15.5 us (12%)
    ppermute x12, waiting for transfers between devices, shift(): lax.ppermute(block, 'frame', [(i, i + distance) for i in range(n) if 0 <=...  42.5 us
    ppermute x12, starting transfers between devices, shift(): lax.ppermute(block, 'frame', [(i, i + distance) for i in range(n) if 0 <=...  31.2 us
    ppermute x8, waiting for transfers between devices, swap(): return lax.ppermute(block, 'frame', [(i, i ^ bit) for i in range(n)])  17.5 us
    ppermute x8, starting transfers between devices, swap(): return lax.ppermute(block, 'frame', [(i, i ^ bit) for i in range(n)])  16 us
    pallas_call x1, Pallas kernels, sums_of(): pl.pallas_call(functools.partial(sum_kernel, [(len(h[2]), len(h[3])) for...  5.05 us
    pallas_call x2, Pallas kernels, pack(): pl.pallas_call(kernel, in_specs=[pl.BlockSpec(memory_space=pl.ANY)] * 4,...  4.06 us
    pallas_call x4, Pallas kernels, products_of(): pl.pallas_call(functools.partial(product_kernel, len(two), len(one), len(...  2.87 us
  transfers between devices with their start and end apart: 20, of which 8 were waited for; matrix products, arithmetic and copies ran while one was open for 0% of the time, Pallas kernels for 7%

profile of v8, /device:TPU:27, one launch (start us, length us, event | category | flops | bytes accessed | tf_op | source)
XLA Modules:
  0.0 123.5 jit_solution(14654716672980370317)
XLA Ops:
  0.0 2.2 %pack.2 = (bf16[2,1024,256]{2,1,0:T(8,128)(2,1)S(1)}, bf16[2,1024,256]{2,1,0:T(8,128)(2,1)S(1)}, bf16[2,1024,256]{2,1,0:T(8,128)(2,1)S(1)}) custom-call(bf16[1,512,1024]{2,1,0:T(8,128)(2,1)} %q_hbm.2, bf16[1,512,1024]{2,1,0:T(8,128)(2,1)} %k_hbm.3, bf16[1,512,1024]{2,1,0:T(8,128)(2,1)} %v_hbm.3, bf16[1,512,1024]{2,1,0:T(8,128)(2,1)} %g_hbm.3), custom_call_target="tpu_custom_call" | custom-call | tf_op jit(solution)/shard_map/pack/pallas_call | solution.py:71
  2.2 1.3 %collective-permute-start = (bf16[2,1024,256]{2,1,0:T(8,128)(2,1)S(1)}, bf16[2,1024,256]{2,1,0:T(8,128)(2,1)S(1)}, u32[]{:S(2)}, u32[]{:S(2)}) collective-permute-start(bf16[2,1024,256]{2,1,0:T(8,128)(2,1)S(1)} %get-tuple-element.34.refs_0_.rest_0_.own), channel_id=1, source_target_pairs={{0,4},{1,5},{2,6},{3,7},{4,8},{5,9},{6,10},{7,11},{8,12},{9,13},{1... | collective-permute-start | bytes 3145736 | tf_op jit(solution)/shard_map/ppermute | solution.py:23
  3.5 4.1 %collective-permute-start.2 = (bf16[2,1024,256]{2,1,0:T(8,128)(2,1)S(1)}, bf16[2,1024,256]{2,1,0:T(8,128)(2,1)S(1)}, u32[]{:S(2)}, u32[]{:S(2)}) collective-permute-start(bf16[2,1024,256]{2,1,0:T(8,128)(2,1)S(1)} %get-tuple-element.37.refs_1_.qg.rest_0_), channel_id=1, source_target_pairs={{4,0},{5,1},{6,2},{7,3},{8,4},{9,5},{10,6},{11,7},{12,8},{13,9},{1... | collective-permute-start | bytes 3145736 | tf_op jit(solution)/shard_map/ppermute | solution.py:23
  7.6 1.3 %collective-permute-start.1 = (bf16[2,1024,256]{2,1,0:T(8,128)(2,1)S(1)}, bf16[2,1024,256]{2,1,0:T(8,128)(2,1)S(1)}, u32[]{:S(2)}, u32[]{:S(2)}) collective-permute-start(bf16[2,1024,256]{2,1,0:T(8,128)(2,1)S(1)} %get-tuple-element.29), channel_id=1, source_target_pairs={{0,2},{1,3},{2,0},{3,1},{4,6},{5,7},{6,4},{7,5},{8,10},{9,11},{10,... | collective-permute-start | bytes 3145736 | tf_op jit(solution)/shard_map/ppermute | solution.py:28
  8.9 1.8 %pack.3 = (bf16[2,1024,256]{2,1,0:T(8,128)(2,1)S(1)}, bf16[2,1024,256]{2,1,0:T(8,128)(2,1)S(1)}) custom-call(bf16[1,512,1024]{2,1,0:T(8,128)(2,1)} %q_hbm.2, bf16[1,512,1024]{2,1,0:T(8,128)(2,1)} %k_hbm.3, bf16[1,512,1024]{2,1,0:T(8,128)(2,1)} %v_hbm.3, bf16[1,512,1024]{2,1,0:T(8,128)(2,1)} %g_hbm.3), custom_call_target="tpu_custom_call" | custom-call | tf_op jit(solution)/shard_map/pack/pallas_call | solution.py:71
  10.7 1.3 %collective-permute-start.4 = (bf16[2,1024,256]{2,1,0:T(8,128)(2,1)S(1)}, bf16[2,1024,256]{2,1,0:T(8,128)(2,1)S(1)}, u32[]{:S(2)}, u32[]{:S(2)}) collective-permute-start(bf16[2,1024,256]{2,1,0:T(8,128)(2,1)S(1)} %get-tuple-element.31.refs_0_.rest_0_.own), channel_id=1, source_target_pairs={{0,4},{1,5},{2,6},{3,7},{4,8},{5,9},{6,10},{7,11},{8,12},{9,13},{1... | collective-permute-start | bytes 3145736 | tf_op jit(solution)/shard_map/ppermute | solution.py:23
  12.0 4.1 %collective-permute-start.5 = (bf16[2,1024,256]{2,1,0:T(8,128)(2,1)S(1)}, bf16[2,1024,256]{2,1,0:T(8,128)(2,1)S(1)}, u32[]{:S(2)}, u32[]{:S(2)}) collective-permute-start(bf16[2,1024,256]{2,1,0:T(8,128)(2,1)S(1)} %get-tuple-element.40.qg.refs_1_.rest_8_), channel_id=1, source_target_pairs={{4,0},{5,1},{6,2},{7,3},{8,4},{9,5},{10,6},{11,7},{12,8},{13,9},{1... | collective-permute-start | bytes 3145736 | tf_op jit(solution)/shard_map/ppermute | solution.py:23
  16.1 12.0 %collective-permute-done.refs_1_.rest_1_.far4 = bf16[2,1024,256]{2,1,0:T(8,128)(2,1)S(1)} collective-permute-done((bf16[2,1024,256]{2,1,0:T(8,128)(2,1)S(1)}, bf16[2,1024,256]{2,1,0:T(8,128)(2,1)S(1)}, u32[]{:S(2)}, u32[]{:S(2)}) %collective-permute-start) | collective-permute-done | bytes 1048608 | tf_op jit(solution)/shard_map/ppermute | solution.py:23
  29.0 2.1 %collective-permute-done.1.refs_2_.rest_2_.refs_0_.two_a.rest_4_ = bf16[2,1024,256]{2,1,0:T(8,128)(2,1)S(1)} collective-permute-done((bf16[2,1024,256]{2,1,0:T(8,128)(2,1)S(1)}, bf16[2,1024,256]{2,1,0:T(8,128)(2,1)S(1)}, u32[]{:S(2)}, u32[]{:S(2)}) %collective-permute-start.1) | collective-permute-done | bytes 1048608 | tf_op jit(solution)/shard_map/ppermute | solution.py:28
  32.3 2.1 %collective-permute-start.8 = (bf16[2,1024,256]{2,1,0:T(8,128)(2,1)S(1)}, bf16[2,1024,256]{2,1,0:T(8,128)(2,1)S(1)}, u32[]{:S(2)}, u32[]{:S(2)}) collective-permute-start(bf16[2,1024,256]{2,1,0:T(8,128)(2,1)S(1)} %collective-permute-done.2.refs_0_.rest_2_), channel_id=1, source_target_pairs={{4,0},{5,1},{6,2},{7,3},{8,4},{9,5},{10,6},{11,7},{12,8},{13,9},{1... | collective-permute-start | bytes 3145736 | tf_op jit(solution)/shard_map/ppermute | solution.py:23
  35.7 14.9 %collective-permute-done.4.refs_1_.rest_1_.far4 = bf16[2,1024,256]{2,1,0:T(8,128)(2,1)S(1)} collective-permute-done((bf16[2,1024,256]{2,1,0:T(8,128)(2,1)S(1)}, bf16[2,1024,256]{2,1,0:T(8,128)(2,1)S(1)}, u32[]{:S(2)}, u32[]{:S(2)}) %collective-permute-start.4) | collective-permute-done | bytes 1048608 | tf_op jit(solution)/shard_map/ppermute | solution.py:23
  50.7 1.3 %collective-permute-start.9 = (bf16[2,1024,256]{2,1,0:T(8,128)(2,1)S(1)}, bf16[2,1024,256]{2,1,0:T(8,128)(2,1)S(1)}, u32[]{:S(2)}, u32[]{:S(2)}) collective-permute-start(bf16[2,1024,256]{2,1,0:T(8,128)(2,1)S(1)} %pick.10), channel_id=1, source_target_pairs={{0,2},{1,3},{2,0},{3,1},{4,6},{5,7},{6,4},{7,5},{8,10},{9,11},{10,... | collective-permute-start | bytes 3145736 | tf_op jit(solution)/shard_map/ppermute | solution.py:28
  52.0 1.6 %collective-permute-done.3.refs_1_.rest_3_.refs_2_.rest_2_.two_b.two_a = bf16[2,1024,256]{2,1,0:T(8,128)(2,1)S(1)} collective-permute-done((bf16[2,1024,256]{2,1,0:T(8,128)(2,1)S(1)}, bf16[2,1024,256]{2,1,0:T(8,128)(2,1)S(1)}, u32[]{:S(2)}, u32[]{:S(2)}) %collective-permute-start.3) | collective-permute-done | bytes 1048608 | tf_op jit(solution)/shard_map/ppermute | solution.py:28
  53.6 5.8 %collective-permute-start.7 = (bf16[2,1024,256]{2,1,0:T(8,128)(2,1)S(1)}, bf16[2,1024,256]{2,1,0:T(8,128)(2,1)S(1)}, u32[]{:S(2)}, u32[]{:S(2)}) collective-permute-start(bf16[2,1024,256]{2,1,0:T(8,128)(2,1)S(1)} %pick.9), channel_id=1, source_target_pairs={{0,1},{1,0},{2,3},{3,2},{4,5},{5,4},{6,7},{7,6},{8,9},{9,8},{10,11... | collective-permute-start | bytes 3145736 | tf_op jit(solution)/shard_map/ppermute | solution.py:28
  59.7 14.2 %collective-permute-done.8.rest_3_ = bf16[2,1024,256]{2,1,0:T(8,128)(2,1)S(1)} collective-permute-done((bf16[2,1024,256]{2,1,0:T(8,128)(2,1)S(1)}, bf16[2,1024,256]{2,1,0:T(8,128)(2,1)S(1)}, u32[]{:S(2)}, u32[]{:S(2)}) %collective-permute-start.8) | collective-permute-done | bytes 1048608 | tf_op jit(solution)/shard_map/ppermute | solution.py:23
  76.5 4.8 %collective-permute-start.17 = (bf16[2,1024,256]{2,1,0:T(8,128)(2,1)S(1)}, bf16[2,1024,256]{2,1,0:T(8,128)(2,1)S(1)}, u32[]{:S(2)}, u32[]{:S(2)}) collective-permute-start(bf16[2,1024,256]{2,1,0:T(8,128)(2,1)S(1)} %collective-permute-done.5.refs_0_.rest_10_), channel_id=1, source_target_pairs={{4,0},{5,1},{6,2},{7,3},{8,4},{9,5},{10,6},{11,7},{12,8},{13,9},{1... | collective-permute-start | bytes 3145736 | tf_op jit(solution)/shard_map/ppermute | solution.py:23
  82.9 2.5 %collective-permute-start.11 = (bf16[2,1024,256]{2,1,0:T(8,128)(2,1)S(1)}, bf16[2,1024,256]{2,1,0:T(8,128)(2,1)S(1)}, u32[]{:S(2)}, u32[]{:S(2)}) collective-permute-start(bf16[2,1024,256]{2,1,0:T(8,128)(2,1)S(1)} %pick.11), channel_id=1, source_target_pairs={{0,1},{1,0},{2,3},{3,2},{4,5},{5,4},{6,7},{7,6},{8,9},{9,8},{10,11... | collective-permute-start | bytes 3145736 | tf_op jit(solution)/shard_map/ppermute | solution.py:28
  85.4 13.8 %collective-permute-done.18.refs_0_.rest_12_ = bf16[2,1024,256]{2,1,0:T(8,128)(2,1)S(1)} collective-permute-done((bf16[2,1024,256]{2,1,0:T(8,128)(2,1)S(1)}, bf16[2,1024,256]{2,1,0:T(8,128)(2,1)S(1)}, u32[]{:S(2)}, u32[]{:S(2)}) %collective-permute-start.18) | collective-permute-done | bytes 1048608 | tf_op jit(solution)/shard_map/ppermute | solution.py:28
  99.3 2.5 %collective-permute-start.19 = (bf16[2,1024,256]{2,1,0:T(8,128)(2,1)S(1)}, bf16[2,1024,256]{2,1,0:T(8,128)(2,1)S(1)}, u32[]{:S(2)}, u32[]{:S(2)}) collective-permute-start(bf16[2,1024,256]{2,1,0:T(8,128)(2,1)S(1)} %pick.13), channel_id=1, source_target_pairs={{0,1},{1,0},{2,3},{3,2},{4,5},{5,4},{6,7},{7,6},{8,9},{9,8},{10,11... | collective-permute-start | bytes 3145736 | tf_op jit(solution)/shard_map/ppermute | solution.py:28
  103.9 2.0 %collective-permute-start.13 = (f32[32,512]{1,0:T(8,128)S(1)}, f32[32,512]{1,0:T(8,128)S(1)}, u32[]{:S(2)}, u32[]{:S(2)}) collective-permute-start(f32[32,512]{1,0:T(8,128)S(1)} %get-tuple-element.43.pair8), channel_id=1, source_target_pairs={{8,0},{9,1},{10,2},{11,3},{12,4},{13,5},{14,6},{15,7},{24,16},{25,... | collective-permute-start | bytes 196616 | tf_op jit(solution)/shard_map/ppermute | solution.py:23
  105.8 2.1 %collective-permute-start.14 = (f32[32,512]{1,0:T(8,128)S(1)}, f32[32,512]{1,0:T(8,128)S(1)}, u32[]{:S(2)}, u32[]{:S(2)}) collective-permute-start(f32[32,512]{1,0:T(8,128)S(1)} %get-tuple-element.44.pair4), channel_id=1, source_target_pairs={{4,0},{5,1},{6,2},{7,3},{8,4},{9,5},{10,6},{11,7},{12,8},{13,9},{1... | collective-permute-start | bytes 196616 | tf_op jit(solution)/shard_map/ppermute | solution.py:23
  108.0 2.9 %collective-permute-start.15 = (f32[32,512]{1,0:T(8,128)S(1)}, f32[32,512]{1,0:T(8,128)S(1)}, u32[]{:S(2)}, u32[]{:S(2)}) collective-permute-start(f32[32,512]{1,0:T(8,128)S(1)} %get-tuple-element.45.pair2), channel_id=1, source_target_pairs={{2,0},{3,1},{4,2},{5,3},{6,4},{7,5},{8,6},{9,7},{10,8},{11,9},{12,... | collective-permute-start | bytes 196616 | tf_op jit(solution)/shard_map/ppermute | solution.py:23
  110.8 4.0 %collective-permute-start.16 = (f32[32,512]{1,0:T(8,128)S(1)}, f32[32,512]{1,0:T(8,128)S(1)}, u32[]{:S(2)}, u32[]{:S(2)}) collective-permute-start(f32[32,512]{1,0:T(8,128)S(1)} %get-tuple-element.46.pair1), channel_id=1, source_target_pairs={{1,0},{2,1},{3,2},{4,3},{5,4},{6,5},{7,6},{8,7},{9,8},{10,9},{11,1... | collective-permute-start | bytes 196616 | tf_op jit(solution)/shard_map/ppermute | solution.py:23
  118.3 5.0 %sums.1 = bf16[512,1024]{1,0:T(8,128)(2,1)} custom-call(f32[32,512]{1,0:T(8,128)S(1)} %get-tuple-element.42.self_pair, f32[32,512]{1,0:T(8,128)S(1)} %collective-permute-done.13.pair8, f32[32,512]{1,0:T(8,128)S(1)} %collective-permute-done.14.pair4, f32[32,512]{1,0:T(8,128)S(1)} %collective-permute-done.15.pair2, ...), custom_call_target="tpu_custom_call" | custom-call | flops 3449999872 | bytes 11070000 | tf_op jit(solution)/shard_map/sums/pallas_call | solution.py:277
  (41 shorter events, 13.3 us)
Async XLA Ops:
  2.2 25.9 %collective-permute-start = (bf16[2,1024,256]{2,1,0:T(8,128)(2,1)S(1)}, bf16[2,1024,256]{2,1,0:T(8,128)(2,1)S(1)}, u32[]{:S(2)}, u32[]{:S(2)}) collective-permute-start(bf16[2,1024,256]{2,1,0:T(8,128)(2,1)S(1)} %get-tuple-element.34.refs_0_.rest_0_.own), channel_id=1, source_target_pairs={{0,4},{1,5},{2,6},{3,7},{4,8},{5,9},{6,10},{7,11},{8,12},{9,13},{1... | collective-permute-start | bytes 3145736 | tf_op jit(solution)/shard_map/ppermute | solution.py:23
  3.5 25.5 %collective-permute-start.2 = (bf16[2,1024,256]{2,1,0:T(8,128)(2,1)S(1)}, bf16[2,1024,256]{2,1,0:T(8,128)(2,1)S(1)}, u32[]{:S(2)}, u32[]{:S(2)}) collective-permute-start(bf16[2,1024,256]{2,1,0:T(8,128)(2,1)S(1)} %get-tuple-element.37.refs_1_.qg.rest_0_), channel_id=1, source_target_pairs={{4,0},{5,1},{6,2},{7,3},{8,4},{9,5},{10,6},{11,7},{12,8},{13,9},{1... | collective-permute-start | bytes 3145736 | tf_op jit(solution)/shard_map/ppermute | solution.py:23
  7.6 23.5 %collective-permute-start.1 = (bf16[2,1024,256]{2,1,0:T(8,128)(2,1)S(1)}, bf16[2,1024,256]{2,1,0:T(8,128)(2,1)S(1)}, u32[]{:S(2)}, u32[]{:S(2)}) collective-permute-start(bf16[2,1024,256]{2,1,0:T(8,128)(2,1)S(1)} %get-tuple-element.29), channel_id=1, source_target_pairs={{0,2},{1,3},{2,0},{3,1},{4,6},{5,7},{6,4},{7,5},{8,10},{9,11},{10,... | collective-permute-start | bytes 3145736 | tf_op jit(solution)/shard_map/ppermute | solution.py:28
  10.7 39.9 %collective-permute-start.4 = (bf16[2,1024,256]{2,1,0:T(8,128)(2,1)S(1)}, bf16[2,1024,256]{2,1,0:T(8,128)(2,1)S(1)}, u32[]{:S(2)}, u32[]{:S(2)}) collective-permute-start(bf16[2,1024,256]{2,1,0:T(8,128)(2,1)S(1)} %get-tuple-element.31.refs_0_.rest_0_.own), channel_id=1, source_target_pairs={{0,4},{1,5},{2,6},{3,7},{4,8},{5,9},{6,10},{7,11},{8,12},{9,13},{1... | collective-permute-start | bytes 3145736 | tf_op jit(solution)/shard_map/ppermute | solution.py:23
  12.0 40.0 %collective-permute-start.5 = (bf16[2,1024,256]{2,1,0:T(8,128)(2,1)S(1)}, bf16[2,1024,256]{2,1,0:T(8,128)(2,1)S(1)}, u32[]{:S(2)}, u32[]{:S(2)}) collective-permute-start(bf16[2,1024,256]{2,1,0:T(8,128)(2,1)S(1)} %get-tuple-element.40.qg.refs_1_.rest_8_), channel_id=1, source_target_pairs={{4,0},{5,1},{6,2},{7,3},{8,4},{9,5},{10,6},{11,7},{12,8},{13,9},{1... | collective-permute-start | bytes 3145736 | tf_op jit(solution)/shard_map/ppermute | solution.py:23
  31.1 22.5 %collective-permute-start.3 = (bf16[2,1024,256]{2,1,0:T(8,128)(2,1)S(1)}, bf16[2,1024,256]{2,1,0:T(8,128)(2,1)S(1)}, u32[]{:S(2)}, u32[]{:S(2)}) collective-permute-start(bf16[2,1024,256]{2,1,0:T(8,128)(2,1)S(1)} %pick.7), channel_id=1, source_target_pairs={{0,2},{1,3},{2,0},{3,1},{4,6},{5,7},{6,4},{7,5},{8,10},{9,11},{10,... | collective-permute-start | bytes 3145736 | tf_op jit(solution)/shard_map/ppermute | solution.py:28
  32.3 41.6 %collective-permute-start.8 = (bf16[2,1024,256]{2,1,0:T(8,128)(2,1)S(1)}, bf16[2,1024,256]{2,1,0:T(8,128)(2,1)S(1)}, u32[]{:S(2)}, u32[]{:S(2)}) collective-permute-start(bf16[2,1024,256]{2,1,0:T(8,128)(2,1)S(1)} %collective-permute-done.2.refs_0_.rest_2_), channel_id=1, source_target_pairs={{4,0},{5,1},{6,2},{7,3},{8,4},{9,5},{10,6},{11,7},{12,8},{13,9},{1... | collective-permute-start | bytes 3145736 | tf_op jit(solution)/shard_map/ppermute | solution.py:23
  34.4 39.5 %collective-permute-start.10 = (bf16[2,1024,256]{2,1,0:T(8,128)(2,1)S(1)}, bf16[2,1024,256]{2,1,0:T(8,128)(2,1)S(1)}, u32[]{:S(2)}, u32[]{:S(2)}) collective-permute-start(bf16[2,1024,256]{2,1,0:T(8,128)(2,1)S(1)} %collective-permute-done.refs_1_.rest_1_.far4), channel_id=1, source_target_pairs={{0,4},{1,5},{2,6},{3,7},{4,8},{5,9},{6,10},{7,11},{8,12},{9,13},{1... | collective-permute-start | bytes 3145736 | tf_op jit(solution)/shard_map/ppermute | solution.py:23
  50.7 25.8 %collective-permute-start.9 = (bf16[2,1024,256]{2,1,0:T(8,128)(2,1)S(1)}, bf16[2,1024,256]{2,1,0:T(8,128)(2,1)S(1)}, u32[]{:S(2)}, u32[]{:S(2)}) collective-permute-start(bf16[2,1024,256]{2,1,0:T(8,128)(2,1)S(1)} %pick.10), channel_id=1, source_target_pairs={{0,2},{1,3},{2,0},{3,1},{4,6},{5,7},{6,4},{7,5},{8,10},{9,11},{10,... | collective-permute-start | bytes 3145736 | tf_op jit(solution)/shard_map/ppermute | solution.py:28
  53.6 28.1 %collective-permute-start.7 = (bf16[2,1024,256]{2,1,0:T(8,128)(2,1)S(1)}, bf16[2,1024,256]{2,1,0:T(8,128)(2,1)S(1)}, u32[]{:S(2)}, u32[]{:S(2)}) collective-permute-start(bf16[2,1024,256]{2,1,0:T(8,128)(2,1)S(1)} %pick.9), channel_id=1, source_target_pairs={{0,1},{1,0},{2,3},{3,2},{4,5},{5,4},{6,7},{7,6},{8,9},{9,8},{10,11... | collective-permute-start | bytes 3145736 | tf_op jit(solution)/shard_map/ppermute | solution.py:28
  59.5 22.2 %collective-permute-start.6 = (bf16[2,1024,256]{2,1,0:T(8,128)(2,1)S(1)}, bf16[2,1024,256]{2,1,0:T(8,128)(2,1)S(1)}, u32[]{:S(2)}, u32[]{:S(2)}) collective-permute-start(bf16[2,1024,256]{2,1,0:T(8,128)(2,1)S(1)} %pick.8), channel_id=1, source_target_pairs={{0,1},{1,0},{2,3},{3,2},{4,5},{5,4},{6,7},{7,6},{8,9},{9,8},{10,11... | collective-permute-start | bytes 3145736 | tf_op jit(solution)/shard_map/ppermute | solution.py:28
  74.0 25.2 %collective-permute-start.18 = (bf16[2,1024,256]{2,1,0:T(8,128)(2,1)S(1)}, bf16[2,1024,256]{2,1,0:T(8,128)(2,1)S(1)}, u32[]{:S(2)}, u32[]{:S(2)}) collective-permute-start(bf16[2,1024,256]{2,1,0:T(8,128)(2,1)S(1)} %pick.12), channel_id=1, source_target_pairs={{0,2},{1,3},{2,0},{3,1},{4,6},{5,7},{6,4},{7,5},{8,10},{9,11},{10,... | collective-permute-start | bytes 3145736 | tf_op jit(solution)/shard_map/ppermute | solution.py:28
  75.2 26.5 %collective-permute-start.12 = (bf16[2,1024,256]{2,1,0:T(8,128)(2,1)S(1)}, bf16[2,1024,256]{2,1,0:T(8,128)(2,1)S(1)}, u32[]{:S(2)}, u32[]{:S(2)}) collective-permute-start(bf16[2,1024,256]{2,1,0:T(8,128)(2,1)S(1)} %collective-permute-done.4.refs_1_.rest_1_.far4), channel_id=1, source_target_pairs={{0,4},{1,5},{2,6},{3,7},{4,8},{5,9},{6,10},{7,11},{8,12},{9,13},{1... | collective-permute-start | bytes 3145736 | tf_op jit(solution)/shard_map/ppermute | solution.py:23
  76.5 34.3 %collective-permute-start.17 = (bf16[2,1024,256]{2,1,0:T(8,128)(2,1)S(1)}, bf16[2,1024,256]{2,1,0:T(8,128)(2,1)S(1)}, u32[]{:S(2)}, u32[]{:S(2)}) collective-permute-start(bf16[2,1024,256]{2,1,0:T(8,128)(2,1)S(1)} %collective-permute-done.5.refs_0_.rest_10_), channel_id=1, source_target_pairs={{4,0},{5,1},{6,2},{7,3},{8,4},{9,5},{10,6},{11,7},{12,8},{13,9},{1... | collective-permute-start | bytes 3145736 | tf_op jit(solution)/shard_map/ppermute | solution.py:23
  82.9 19.2 %collective-permute-start.11 = (bf16[2,1024,256]{2,1,0:T(8,128)(2,1)S(1)}, bf16[2,1024,256]{2,1,0:T(8,128)(2,1)S(1)}, u32[]{:S(2)}, u32[]{:S(2)}) collective-permute-start(bf16[2,1024,256]{2,1,0:T(8,128)(2,1)S(1)} %pick.11), channel_id=1, source_target_pairs={{0,1},{1,0},{2,3},{3,2},{4,5},{5,4},{6,7},{7,6},{8,9},{9,8},{10,11... | collective-permute-start | bytes 3145736 | tf_op jit(solution)/shard_map/ppermute | solution.py:28
  99.3 18.0 %collective-permute-start.19 = (bf16[2,1024,256]{2,1,0:T(8,128)(2,1)S(1)}, bf16[2,1024,256]{2,1,0:T(8,128)(2,1)S(1)}, u32[]{:S(2)}, u32[]{:S(2)}) collective-permute-start(bf16[2,1024,256]{2,1,0:T(8,128)(2,1)S(1)} %pick.13), channel_id=1, source_target_pairs={{0,1},{1,0},{2,3},{3,2},{4,5},{5,4},{6,7},{7,6},{8,9},{9,8},{10,11... | collective-permute-start | bytes 3145736 | tf_op jit(solution)/shard_map/ppermute | solution.py:28
  102.0 1.2 copy-start.3
  102.1 12.8 %copy-start = (bf16[1024,1024]{1,0:T(8,128)(2,1)S(1)}, bf16[1024,1024]{1,0:T(8,128)(2,1)}, u32[]{:S(2)}) copy-start(bf16[1024,1024]{1,0:T(8,128)(2,1)} %w_query.3) | copy-start | bytes 6291460
  103.9 13.5 %collective-permute-start.13 = (f32[32,512]{1,0:T(8,128)S(1)}, f32[32,512]{1,0:T(8,128)S(1)}, u32[]{:S(2)}, u32[]{:S(2)}) collective-permute-start(f32[32,512]{1,0:T(8,128)S(1)} %get-tuple-element.43.pair8), channel_id=1, source_target_pairs={{8,0},{9,1},{10,2},{11,3},{12,4},{13,5},{14,6},{15,7},{24,16},{25,... | collective-permute-start | bytes 196616 | tf_op jit(solution)/shard_map/ppermute | solution.py:23
  105.8 11.5 %collective-permute-start.14 = (f32[32,512]{1,0:T(8,128)S(1)}, f32[32,512]{1,0:T(8,128)S(1)}, u32[]{:S(2)}, u32[]{:S(2)}) collective-permute-start(f32[32,512]{1,0:T(8,128)S(1)} %get-tuple-element.44.pair4), channel_id=1, source_target_pairs={{4,0},{5,1},{6,2},{7,3},{8,4},{9,5},{10,6},{11,7},{12,8},{13,9},{1... | collective-permute-start | bytes 196616 | tf_op jit(solution)/shard_map/ppermute | solution.py:23
  108.0 9.4 %collective-permute-start.15 = (f32[32,512]{1,0:T(8,128)S(1)}, f32[32,512]{1,0:T(8,128)S(1)}, u32[]{:S(2)}, u32[]{:S(2)}) collective-permute-start(f32[32,512]{1,0:T(8,128)S(1)} %get-tuple-element.45.pair2), channel_id=1, source_target_pairs={{2,0},{3,1},{4,2},{5,3},{6,4},{7,5},{8,6},{9,7},{10,8},{11,9},{12,... | collective-permute-start | bytes 196616 | tf_op jit(solution)/shard_map/ppermute | solution.py:23
  110.8 7.1 %collective-permute-start.16 = (f32[32,512]{1,0:T(8,128)S(1)}, f32[32,512]{1,0:T(8,128)S(1)}, u32[]{:S(2)}, u32[]{:S(2)}) collective-permute-start(f32[32,512]{1,0:T(8,128)S(1)} %get-tuple-element.46.pair1), channel_id=1, source_target_pairs={{1,0},{2,1},{3,2},{4,3},{5,4},{6,5},{7,6},{8,7},{9,8},{10,9},{11,1... | collective-permute-start | bytes 196616 | tf_op jit(solution)/shard_map/ppermute | solution.py:23
  116.1 1.8 %copy-start.1 = (bf16[1024,1024]{1,0:T(8,128)(2,1)S(1)}, bf16[1024,1024]{1,0:T(8,128)(2,1)}, u32[]{:S(2)}) copy-start(bf16[1024,1024]{1,0:T(8,128)(2,1)} %w_key.1) | copy-start | bytes 6291460
  116.1 2.2 %copy-start.2 = (bf16[1024,1024]{1,0:T(8,128)(2,1)S(1)}, bf16[1024,1024]{1,0:T(8,128)(2,1)}, u32[]{:S(2)}) copy-start(bf16[1024,1024]{1,0:T(8,128)(2,1)} %w_value.1) | copy-start | bytes 6291460
